TPU v7x, 32 devices: a whole 2x2x4 slice. The times are simulated.
32 devices in a mesh: groups: 2 (over x), cache: 8 (over z, y), tensor: 2 (over core).
Axes of the slice: x: 2, y: 2, z: 4, core: 2. Of those that a mesh axis runs over, the one named last changes fastest.
Arguments:
- x_in: bfloat16 [8192, 4096], P(('groups', 'cache'), 'tensor'), parts along dimension 0, may hold values from -6 to 6
- z_in: bfloat16 [8192, 4096], P(('groups', 'cache'), 'tensor'), parts along dimension 0, may hold values from -6 to 6
- bc_in: bfloat16 [8192, 512], P(('groups', 'cache')), parts along dimension 0, may hold values from -6 to 6
- dt_in: float32 [8192, 64], P(('groups', 'cache'), 'tensor'), parts along dimension 0, may hold values from -3 to 43
- conv_x: bfloat16 [4, 4096], P(None, 'tensor'), may hold values from -3 to 3
- conv_bc: bfloat16 [4, 512], replicated, may hold values from -3 to 3
- a_log: float32 [64], P('tensor'), may hold values from -8.2 to -2.8
- dt_bias: float32 [64], P('tensor'), may hold values from -1 to 1
- d_skip: float32 [64], P('tensor'), may hold values from 0.02 to 16
- norm_gain: float32 [4096], P('tensor'), may hold values from 0.25 to 1.75
- out_weight: bfloat16 [2560, 4096], P('cache', 'tensor'), may hold values from -0.09375 to 0.09375
- store_ssm: float32 [16, 64, 64, 256], P(('groups', 'cache'), 'tensor'), parts along dimension 0, may hold values from -6 to 6
- stored_conv_inputs: float32 [16, 3, 4096], P(('groups', 'cache'), None, 'tensor'), parts along dimension 0, may hold values from -6 to 6
- store_convbc: float32 [16, 3, 512], P(('groups', 'cache')), parts along dimension 0, may hold values from -6 to 6
- hits: int32 [16, 2], P('groups'), parts along dimension 0, may hold values from 0 to 7, as said below
- assign: int32 [16], P('groups'), parts along dimension 0, may hold values from 0 to 7, each once
- lengths: int32 [16], P(('groups', 'cache')), parts along dimension 0, may hold values from 128 to 512, as said below
Outputs:
- mixed: bfloat16 [8192, 2560], P(('groups', 'cache'), 'tensor'), parts along dimension 0
There are 2 independent parts, one for each index of `groups`. A program takes and returns all parts, laid end to end along the dimension named above; an argument that names none is the same for every part. Nothing has to cross between parts.
Inputs may be any that keep to these rules, and one draw needn't show every extreme that they name: hits[r, 0] is the cache index of the device that stores request r's prefix state and hits[r, 1] its slot there, below 1. No cache index stores the states of more than 4 requests, and one stores exactly 4. Several requests may name the same slot. `assign`: each request appears at exactly one position. `lengths`: one position has all 512 tokens valid.
All inputs are finite; a program needn't handle non-finite values.
Results may differ from a plain program's by a relative error of at most 0.0057.
Values may be sent and summed in bfloat16 or wider, within the bound.
No kernel may reach another device: no remote copies, remote signals or barrier semaphores. Data moves between devices by JAX's collectives and lax.ppermute only.
A program may use at most 128 MiB of HBM per device.

v0:
```python
import jax
import jax.numpy as jnp
from jax import lax
from jax.sharding import PartitionSpec as P

BLOCK = 128
INNER = 4096


def conv_silu(prev, current, weight):
    length = current.shape[0]
    seq = jnp.concatenate([prev, current.astype(jnp.float32)], axis=0)
    total = jnp.zeros(current.shape, jnp.float32)
    for k in range(weight.shape[0]):
        total = total + weight[k].astype(jnp.float32) * seq[k : k + length]
    return jax.nn.silu(total).astype(jnp.bfloat16)


def block_step(state, inputs):
    x_block, b_block, readout_tile, dt_block, rate_block = inputs
    cum = jnp.cumsum(rate_block, axis=0)
    scores = lax.dot_general(
        readout_tile, b_block, (((1,), (1,)), ((), ())), preferred_element_type=jnp.float32
    )
    cum_heads = cum.T
    diff = cum_heads[:, :, None] - cum_heads[:, None, :]
    size = cum.shape[0]
    causal = jnp.arange(size)[:, None] >= jnp.arange(size)[None, :]
    decay = jnp.exp(jnp.where(causal[None], diff, -jnp.inf))
    parameter_tensors = (scores[None] * decay * dt_block.T[:, None, :]).astype(jnp.bfloat16)
    intra = jnp.einsum(
        "hts,shp->thp", parameter_tensors, x_block, preferred_element_type=jnp.float32
    )
    from_state = jnp.exp(cum)[:, :, None] * jnp.einsum(
        "tn,hpn->thp", readout_tile.astype(jnp.float32), state, precision=lax.Precision.HIGHEST
    )
    ending = cum[-1]
    coef = jnp.exp(ending[None, :] - cum) * dt_block
    update = jnp.einsum(
        "shp,sn->hpn",
        x_block.astype(jnp.float32) * coef[:, :, None],
        b_block.astype(jnp.float32),
        precision=lax.Precision.HIGHEST,
    )
    new_state = jnp.exp(ending)[:, None, None] * state + update
    return (new_state, intra + from_state)


def body(
    x_in,
    z_in,
    bc_in,
    dt_in,
    conv_x,
    conv_bc,
    a_log,
    dt_bias,
    d_skip,
    norm_gain,
    out_weight,
    store_ssm,
    stored_conv_inputs,
    store_convbc,
    hits,
    assign,
    lengths,
):
    ncache = lax.axis_size("cache")
    requests = hits.shape[0]
    per_dev = requests // ncache
    local_slots = store_ssm.shape[0]
    heads_here = store_ssm.shape[1]
    head_dim = store_ssm.shape[2]
    state_size = store_ssm.shape[3]
    taps_prev = stored_conv_inputs.shape[1]
    feature_lanes = x_in.shape[1]
    owner = hits[:, 0]
    slot = hits[:, 1]
    request_ids = jnp.arange(requests)
    convx_send = stored_conv_inputs.reshape(local_slots, ncache, -1)
    convbc_send = store_convbc.reshape(local_slots, ncache, -1)
    received = (
        lax.all_to_all(store_ssm, "cache", split_axis=1, concat_axis=0, tiled=True),
        lax.all_to_all(convx_send, "cache", split_axis=1, concat_axis=0, tiled=True),
        lax.all_to_all(convbc_send, "cache", split_axis=1, concat_axis=0, tiled=True),
    )
    row_of = owner * local_slots + slot
    position_hits = (assign[:, None] == request_ids[None, :]).astype(jnp.int32)
    row_at = jnp.sum(position_hits * row_of[None, :], axis=1)
    outgoing = (
        jnp.take(received[0], row_at, axis=0),
        jnp.take(received[1], row_at, axis=0),
        jnp.take(received[2], row_at, axis=0),
    )
    ssm_start, convx_start, convbc_start = (
        lax.all_to_all(outgoing[0], "cache", split_axis=0, concat_axis=1, tiled=True),
        lax.all_to_all(outgoing[1], "cache", split_axis=0, concat_axis=1, tiled=True),
        lax.all_to_all(outgoing[2], "cache", split_axis=0, concat_axis=1, tiled=True),
    )
    convx_start = convx_start.reshape(per_dev, taps_prev, feature_lanes)
    convbc_start = convbc_start.reshape(per_dev, taps_prev, 2 * state_size)
    tokens_each = x_in.shape[0] // per_dev
    nblocks = tokens_each // BLOCK
    decay_rate = -jnp.exp(a_log)
    xs = conv_silu(convx_start[0], x_in, conv_x)
    bcs = conv_silu(convbc_start[0], bc_in, conv_bc)
    b_all = bcs[:, :state_size]
    c_all = bcs[:, state_size:]
    step_size = jax.nn.softplus(dt_in + dt_bias[None, :])
    rate = step_size * decay_rate[None, :]
    x3 = xs.reshape(tokens_each, heads_here, head_dim)
    inputs = (
        x3.reshape(nblocks, BLOCK, heads_here, head_dim),
        b_all.reshape(nblocks, BLOCK, state_size),
        c_all.reshape(nblocks, BLOCK, state_size),
        step_size.reshape(nblocks, BLOCK, heads_here),
        rate.reshape(nblocks, BLOCK, heads_here),
    )
    final, outs = lax.scan(block_step, ssm_start[0], inputs)
    ssm_out = outs.reshape(tokens_each, heads_here, head_dim) + d_skip[None, :, None] * x3.astype(
        jnp.float32
    )
    gated_parts = ssm_out.reshape(tokens_each, feature_lanes) * jax.nn.silu(
        z_in.astype(jnp.float32)
    )
    squares = lax.psum(jnp.sum(gated_parts * gated_parts, axis=1), "tensor")
    mean_sq = squares / INNER
    normed = (gated_parts * lax.rsqrt(mean_sq + 1e-05)[:, None] * norm_gain[None, :]).astype(
        jnp.bfloat16
    )
    partial_out = lax.dot_general(
        normed,
        lax.all_gather(out_weight, "cache", axis=0, tiled=True),
        (((1,), (1,)), ((), ())),
        preferred_element_type=jnp.float32,
    )
    summed = lax.psum_scatter(partial_out, "tensor", scatter_dimension=1, tiled=True)
    valid = (jnp.arange(tokens_each)[None, :] < lengths[:, None]).reshape(-1)
    return jnp.where(valid[:, None], summed, 0.0).astype(jnp.bfloat16)


def solution(mesh):
    return jax.shard_map(
        body,
        mesh=mesh,
        in_specs=(
            P(("groups", "cache"), "tensor"),
            P(("groups", "cache"), "tensor"),
            P(("groups", "cache"), None),
            P(("groups", "cache"), "tensor"),
            P(None, "tensor"),
            P(),
            P("tensor"),
            P("tensor"),
            P("tensor"),
            P("tensor"),
            P("cache", "tensor"),
            P(("groups", "cache"), "tensor", None, None),
            P(("groups", "cache"), None, "tensor"),
            P(("groups", "cache"), None, None),
            P("groups", None),
            P("groups"),
            P(("groups", "cache")),
        ),
        out_specs=P(("groups", "cache"), "tensor"),
        check_vma=False,
    )
```

profile of v0, /device:TPU:0, one launch (start us, length us, event | category | flops | bytes accessed | tf_op | source)
XLA Modules:
  0.0 432.2 jit_solution(9121441121892779873)
XLA Ops:
  8.1 13.6 %all_to_all.63 = f32[1,8,192]{2,0,1:T(1,128)S(1)} all-to-all(f32[1,8,192]{2,0,1:T(1,128)S(1)} %reshape.187), channel_id=1, replica_groups=mesh['groups'=2,'cache'=8,'tensor'=2] {'cache'}, dimensions={1} | all-to-all | bytes 12288 | tf_op jit(solution)/shard_map/all_to_all | solution.py:85
  21.7 10.2 %all_to_all.64 = f32[1,8,768]{2,0,1:T(1,128)S(1)} all-to-all(f32[1,8,768]{2,0,1:T(1,128)} %bitcast.124), channel_id=1, replica_groups=mesh['groups'=2,'cache'=8,'tensor'=2] {'cache'}, dimensions={1} | all-to-all | bytes 49152 | tf_op jit(solution)/shard_map/all_to_all | solution.py:84
  31.9 3.6 all-to-all-start
  37.6 75.6 %all-to-all-done = f32[1,32,64,256]{3,2,0,1:T(8,128)S(1)} async-done(((f32[1,32,64,256]{3,2,0,1:T(8,128)}), f32[1,32,64,256]{3,2,0,1:T(8,128)S(1)}, u32[]{:S(2)}, u32[]{:S(2)}) %all-to-all-start) | async-done | bytes 2097184 | tf_op jit(solution)/shard_map/all_to_all | solution.py:83
  119.2 3.7 all-to-all-done.5
  123.0 5.0 %all-to-all-start.3 = ((f32[8,1,768]{2,1,0:T(1,128)}), f32[8,1,768]{2,1,0:T(1,128)S(1)}, u32[]{:S(2)}, u32[]{:S(2)}) async-start(f32[8,1,768]{2,1,0:T(1,128)} %copy.73), calls=%async_computation.3 | async-start | bytes 49152 | tf_op jit(solution)/shard_map/all_to_all | solution.py:97
  128.0 3.4 broadcast_select_fusion
  131.3 3.6 all-to-all-done.3
  135.6 4.0 all-to-all-start.1
  139.6 3.9 copy.74
  143.6 4.3 convert_element_type.51
  149.8 3.9 copy.80
  157.2 12.5 %multiply_convert_fusion.3 = bf16[512,2048]{0,1:T(8,128)(2,1)} fusion(f32[512,2048]{0,1:T(8,128)} %convert_element_type.51, f32[3,2048]{0,1:T(8,128)S(1)} %copy.75, f32[2048]{0:T(1024)S(1)} %bitcast.122, f32[2048]{0:T(1024)S(1)} %bitcast.123, f32[2048]{0:T(1024)S(1)} %bitcast.121, f32[2048]{0:T(1024)S(1)} %bitcast.120), kind=kLoop, calls=%fused_computation.63 | loop fusion | flops 15728640 | bytes 6348800 | tf_op jit(solution)/shard_map/convert_element_type | solution.py:16
  169.7 4.0 reshape_reshape.3
  173.6 3.4 copy.78
  177.1 61.5 %all-to-all-done.1 = f32[8,4,64,256]{3,2,1,0:T(8,128)S(1)} async-done(((f32[8,4,64,256]{3,2,1,0:T(8,128)}), f32[8,4,64,256]{3,2,1,0:T(8,128)S(1)}, u32[]{:S(2)}, u32[]{:S(2)}) %all-to-all-start.1) | async-done | bytes 2097184 | tf_op jit(solution)/shard_map/all_to_all | solution.py:96
  238.5 152.2 %while.12 = (s32[]{:T(128)}, f32[32,64,256]{2,1,0:T(8,128)S(1)}, f32[4,128,32,64]{1,0,3,2:T(4,128)}, f32[4,128,32]{2,1,0:T(8,128)}, bf16[4,128,32,64]{1,3,2,0:T(...) while((s32[]{:T(128)}, f32[32,64,256]{2,1,0:T(8,128)S(1)}, ...), condition=%wide.region_3.4_spmd, body=%wide.region_1.0_spmd.sunk | while | flops 1691373568 | bytes 13389185 | solution.py:119
  246.9 26.4 %dynamic_update_slice.5 = f32[4,128,32,64]{1,0,3,2:T(4,128)} dynamic-update-slice(f32[4,128,32,64]{1,0,3,2:T(4,128)} %get-tuple-element.184, f32[1,128,32,64]{1,0,3,2:T(1,128)S(1)} %bitcast.109, s32[]{:T(128)} %get-tuple-element.182, s32[]{:T(128)} %constant.71.clone.1..sunk, s32[]{:T(128)} %constant.71.clone.1..sunk, s32[]{:T(128)} %constant.71.clone.1..sunk) | dynamic-update-slice | bytes 2097156 | tf_op jit(solution)/shard_map/while/body/jit(dynamic_update_index_in_dim)/dynamic_update_slice | solution.py:119
  285.0 26.4 %dynamic_update_slice.5 = f32[4,128,32,64]{1,0,3,2:T(4,128)} dynamic-update-slice(f32[4,128,32,64]{1,0,3,2:T(4,128)} %get-tuple-element.184, f32[1,128,32,64]{1,0,3,2:T(1,128)S(1)} %bitcast.109, s32[]{:T(128)} %get-tuple-element.182, s32[]{:T(128)} %constant.71.clone.1..sunk, s32[]{:T(128)} %constant.71.clone.1..sunk, s32[]{:T(128)} %constant.71.clone.1..sunk) | dynamic-update-slice | bytes 2097156 | tf_op jit(solution)/shard_map/while/body/jit(dynamic_update_index_in_dim)/dynamic_update_slice | solution.py:119
  323.0 26.4 %dynamic_update_slice.5 = f32[4,128,32,64]{1,0,3,2:T(4,128)} dynamic-update-slice(f32[4,128,32,64]{1,0,3,2:T(4,128)} %get-tuple-element.184, f32[1,128,32,64]{1,0,3,2:T(1,128)S(1)} %bitcast.109, s32[]{:T(128)} %get-tuple-element.182, s32[]{:T(128)} %constant.71.clone.1..sunk, s32[]{:T(128)} %constant.71.clone.1..sunk, s32[]{:T(128)} %constant.71.clone.1..sunk) | dynamic-update-slice | bytes 2097156 | tf_op jit(solution)/shard_map/while/body/jit(dynamic_update_index_in_dim)/dynamic_update_slice | solution.py:119
  361.1 26.4 %dynamic_update_slice.5 = f32[4,128,32,64]{1,0,3,2:T(4,128)} dynamic-update-slice(f32[4,128,32,64]{1,0,3,2:T(4,128)} %get-tuple-element.184, f32[1,128,32,64]{1,0,3,2:T(1,128)S(1)} %bitcast.109, s32[]{:T(128)} %get-tuple-element.182, s32[]{:T(128)} %constant.71.clone.1..sunk, s32[]{:T(128)} %constant.71.clone.1..sunk, s32[]{:T(128)} %constant.71.clone.1..sunk) | dynamic-update-slice | bytes 2097156 | tf_op jit(solution)/shard_map/while/body/jit(dynamic_update_index_in_dim)/dynamic_update_slice | solution.py:119
  390.7 5.7 %multiply_reduce_fusion = (f32[512]{0:T(512)S(1)}, f32[512,2048]{0,1:T(8,128)}) fusion(bf16[512,2048]{0,1:T(8,128)(2,1)} %copy.80, bf16[512,2048]{0,1:T(8,128)(2,1)} %multiply_convert_fusion.3, f32[2048]{0:T(1024)} %mul.255, f32[256,8,4,128]{3,2,1,0:T(4,128)} %bitcast.112), kind=kLoop, calls=%fused_computation.62 | loop fusion | flops 11533824 | bytes 12593152 | tf_op jit(solution)/shard_map/reduce_sum | solution.py:126
  399.1 12.0 %fusion.41 = f32[512,2560]{1,0:T(8,128)} fusion(bf16[2560,2048]{1,0:T(8,128)(2,1)} %all-gather.2.cloned.1.call-done, f32[512,2048]{0,1:T(8,128)} %get-tuple-element.97, f32[2048]{0:T(1024)S(1)} %copy-done.7, f32[512]{0:T(512)S(1)} %add_rsqrt_fusion), kind=kOutput, calls=%fused_computation.65 | convolution fusion | flops 5371854848 | bytes 19933184 | tf_op jit(solution)/shard_map/dot_general | solution.py:131
  411.7 10.6 %reduce-scatter.2.cloned.1.call-done = f32[512,1280]{1,0:T(8,128)} async-done(((f32[512,2560]{1,0:T(8,128)}), f32[512,1280]{1,0:T(8,128)}) %reduce-scatter.2.cloned.1.call-update) | async-done | bytes 2621456 | tf_op jit(solution)/shard_map/reduce_scatter | solution.py:137
  (121 shorter events, 67.6 us)
Async XLA Ops:
  6.5 29.0 %copy-start.8 = (s32[8,2]{0,1:T(2,128)S(1)}, s32[8,2]{0,1:T(2,128)}, u32[]{:S(2)}) copy-start(s32[8,2]{0,1:T(2,128)} %param.33) | copy-start | bytes 196
  6.5 29.0 %copy-start.9 = (s32[8]{0:T(128)S(1)}, s32[8]{0:T(128)}, u32[]{:S(2)}) copy-start(s32[8]{0:T(128)} %param.34) | copy-start | bytes 100
  6.5 392.5 %all-gather.2.cloned.1.call-start = ((), (), s32[]{:S(2)}) async-start(), calls=%async_computation.7 | async-start | bytes 11796480 | tf_op jit(solution)/shard_map/all_gather | solution.py:133
  31.9 81.3 %all-to-all-start = ((f32[1,32,64,256]{3,2,0,1:T(8,128)}), f32[1,32,64,256]{3,2,0,1:T(8,128)S(1)}, u32[]{:S(2)}, u32[]{:S(2)}) async-start(f32[1,32,64,256]{3,2,0,1:T(8,128)} %bitcast.116), calls=%async_computation | async-start | bytes 4194304 | tf_op jit(solution)/shard_map/all_to_all | solution.py:83
  113.2 9.8 %all-to-all-start.5 = ((f32[8,1,192]{2,1,0:T(1,128)}), f32[8,1,192]{2,1,0:T(1,128)S(1)}, u32[]{:S(2)}, u32[]{:S(2)}) async-start(f32[8,1,192]{2,1,0:T(1,128)} %copy.77), calls=%async_computation.5 | async-start | bytes 16384 | tf_op jit(solution)/shard_map/all_to_all | solution.py:98
  123.0 12.0 %all-to-all-start.3 = ((f32[8,1,768]{2,1,0:T(1,128)}), f32[8,1,768]{2,1,0:T(1,128)S(1)}, u32[]{:S(2)}, u32[]{:S(2)}) async-start(f32[8,1,768]{2,1,0:T(1,128)} %copy.73), calls=%async_computation.3 | async-start | bytes 49152 | tf_op jit(solution)/shard_map/all_to_all | solution.py:97
  135.0 0.6 copy-start.1
  135.6 103.0 %all-to-all-start.1 = ((f32[8,4,64,256]{3,2,1,0:T(8,128)}), f32[8,4,64,256]{3,2,1,0:T(8,128)S(1)}, u32[]{:S(2)}, u32[]{:S(2)}) async-start(f32[8,4,64,256]{3,2,1,0:T(8,128)} %broadcast_select_fusion), calls=%async_computation.1 | async-start | bytes 4194304 | tf_op jit(solution)/shard_map/all_to_all | solution.py:96
  139.6 282.7 %reduce-scatter.2.cloned.1.call-start = ((), (), s32[]{:S(2)}) async-start(), calls=%async_computation.8 | async-start | bytes 7864320 | tf_op jit(solution)/shard_map/reduce_scatter | solution.py:137
  143.6 4.3 copy-start
  143.6 4.4 %copy-start.10 = (f32[32]{0:T(128)S(1)}, f32[32]{0:T(128)}, u32[]{:S(2)}) copy-start(f32[32]{0:T(128)} %param.25) | copy-start | bytes 388
  143.6 4.4 %copy-start.2 = (f32[512,32]{0,1:T(8,128)S(1)}, f32[512,32]{0,1:T(8,128)}, u32[]{:S(2)}) copy-start(f32[512,32]{0,1:T(8,128)} %param.22) | copy-start | bytes 196612
  143.6 4.4 %copy-start.5 = (f32[32]{0:T(128)S(1)}, f32[32]{0:T(128)}, u32[]{:S(2)}) copy-start(f32[32]{0:T(128)} %param.26) | copy-start | bytes 388
  147.8 5.9 %copy-start.6 = (f32[32]{0:T(128)S(1)}, f32[32]{0:T(128)}, u32[]{:S(2)}) copy-start(f32[32]{0:T(128)} %param.27) | copy-start | bytes 388
  147.8 6.6 %copy-start.4 = (bf16[4,512]{1,0:T(4,128)(2,1)S(1)}, bf16[4,512]{1,0:T(4,128)(2,1)}, u32[]{:S(2)}) copy-start(bf16[4,512]{1,0:T(4,128)(2,1)} %param.24) | copy-start | bytes 12292
  147.8 6.6 %copy-start.3 = (bf16[4,2048]{1,0:T(4,128)(2,1)S(1)}, bf16[4,2048]{1,0:T(4,128)(2,1)}, u32[]{:S(2)}) copy-start(bf16[4,2048]{1,0:T(4,128)(2,1)} %param.23) | copy-start | bytes 49156
  390.7 8.4 %copy-start.7 = (f32[2048]{0:T(1024)S(1)}, f32[2048]{0:T(1024)}, u32[]{:S(2)}) copy-start(f32[2048]{0:T(1024)} %param.28) | copy-start | bytes 24580
Sparse Core Ops, SparseCore 0:
  9.5 234.5 all-gather.1
  411.2 11.0 reduce-scatter.1
where the time goes:
time: 437 us; the launch traced here: 432 us
  waiting for transfers between devices  156 us (36%)
  local copies, waits for them, and re-layouts  134 us (31%)
  matrix products  49.4 us (11%)
  other arithmetic  36 us (8%)
  blocking collectives  26.4 us (6%)
  starting transfers between devices  15.9 us (4%)
  between operations  14.3 us (3%)
    dynamic_update_slice x4, local copies, waits for them, and re-layouts, body(): final, outs = lax.scan(block_step, ssm_start[0], inputs)  106 us
    all_to_all x1, waiting for transfers between devices, body(): lax.all_to_all(store_ssm, 'cache', split_axis=1, concat_axis=0, tiled=True)  75.6 us
    all_to_all x1, waiting for transfers between devices, body(): lax.all_to_all(outgoing[0], 'cache', split_axis=0, concat_axis=1, tiled=T...  61.5 us
    all_to_all x1, blocking collectives, body(): lax.all_to_all(convbc_send, 'cache', split_axis=1, concat_axis=0, tiled=T...  13.6 us
    convert_element_type x2, other arithmetic, conv_silu(): return jax.nn.silu(total).astype(jnp.bfloat16)  13.1 us
    dot_general x4, matrix products, block_step(): jnp.einsum('shp,sn->hpn', x_block.astype(jnp.float32) * coef[:, :, None],...  12.5 us
    dot_general x1, matrix products, body(): lax.dot_general(normed, lax.all_gather(out_weight, 'cache', axis=0, tiled...  12 us
    dot_general x4, matrix products, block_step(): jnp.einsum('hts,shp->thp', parameter_tensors, x_block, preferred_element_...  11.7 us
  transfers between devices with their start and end apart: 6, of which 5 were waited for; matrix products, arithmetic and copies ran while one was open for 47% of the time, Pallas kernels for 0%

commit v1 on v0

v1 whole, which is shorter than its diff:
```python
import functools

import jax
import jax.numpy as jnp
from jax import lax
from jax.experimental import pallas as pl
from jax.experimental.pallas import tpu as pltpu
from jax.sharding import PartitionSpec as P

BLOCK = 128
INNER = 4096
LOG2E = 1.4426950408889634
GROUP = 8
NEG = -1e30


def silu(u):
    return u * (0.5 * jnp.tanh(0.5 * u) + 0.5)


def conv_silu(prev, current, weight):
    length = current.shape[0]
    seq = jnp.concatenate([prev, current.astype(jnp.float32)], axis=0)
    total = jnp.zeros(current.shape, jnp.float32)
    for k in range(weight.shape[0]):
        total = total + weight[k].astype(jnp.float32) * seq[k : k + length]
    return silu(total).astype(jnp.bfloat16)


def dot(a, b):
    return jnp.dot(a, b, preferred_element_type=jnp.float32)


def spread(cols, first, head, rows, lane, width):
    left = jnp.broadcast_to(cols[rows, first + head : first + head + 1], (BLOCK, 2 * width))
    right = jnp.broadcast_to(
        cols[rows, first + head + 1 : first + head + 2], (BLOCK, 2 * width)
    )
    return left, right, jnp.where(lane < width, left, right)


def scan_kernel(x_ref, prev_ref, taps_ref, cols_ref, arow_ref, skip_ref, g_ref, bt_ref, c_ref, y_ref, seq, xs):
    tokens, lanes = x_ref.shape
    nblocks = tokens // BLOCK
    width = lanes // GROUP
    pair = 2 * width
    taps = taps_ref.shape[0]
    seq[0:8, :] = prev_ref[...]
    for k in range(nblocks):
        seq[8 + k * BLOCK : 8 + (k + 1) * BLOCK, :] = x_ref[
            k * BLOCK : (k + 1) * BLOCK, :
        ].astype(jnp.float32)
    for k in range(nblocks):
        base = 8 - (taps - 1) + k * BLOCK
        total = taps_ref[0:1, :].astype(jnp.float32) * seq[base : base + BLOCK, :]
        for j in range(1, taps):
            total = total + taps_ref[j : j + 1, :].astype(jnp.float32) * seq[
                base + j : base + j + BLOCK, :
            ]
        xs[k * BLOCK : (k + 1) * BLOCK, :] = silu(total).astype(jnp.bfloat16)
    lane = lax.broadcasted_iota(jnp.int32, (BLOCK, pair), 1)
    causal = lax.broadcasted_iota(jnp.int32, (BLOCK, BLOCK), 0) >= lax.broadcasted_iota(
        jnp.int32, (BLOCK, BLOCK), 1
    )
    for p in range(GROUP // 2):
        here = slice(p * pair, (p + 1) * pair)
        head = 2 * p
        state = None
        for k in range(nblocks):
            rows = slice(k * BLOCK, (k + 1) * BLOCK)
            x2 = xs[rows, here]
            left, right, cum = spread(cols_ref, 0, head, rows, lane, width)
            weights = []
            for i, col in ((0, left), (1, right)):
                diff = col - arow_ref[head + i : head + i + 1, rows]
                decay = jnp.exp2(jnp.where(causal, diff, NEG))
                weights.append((decay * g_ref[rows, :]).astype(jnp.bfloat16))
            zero = jnp.zeros_like(x2)
            both = jnp.concatenate(
                [jnp.where(lane < width, x2, zero), jnp.where(lane < width, zero, x2)], axis=0
            )
            out = dot(jnp.concatenate(weights, axis=1), both)
            x2f = x2.astype(jnp.float32)
            out = out + skip_ref[:, here] * x2f
            if k > 0:
                out = out + jnp.exp2(cum) * dot(c_ref[rows, :], state.astype(jnp.bfloat16))
            y_ref[rows, here] = out
            if k < nblocks - 1:
                _, _, acol = spread(cols_ref, GROUP, head, rows, lane, width)
                end = cum[BLOCK - 1 : BLOCK, :]
                scaled = (x2f * jnp.exp2(end - acol)).astype(jnp.bfloat16)
                update = dot(bt_ref[:, rows], scaled)
                state = update if k == 0 else jnp.exp2(end) * state + update


def scan_call(x_in, prev, taps, cols, arow, skip, g, bt, c):
    tokens, channels = x_in.shape
    groups = cols.shape[0]
    lanes = channels // groups
    n = c.shape[1]
    return pl.pallas_call(
        scan_kernel,
        grid=(groups,),
        in_specs=[
            pl.BlockSpec((tokens, lanes), lambda i: (0, i)),
            pl.BlockSpec((8, lanes), lambda i: (0, i)),
            pl.BlockSpec((taps.shape[0], lanes), lambda i: (0, i)),
            pl.BlockSpec((None, tokens, 2 * GROUP), lambda i: (i, 0, 0)),
            pl.BlockSpec((GROUP, tokens), lambda i: (i, 0)),
            pl.BlockSpec((1, lanes), lambda i: (0, i)),
            pl.BlockSpec((tokens, BLOCK), lambda i: (0, 0)),
            pl.BlockSpec((n, tokens), lambda i: (0, 0)),
            pl.BlockSpec((tokens, n), lambda i: (0, 0)),
        ],
        out_specs=pl.BlockSpec((tokens, lanes), lambda i: (0, i)),
        out_shape=jax.ShapeDtypeStruct((tokens, channels), jnp.float32),
        scratch_shapes=[
            pltpu.VMEM((tokens + 8, lanes), jnp.float32),
            pltpu.VMEM((tokens, lanes), jnp.bfloat16),
        ],
        compiler_params=pltpu.CompilerParams(vmem_limit_bytes=40 * 2**20),
        cost_estimate=pl.CostEstimate(
            flops=2 * tokens * channels * 1024, bytes_accessed=tokens * channels * 6, transcendentals=tokens * channels * 4
        ),
        name="scan_blocks",
    )(x_in, prev, taps, cols, arow, skip, g, bt, c)


def gate_kernel(y_ref, z_ref, cols_ref, h_ref, c_ref, gain_ref, out_ref, sq_ref):
    tokens, lanes = y_ref.shape
    nblocks = tokens // BLOCK
    width = lanes // GROUP
    pair = 2 * width
    lane = lax.broadcasted_iota(jnp.int32, (BLOCK, pair), 1)

    @pl.when(pl.program_id(0) == 0)
    def _():
        sq_ref[...] = jnp.zeros_like(sq_ref)

    for k in range(nblocks):
        rows = slice(k * BLOCK, (k + 1) * BLOCK)
        read = lax.dot_general(
            c_ref[rows, :], h_ref[...], (((1,), (1,)), ((), ())), preferred_element_type=jnp.float32
        )
        total = sq_ref[rows, :]
        for p in range(GROUP // 2):
            here = slice(p * pair, (p + 1) * pair)
            _, _, cum = spread(cols_ref, 0, 2 * p, rows, lane, width)
            out = y_ref[rows, here] + jnp.exp2(cum) * read[:, here]
            gated = out * silu(z_ref[rows, here].astype(jnp.float32))
            total = total + gated * gated
            out_ref[rows, here] = (gated * gain_ref[:, here]).astype(jnp.bfloat16)
        sq_ref[rows, :] = total


def gate_call(y, z, cols, h, c, gain):
    tokens, channels = y.shape
    groups = cols.shape[0]
    lanes = channels // groups
    n = c.shape[1]
    return pl.pallas_call(
        gate_kernel,
        grid=(groups,),
        in_specs=[
            pl.BlockSpec((tokens, lanes), lambda i: (0, i)),
            pl.BlockSpec((tokens, lanes), lambda i: (0, i)),
            pl.BlockSpec((None, tokens, GROUP), lambda i: (i, 0, 0)),
            pl.BlockSpec((lanes, n), lambda i: (i, 0)),
            pl.BlockSpec((tokens, n), lambda i: (0, 0)),
            pl.BlockSpec((1, lanes), lambda i: (0, i)),
        ],
        out_specs=[
            pl.BlockSpec((tokens, lanes), lambda i: (0, i)),
            pl.BlockSpec((tokens, 128), lambda i: (0, 0)),
        ],
        out_shape=[
            jax.ShapeDtypeStruct((tokens, channels), jnp.bfloat16),
            jax.ShapeDtypeStruct((tokens, 128), jnp.float32),
        ],
        compiler_params=pltpu.CompilerParams(vmem_limit_bytes=40 * 2**20),
        cost_estimate=pl.CostEstimate(
            flops=2 * tokens * channels * 256, bytes_accessed=tokens * channels * 9, transcendentals=tokens * channels * 2
        ),
        name="gate_blocks",
    )(y, z, cols, h, c, gain)


def gather_all(value, axis):
    n = lax.axis_size(axis)
    if n & (n - 1):
        return lax.all_gather(value, axis, axis=0)
    me = lax.axis_index(axis)
    held = value[None]
    step = 1
    while step < n:
        other = lax.ppermute(held, axis, [(i, i ^ step) for i in range(n)])
        low = (me & step) == 0
        held = jnp.concatenate(
            [jnp.where(low, held, other), jnp.where(low, other, held)], axis=0
        )
        step *= 2
    return held


def ring_order(n):
    if n == 8:
        return [0, 2, 4, 6, 7, 5, 3, 1]
    return list(range(n))


def ring_gather(block, axis):
    n = lax.axis_size(axis)
    rows = block.shape[0]
    order = ring_order(n)
    place = [order.index(i) for i in range(n)]
    ahead = [(order[i], order[(i + 1) % n]) for i in range(n)]
    back = [(b, a) for a, b in ahead]
    me = jnp.asarray(place)[lax.axis_index(axis)]
    ids = jnp.asarray(order)
    full = jnp.zeros((n * rows, block.shape[1]), block.dtype)

    def put(full, piece, offset, first=0):
        at = ids[lax.rem(me + offset + n, n)] * rows + first
        return lax.dynamic_update_slice(full, piece, (at, 0))

    full = put(full, block, 0)
    a = b = block
    for k in range(1, (n - 1) // 2 + 1):
        a = lax.ppermute(a, axis, ahead)
        b = lax.ppermute(b, axis, back)
        full = put(put(full, a, -k), b, k)
    if n % 2 == 0:
        k = n // 2
        half = rows // 2
        full = put(full, lax.ppermute(a[:half], axis, ahead), -k)
        full = put(full, lax.ppermute(b[half:], axis, back), k, half)
    return full


def body(
    x_in,
    z_in,
    bc_in,
    dt_in,
    conv_x,
    conv_bc,
    a_log,
    dt_bias,
    d_skip,
    norm_gain,
    out_weight,
    store_ssm,
    stored_conv_inputs,
    store_convbc,
    hits,
    assign,
    lengths,
):
    ncache = lax.axis_size("cache")
    requests = hits.shape[0]
    local_slots, heads, width, n = store_ssm.shape
    taps_prev = stored_conv_inputs.shape[1]
    tokens, channels = x_in.shape
    nblocks = tokens // BLOCK
    groups = heads // GROUP

    row_of = hits[:, 0] * local_slots + hits[:, 1]
    position_hits = (assign[:, None] == jnp.arange(requests)[None, :]).astype(jnp.int32)
    row_at = jnp.sum(position_hits * row_of[None, :], axis=1)
    row_here = row_at[lax.axis_index("cache")]

    states = store_ssm.astype(jnp.bfloat16).reshape(local_slots, heads, width * n)
    states = lax.all_to_all(states, "cache", split_axis=1, concat_axis=0, tiled=True)
    states = jnp.take(states, row_at, axis=0)
    start = lax.all_to_all(states, "cache", split_axis=0, concat_axis=1, tiled=True)
    start = start.reshape(channels, n)

    small = jnp.concatenate([stored_conv_inputs, store_convbc], axis=2)
    small = gather_all(small.reshape(-1, 128), "cache")
    small = lax.dynamic_index_in_dim(
        small.reshape(ncache * local_slots, taps_prev, -1), row_here, 0, keepdims=False
    )
    prev_x = jnp.concatenate(
        [jnp.zeros((8 - taps_prev, channels), jnp.float32), small[:, :channels]], axis=0
    )

    weight = ring_gather(out_weight, "cache")

    bcs = conv_silu(small[:, channels:], bc_in, conv_bc)
    b = bcs[:, :n]
    c = bcs[:, n:]
    step_size = jax.nn.softplus(dt_in + dt_bias[None, :])
    rate = step_size * (-LOG2E * jnp.exp(a_log))[None, :]
    b3 = b.reshape(nblocks, BLOCK, n)
    c3 = c.reshape(nblocks, BLOCK, n)
    g = jnp.einsum("ktn,ksn->kts", c3, b3, preferred_element_type=jnp.float32)
    causal = jnp.arange(BLOCK)[:, None] >= jnp.arange(BLOCK)[None, :]
    g = jnp.where(causal[None], g, 0.0).reshape(tokens, BLOCK)
    cum = jnp.einsum(
        "ts,ksh->kth",
        causal.astype(jnp.float32),
        rate.reshape(nblocks, BLOCK, heads),
        precision=lax.Precision.HIGHEST,
    )
    ends = cum[:, -1, :]
    before = jnp.concatenate([jnp.zeros((1, heads), jnp.float32), jnp.cumsum(ends, axis=0)[:-1]])
    whole = (cum + before[:, None, :]).reshape(tokens, heads)
    cum = cum.reshape(tokens, heads)
    acol = cum - jnp.log2(step_size)

    def grouped(v):
        return v.reshape(tokens, groups, GROUP).transpose(1, 0, 2)

    cols = jnp.concatenate([grouped(cum), grouped(acol)], axis=2)
    skip = jnp.repeat(d_skip, width)[None, :]
    y = scan_call(x_in, prev_x, conv_x, cols, acol.T, skip, g, b.T, c)
    gated, squares = gate_call(y, z_in, grouped(whole), start, c, norm_gain[None, :])

    swap = [(0, 1), (1, 0)]
    half = weight.shape[0] // 2
    core = lax.axis_index("tensor")
    squares = jnp.sum(squares, axis=1)
    squares = squares + lax.ppermute(squares, "tensor", swap)

    def project(index):
        part = lax.dynamic_slice_in_dim(weight, index * half, half, 0)
        return lax.dot_general(
            gated, part, (((1,), (1,)), ((), ())), preferred_element_type=jnp.float32
        )

    other = lax.ppermute(project(1 - core).astype(jnp.bfloat16), "tensor", swap)
    summed = project(core) + other.astype(jnp.float32)
    mixed = summed * lax.rsqrt(squares / INNER + 1e-05)[:, None]
    valid = jnp.arange(tokens) < lengths[0]
    return jnp.where(valid[:, None], mixed, 0.0).astype(jnp.bfloat16)


def solution(mesh):
    return jax.shard_map(
        body,
        mesh=mesh,
        in_specs=(
            P(("groups", "cache"), "tensor"),
            P(("groups", "cache"), "tensor"),
            P(("groups", "cache"), None),
            P(("groups", "cache"), "tensor"),
            P(None, "tensor"),
            P(),
            P("tensor"),
            P("tensor"),
            P("tensor"),
            P("tensor"),
            P("cache", "tensor"),
            P(("groups", "cache"), "tensor", None, None),
            P(("groups", "cache"), None, "tensor"),
            P(("groups", "cache"), None, None),
            P("groups", None),
            P("groups"),
            P(("groups", "cache")),
        ),
        out_specs=P(("groups", "cache"), "tensor"),
        check_vma=False,
    )
```

time: 437 us -> 195 us (0.45)
  waiting for transfers between devices: 156 us -> 42.2 us
  local copies, waits for them, and re-layouts: 134 us -> 58.8 us
  matrix products: 49.4 us -> 14.1 us
  blocking collectives: 26.4 us -> 0 us
  other arithmetic: 36 us -> 16.2 us
  starting transfers between devices: 15.9 us -> 32.8 us
  Pallas kernels: 0 us -> 15.4 us
    all_to_all x4 -> x2, waiting for transfers between devices: 144 us -> 0.01 us  [the longest x1 0.01 us: body(): lax.all_to_all(states, 'cache', split_axis=1, concat_axis=0, tiled=True)]
    dynamic_update_slice x4 -> x9, local copies, waits for them, and re-layouts: 106 us -> 19.3 us  [put(): return lax.dynamic_update_slice(full, piece, (at, 0))]
    ppermute x0 -> x13, waiting for transfers between devices: none -> 42.2 us  [the longest x3 20.8 us: ring_gather(): a = lax.ppermute(a, axis, ahead)]
    dot_general x17 -> x4, matrix products: 49.4 us -> 14.1 us  [the longest x2 13.6 us: project(): lax.dot_general(gated, part, (((1,), (1,)), ((), ())), preferred_element_...]
    all_to_all x2 -> x0, blocking collectives: 23.8 us -> none  [the longest x1 13.6 us: body(): lax.all_to_all(convbc_send, 'cache', split_axis=1, concat_axis=0, tiled=T...]
    ppermute x0 -> x13, starting transfers between devices: none -> 23.6 us  [the longest x3 8.85 us: gather_all(): other = lax.ppermute(held, axis, [(i, i ^ step) for i in range(n)])]
    pallas_call x0 -> x2, Pallas kernels: none -> 15.4 us  [the longest x1 11.4 us: scan_call(): pl.pallas_call(scan_kernel, grid=(groups,), in_specs=[pl.BlockSpec((token...]
    convert_element_type x3 -> x2, other arithmetic: 16.1 us -> 3.07 us  [the longest x1 1.73 us: body(): store_ssm.astype(jnp.bfloat16).reshape(local_slots, heads, width * n)]
  transfers between devices with their start and end apart: 6 -> 15, of which waited for: 5 -> 7; matrix products, arithmetic and copies ran while one was open for 47% -> 35% of each run, Pallas kernels for 0% -> 8%
where the time goes in v1:
time: 195 us; the launch traced here: 194 us
  local copies, waits for them, and re-layouts  58.8 us (30%)
  waiting for transfers between devices  42.2 us (22%)
  starting transfers between devices  32.8 us (17%)
  other arithmetic  16.2 us (8%)
  Pallas kernels  15.4 us (8%)
  between operations  14.8 us (8%)
  matrix products  14.1 us (7%)
    ppermute x3, waiting for transfers between devices, ring_gather(): a = lax.ppermute(a, axis, ahead)  20.8 us
    dynamic_update_slice x9, local copies, waits for them, and re-layouts, put(): return lax.dynamic_update_slice(full, piece, (at, 0))  19.3 us
    dot_general x2, matrix products, project(): lax.dot_general(gated, part, (((1,), (1,)), ((), ())), preferred_element_...  13.6 us
    pallas_call x1, Pallas kernels, scan_call(): pl.pallas_call(scan_kernel, grid=(groups,), in_specs=[pl.BlockSpec((token...  11.4 us
    unnamed x47, local copies, waits for them, and re-layouts  11.1 us
    all_to_all x2, local copies, waits for them, and re-layouts, body(): lax.all_to_all(states, 'cache', split_axis=1, concat_axis=0, tiled=True)  9.01 us
    ppermute x3, waiting for transfers between devices, gather_all(): other = lax.ppermute(held, axis, [(i, i ^ step) for i in range(n)])  8.92 us
    ppermute x3, starting transfers between devices, gather_all(): other = lax.ppermute(held, axis, [(i, i ^ step) for i in range(n)])  8.85 us
  transfers between devices with their start and end apart: 15, of which 7 were waited for; matrix products, arithmetic and copies ran while one was open for 35% of the time, Pallas kernels for 8%

profile of v1, /device:TPU:0, one launch (start us, length us, event | category | flops | bytes accessed | tf_op | source)
XLA Modules:
  0.0 194.3 jit_solution(8707708733538649670)
XLA Ops:
  0.0 3.0 %collective-permute-start.3 = (bf16[320,2048]{1,0:T(8,128)(2,1)}, bf16[320,2048]{1,0:T(8,128)(2,1)}, u32[]{:S(2)}, u32[]{:S(2)}) collective-permute-start(bf16[320,2048]{1,0:T(8,128)(2,1)} %param.29), channel_id=1, source_target_pairs={{0,4},{4,8},{8,12},{12,14},{14,10},{10,6},{6,2},{2,0},{1,5},{5,9},... | collective-permute-start | bytes 3932168 | tf_op jit(solution)/shard_map/ppermute | solution.py:229
  8.7 7.1 %reduce.6 = bf16[32,16384]{1,0:T(8,128)(2,1)S(1)} reduce(bf16[32,1,16384]{2,1,0:T(2,128)(2,1)S(1)} %bitcast.87, bf16[]{:T(256)} %broadcast.77), dimensions={1}, to_apply=%bitcast.70.reduce_sub_computation | reduce | bytes 2097154
  17.5 4.9 %all-to-all-start = ((bf16[8,2,32768]{2,1,0:T(2,128)(2,1)}), bf16[8,2,32768]{2,1,0:T(2,128)(2,1)S(1)}, u32[]{:S(2)}, u32[]{:S(2)}) async-start(bf16[8,2,32768]{2,1,0:T(2,128)(2,1)} %reshape.149), calls=%async_computation | async-start | bytes 2097152 | tf_op jit(solution)/shard_map/all_to_all | solution.py:273
  31.9 5.4 %broadcast_in_dim.67 = bf16[2560,2048]{1,0:T(8,128)(2,1)} broadcast(bf16[]{:T(256)} %constant.116.clone.1), dimensions={} | broadcast | bytes 10485762 | tf_op jit(solution)/shard_map/broadcast_in_dim | solution.py:220
  40.7 8.9 %collective-permute-done.1 = f32[2,60,128]{2,1,0:T(8,128)S(1)} collective-permute-done((f32[2,60,128]{2,1,0:T(8,128)S(1)}, f32[2,60,128]{2,1,0:T(8,128)S(1)}, u32[]{:S(2)}, u32[]{:S(2)}) %collective-permute-start.1) | collective-permute-done | bytes 61472 | tf_op jit(solution)/shard_map/ppermute | solution.py:196
  50.2 4.7 %collective-permute-start.2 = (f32[4,60,128]{2,1,0:T(8,128)}, f32[4,60,128]{2,1,0:T(8,128)S(1)}, u32[]{:S(2)}, u32[]{:S(2)}) collective-permute-start(f32[4,60,128]{2,1,0:T(8,128)} %pad_maximum_fusion.2), channel_id=1, source_target_pairs={{0,8},{2,10},{4,12},{6,14},{8,0},{10,2},{12,4},{14,6},{1,9},{3,11}... | collective-permute-start | bytes 368648 | tf_op jit(solution)/shard_map/ppermute | solution.py:196
  69.6 3.5 %reshape.150 = bf16[32,1,16384]{2,1,0:T(2,128)(2,1)} reshape(bf16[8,2,32768]{2,1,0:T(2,128)(2,1)S(1)} %all-to-all-done) | data formatting | bytes 2097152
  73.1 7.8 %bitcast_reduce_fusion = bf16[32,16384]{1,0:T(8,128)(2,1)S(1)} fusion(bf16[32,1,16384]{2,1,0:T(2,128)(2,1)} %reshape.150), kind=kLoop, calls=%fused_computation.76 | loop fusion | bytes 2097152 | tf_op jit(solution)/shard_map/all_to_all | solution.py:273
  82.1 2.7 %gather_fusion = bf16[8,4,16384]{2,1,0:T(4,128)(2,1)S(1)} fusion(bf16[8,4,16384]{2,1,0:T(4,128)(2,1)} %all_to_all.7, s32[1024]{0:T(1024)S(1)} %pad_clamp_fusion), kind=kCustom, calls=%fused_computation | custom fusion | bytes 2097184 | tf_op jit(solution)/shard_map/jit(_take)/gather | solution.py:274
  86.3 4.4 %all-to-all-start.1 = ((bf16[8,4,16384]{2,1,0:T(4,128)(2,1)}), bf16[8,4,16384]{2,1,0:T(4,128)(2,1)}, u32[]{:S(2)}, u32[]{:S(2)}) async-start(bf16[8,4,16384]{2,1,0:T(4,128)(2,1)} %broadcast_select_fusion), calls=%async_computation.1 | async-start | bytes 2097152 | tf_op jit(solution)/shard_map/all_to_all | solution.py:275
  92.1 10.2 %collective-permute-done.5 = bf16[320,2048]{1,0:T(8,128)(2,1)} collective-permute-done((bf16[320,2048]{1,0:T(8,128)(2,1)}, bf16[320,2048]{1,0:T(8,128)(2,1)}, u32[]{:S(2)}, u32[]{:S(2)}) %collective-permute-start.5) | collective-permute-done | bytes 1310752 | tf_op jit(solution)/shard_map/ppermute | solution.py:229
  104.2 2.9 %collective-permute-start.8 = (bf16[320,2048]{1,0:T(8,128)(2,1)}, bf16[320,2048]{1,0:T(8,128)(2,1)}, u32[]{:S(2)}, u32[]{:S(2)}) collective-permute-start(bf16[320,2048]{1,0:T(8,128)(2,1)} %collective-permute-done.6), channel_id=1, source_target_pairs={{4,0},{8,4},{12,8},{14,12},{10,14},{6,10},{2,6},{0,2},{5,1},{9,5},... | collective-permute-start | bytes 3932168 | tf_op jit(solution)/shard_map/ppermute | solution.py:230
  109.1 11.4 %scan_blocks.1.y_ref = f32[512,2048]{1,0:T(8,128)S(1)} custom-call(bf16[512,2048]{1,0:T(8,128)(2,1)S(1)} %copy-done.2, f32[8,2048]{1,0:T(8,128)S(1)} %concatenate.28.prev_ref, bf16[4,2048]{1,0:T(4,128)(2,1)S(1)} %copy-done.4, f32[4,512,16]{2,1,0:T(8,128)S(1)} %copy.50.cols_ref, f32[32,512]{1,0:T(8,128)S(1)} %get-tuple-element.14.arow_ref, ...), custom_call_target="tpu_custom_call" | custom-call | flops 2147483648 | bytes 6291456 | tf_op jit(solution)/shard_map/scan_blocks/pallas_call | solution.py:101
  120.5 3.5 %constant_dynamic-update-slice_fusion.7 = bf16[2560,2048]{1,0:T(8,128)(2,1)} fusion(bf16[2560,2048]{1,0:T(8,128)(2,1)} %constant_dynamic-update-slice_fusion.8, bf16[320,2048]{1,0:T(8,128)(2,1)} %collective-permute-done.3, s32[]{:T(128)S(6)} %select_n.155), kind=kLoop, calls=%fused_computation.60 | loop fusion | bytes 2621444 | tf_op jit(solution)/shard_map/dynamic_update_slice | solution.py:224
  124.1 2.5 %constant_dynamic-update-slice_fusion.6 = bf16[2560,2048]{1,0:T(8,128)(2,1)} fusion(bf16[2560,2048]{1,0:T(8,128)(2,1)} %constant_dynamic-update-slice_fusion.7, bf16[320,2048]{1,0:T(8,128)(2,1)} %collective-permute-done.4, s32[]{:T(128)S(6)} %select_n.157), kind=kLoop, calls=%fused_computation.59 | loop fusion | bytes 2621444 | tf_op jit(solution)/shard_map/dynamic_update_slice | solution.py:224
  126.6 2.5 %constant_dynamic-update-slice_fusion.5 = bf16[2560,2048]{1,0:T(8,128)(2,1)} fusion(bf16[2560,2048]{1,0:T(8,128)(2,1)} %constant_dynamic-update-slice_fusion.6, bf16[320,2048]{1,0:T(8,128)(2,1)} %collective-permute-done.5, s32[]{:T(128)S(6)} %select_n.159), kind=kLoop, calls=%fused_computation.58 | loop fusion | bytes 2621444 | tf_op jit(solution)/shard_map/dynamic_update_slice | solution.py:224
  129.2 10.6 %collective-permute-done.7 = bf16[320,2048]{1,0:T(8,128)(2,1)} collective-permute-done((bf16[320,2048]{1,0:T(8,128)(2,1)}, bf16[320,2048]{1,0:T(8,128)(2,1)}, u32[]{:S(2)}, u32[]{:S(2)}) %collective-permute-start.7) | collective-permute-done | bytes 1310752 | tf_op jit(solution)/shard_map/ppermute | solution.py:229
  141.7 6.1 %collective-permute-start.9 = (bf16[160,2048]{1,0:T(8,128)(2,1)}, bf16[160,2048]{1,0:T(8,128)(2,1)S(1)}, u32[]{:S(2)}, u32[]{:S(2)}) collective-permute-start(bf16[160,2048]{1,0:T(8,128)(2,1)} %slice.79), channel_id=1, source_target_pairs={{0,4},{4,8},{8,12},{12,14},{14,10},{10,6},{6,2},{2,0},{1,5},{5,9},... | collective-permute-start | bytes 1966088 | tf_op jit(solution)/shard_map/ppermute | solution.py:235
  155.9 4.0 %gate_blocks.1 = (bf16[512,2048]{1,0:T(8,128)(2,1)S(1)}, f32[512,128]{1,0:T(8,128)S(1)}) custom-call(f32[512,2048]{1,0:T(8,128)S(1)} %copy-done.1, bf16[512,2048]{1,0:T(8,128)(2,1)S(1)} %copy-done.3, f32[4,512,8]{2,1,0:T(8,128)S(1)} %bitcast.84, bf16[2048,256]{1,0:T(8,128)(2,1)S(1)} %reshape.131.h_ref, bf16[512,256]{1,0:T(8,128)(2,1)S(1)} %get-tuple-element.11.c_ref, ...), custom_call_target="tpu_custom_call" | custom-call | flops 536870912 | bytes 9437184 | tf_op jit(solution)/shard_map/gate_blocks/pallas_call | solution.py:161
  161.7 2.5 %constant_dynamic-update-slice_fusion.3 = bf16[2560,2048]{1,0:T(8,128)(2,1)} fusion(bf16[2560,2048]{1,0:T(8,128)(2,1)} %constant_dynamic-update-slice_fusion.4, bf16[320,2048]{1,0:T(8,128)(2,1)} %collective-permute-done.7, s32[]{:T(128)S(6)} %select_n.163), kind=kLoop, calls=%fused_computation.56 | loop fusion | bytes 2621444 | tf_op jit(solution)/shard_map/dynamic_update_slice | solution.py:224
  164.2 2.6 %constant_dynamic-update-slice_fusion.2 = bf16[2560,2048]{1,0:T(8,128)(2,1)} fusion(bf16[2560,2048]{1,0:T(8,128)(2,1)} %constant_dynamic-update-slice_fusion.3, bf16[320,2048]{1,0:T(8,128)(2,1)} %collective-permute-done.8, s32[]{:T(128)S(6)} %select_n.165), kind=kLoop, calls=%fused_computation.55 | loop fusion | bytes 2621444 | tf_op jit(solution)/shard_map/dynamic_update_slice | solution.py:224
  167.7 8.8 %collective-permute-done.10 = bf16[160,2048]{1,0:T(8,128)(2,1)S(1)} collective-permute-done((bf16[160,2048]{1,0:T(8,128)(2,1)S(1)}, bf16[160,2048]{1,0:T(8,128)(2,1)S(1)}, u32[]{:S(2)}, u32[]{:S(2)}) %collective-permute-start.10) | collective-permute-done | bytes 655392 | tf_op jit(solution)/shard_map/ppermute | solution.py:236
  177.4 6.5 %fusion.16 = bf16[512,1280]{1,0:T(8,128)(2,1)} fusion(bf16[512,2048]{1,0:T(8,128)(2,1)S(1)} %get-tuple-element.7, bf16[2560,2048]{1,0:T(8,128)(2,1)} %constant_dynamic-update-slice_fusion, s32[]{:T(128)S(6)} %select_n.171), kind=kOutput, calls=%fused_computation.9 | convolution fusion | flops 2685009920 | bytes 8650756 | tf_op jit(solution)/shard_map/dot_general | solution.py:327
  187.1 7.2 %fusion.13 = bf16[512,1280]{1,0:T(8,128)(2,1)} fusion(bf16[512,2048]{1,0:T(8,128)(2,1)} %copy-done.6, bf16[2560,2048]{1,0:T(8,128)(2,1)} %constant_dynamic-update-slice_fusion, s32[]{:T(128)S(6)} %select_n.170, bf16[512,1280]{1,0:T(8,128)(2,1)S(1)} %collective-permute-done.11, f32[512]{0:T(512)S(1)} %add_rsqrt_fusion, pred[512]{0:T(512)(128)(4,1)S(1)} %iota_compare_fusion.3), kind=kOutput, calls=%fused_computation.8 | convolution fusion | flops 2687631360 | bytes 9964036 | tf_op jit(solution)/shard_map/dot_general | solution.py:327
  (126 shorter events, 45.9 us)
Async XLA Ops:
  0.0 67.5 %collective-permute-start.3 = (bf16[320,2048]{1,0:T(8,128)(2,1)}, bf16[320,2048]{1,0:T(8,128)(2,1)}, u32[]{:S(2)}, u32[]{:S(2)}) collective-permute-start(bf16[320,2048]{1,0:T(8,128)(2,1)} %param.29), channel_id=1, source_target_pairs={{0,4},{4,8},{8,12},{12,14},{14,10},{10,6},{6,2},{2,0},{1,5},{5,9},... | collective-permute-start | bytes 3932168 | tf_op jit(solution)/shard_map/ppermute | solution.py:229
  3.0 64.6 %collective-permute-start.4 = (bf16[320,2048]{1,0:T(8,128)(2,1)}, bf16[320,2048]{1,0:T(8,128)(2,1)}, u32[]{:S(2)}, u32[]{:S(2)}) collective-permute-start(bf16[320,2048]{1,0:T(8,128)(2,1)} %param.29), channel_id=1, source_target_pairs={{4,0},{8,4},{12,8},{14,12},{10,14},{6,10},{2,6},{0,2},{5,1},{9,5},... | collective-permute-start | bytes 3932168 | tf_op jit(solution)/shard_map/ppermute | solution.py:230
  3.9 34.6 %collective-permute-start = (f32[1,60,128]{2,1,0:T(8,128)S(1)}, f32[1,60,128]{2,1,0:T(8,128)S(1)}, u32[]{:S(2)}, u32[]{:S(2)}) collective-permute-start(f32[1,60,128]{2,1,0:T(8,128)S(1)} %broadcast_in_dim_reshape.6), channel_id=1, source_target_pairs={{0,2},{2,0},{4,6},{6,4},{8,10},{10,8},{12,14},{14,12},{1,3},{3,1},... | collective-permute-start | bytes 92168 | tf_op jit(solution)/shard_map/ppermute | solution.py:196
  15.8 15.1 %copy-start.18 = (f32[32]{0:T(128)S(1)}, f32[32]{0:T(128)}, u32[]{:S(2)}) copy-start(f32[32]{0:T(128)} %param.25) | copy-start | bytes 388
  15.8 15.1 %copy-start.12 = (f32[512,32]{0,1:T(8,128)S(1)}, f32[512,32]{0,1:T(8,128)}, u32[]{:S(2)}) copy-start(f32[512,32]{0,1:T(8,128)} %param.22) | copy-start | bytes 196612
  15.8 15.8 %copy-start.19 = (s32[8]{0:T(128)S(1)}, s32[8]{0:T(128)}, u32[]{:S(2)}) copy-start(s32[8]{0:T(128)} %param.34) | copy-start | bytes 100
  17.5 52.2 %all-to-all-start = ((bf16[8,2,32768]{2,1,0:T(2,128)(2,1)}), bf16[8,2,32768]{2,1,0:T(2,128)(2,1)S(1)}, u32[]{:S(2)}, u32[]{:S(2)}) async-start(bf16[8,2,32768]{2,1,0:T(2,128)(2,1)} %reshape.149), calls=%async_computation | async-start | bytes 2097152 | tf_op jit(solution)/shard_map/all_to_all | solution.py:273
  37.2 25.3 %copy-start.9 = (bf16[512,512]{1,0:T(8,128)(2,1)S(1)}, bf16[512,512]{1,0:T(8,128)(2,1)}, u32[]{:S(2)}) copy-start(bf16[512,512]{1,0:T(8,128)(2,1)} %param.21) | copy-start | bytes 1572868
  38.4 25.6 %copy-start.16 = (f32[32]{0:T(128)S(1)}, f32[32]{0:T(128)}, u32[]{:S(2)}) copy-start(f32[32]{0:T(128)} %param.27) | copy-start | bytes 388
  38.6 11.0 %collective-permute-start.1 = (f32[2,60,128]{2,1,0:T(8,128)S(1)}, f32[2,60,128]{2,1,0:T(8,128)S(1)}, u32[]{:S(2)}, u32[]{:S(2)}) collective-permute-start(f32[2,60,128]{2,1,0:T(8,128)S(1)} %pad_maximum_fusion.4), channel_id=1, source_target_pairs={{0,4},{2,6},{4,0},{6,2},{8,12},{10,14},{12,8},{14,10},{1,5},{3,7},... | collective-permute-start | bytes 184328 | tf_op jit(solution)/shard_map/ppermute | solution.py:196
  50.2 15.6 %collective-permute-start.2 = (f32[4,60,128]{2,1,0:T(8,128)}, f32[4,60,128]{2,1,0:T(8,128)S(1)}, u32[]{:S(2)}, u32[]{:S(2)}) collective-permute-start(f32[4,60,128]{2,1,0:T(8,128)} %pad_maximum_fusion.2), channel_id=1, source_target_pairs={{0,8},{2,10},{4,12},{6,14},{8,0},{10,2},{12,4},{14,6},{1,9},{3,11}... | collective-permute-start | bytes 368648 | tf_op jit(solution)/shard_map/ppermute | solution.py:196
  67.6 34.7 %collective-permute-start.5 = (bf16[320,2048]{1,0:T(8,128)(2,1)}, bf16[320,2048]{1,0:T(8,128)(2,1)}, u32[]{:S(2)}, u32[]{:S(2)}) collective-permute-start(bf16[320,2048]{1,0:T(8,128)(2,1)} %collective-permute-done.3), channel_id=1, source_target_pairs={{0,4},{4,8},{8,12},{12,14},{14,10},{10,6},{6,2},{2,0},{1,5},{5,9},... | collective-permute-start | bytes 3932168 | tf_op jit(solution)/shard_map/ppermute | solution.py:229
  67.6 36.6 %collective-permute-start.6 = (bf16[320,2048]{1,0:T(8,128)(2,1)}, bf16[320,2048]{1,0:T(8,128)(2,1)}, u32[]{:S(2)}, u32[]{:S(2)}) collective-permute-start(bf16[320,2048]{1,0:T(8,128)(2,1)} %collective-permute-done.4), channel_id=1, source_target_pairs={{4,0},{8,4},{12,8},{14,12},{10,14},{6,10},{2,6},{0,2},{5,1},{9,5},... | collective-permute-start | bytes 3932168 | tf_op jit(solution)/shard_map/ppermute | solution.py:230
  86.3 20.8 %copy-start.11 = (pred[128,128]{1,0:T(8,128)(4,1)S(1)}, pred[128,128]{1,0:T(8,128)(4,1)}, u32[]{:S(2)}) copy-start(pred[128,128]{1,0:T(8,128)(4,1)} %iota_compare_fusion) | copy-start | bytes 49156
  86.3 64.0 %all-to-all-start.1 = ((bf16[8,4,16384]{2,1,0:T(4,128)(2,1)}), bf16[8,4,16384]{2,1,0:T(4,128)(2,1)}, u32[]{:S(2)}, u32[]{:S(2)}) async-start(bf16[8,4,16384]{2,1,0:T(4,128)(2,1)} %broadcast_select_fusion), calls=%async_computation.1 | async-start | bytes 2097152 | tf_op jit(solution)/shard_map/all_to_all | solution.py:275
  90.7 16.8 %slice-start.1 = ((f32[3,2560]{1,0:T(4,128)}), f32[3,2048]{1,0:T(4,128)S(1)}, s32[]{:S(2)}) async-start(f32[3,2560]{1,0:T(4,128)} %copy-done.10), calls=%async_computation.3 | async-start | bytes 65536 | tf_op jit(solution)/shard_map/slice | solution.py:284
  90.7 16.8 %copy-start.4 = (bf16[4,2048]{1,0:T(4,128)(2,1)S(1)}, bf16[4,2048]{1,0:T(4,128)(2,1)}, u32[]{:S(2)}) copy-start(bf16[4,2048]{1,0:T(4,128)(2,1)} %taps_ref.1) | copy-start | bytes 49156
  102.3 37.5 %collective-permute-start.7 = (bf16[320,2048]{1,0:T(8,128)(2,1)}, bf16[320,2048]{1,0:T(8,128)(2,1)}, u32[]{:S(2)}, u32[]{:S(2)}) collective-permute-start(bf16[320,2048]{1,0:T(8,128)(2,1)} %collective-permute-done.5), channel_id=1, source_target_pairs={{0,4},{4,8},{8,12},{12,14},{14,10},{10,6},{6,2},{2,0},{1,5},{5,9},... | collective-permute-start | bytes 3932168 | tf_op jit(solution)/shard_map/ppermute | solution.py:229
  104.2 55.7 %collective-permute-start.8 = (bf16[320,2048]{1,0:T(8,128)(2,1)}, bf16[320,2048]{1,0:T(8,128)(2,1)}, u32[]{:S(2)}, u32[]{:S(2)}) collective-permute-start(bf16[320,2048]{1,0:T(8,128)(2,1)} %collective-permute-done.6), channel_id=1, source_target_pairs={{4,0},{8,4},{12,8},{14,12},{10,14},{6,10},{2,6},{0,2},{5,1},{9,5},... | collective-permute-start | bytes 3932168 | tf_op jit(solution)/shard_map/ppermute | solution.py:230
  141.7 25.1 %collective-permute-start.9 = (bf16[160,2048]{1,0:T(8,128)(2,1)}, bf16[160,2048]{1,0:T(8,128)(2,1)S(1)}, u32[]{:S(2)}, u32[]{:S(2)}) collective-permute-start(bf16[160,2048]{1,0:T(8,128)(2,1)} %slice.79), channel_id=1, source_target_pairs={{0,4},{4,8},{8,12},{12,14},{14,10},{10,6},{6,2},{2,0},{1,5},{5,9},... | collective-permute-start | bytes 1966088 | tf_op jit(solution)/shard_map/ppermute | solution.py:235
  159.9 17.5 %copy-start.6 = (bf16[512,2048]{1,0:T(8,128)(2,1)}, bf16[512,2048]{1,0:T(8,128)(2,1)S(1)}, u32[]{:S(2)}) copy-start(bf16[512,2048]{1,0:T(8,128)(2,1)S(1)} %get-tuple-element.7) | copy-start | bytes 6291460
  161.6 14.9 %collective-permute-start.10 = (bf16[160,2048]{1,0:T(8,128)(2,1)S(1)}, bf16[160,2048]{1,0:T(8,128)(2,1)S(1)}, u32[]{:S(2)}, u32[]{:S(2)}) collective-permute-start(bf16[160,2048]{1,0:T(8,128)(2,1)S(1)} %slice.80), channel_id=1, source_target_pairs={{4,0},{8,4},{12,8},{14,12},{10,14},{6,10},{2,6},{0,2},{5,1},{9,5},... | collective-permute-start | bytes 1966088 | tf_op jit(solution)/shard_map/ppermute | solution.py:236
  183.9 3.2 %collective-permute-start.11 = (bf16[512,1280]{1,0:T(8,128)(2,1)}, bf16[512,1280]{1,0:T(8,128)(2,1)S(1)}, u32[]{:S(2)}, u32[]{:S(2)}) collective-permute-start(bf16[512,1280]{1,0:T(8,128)(2,1)} %fusion.16), channel_id=1, source_target_pairs={{0,1},{1,0},{2,3},{3,2},{4,5},{5,4},{6,7},{7,6},{8,9},{9,8},{10,11... | collective-permute-start | bytes 3932168 | tf_op jit(solution)/shard_map/ppermute | solution.py:331
  184.7 2.2 %collective-permute-start.12 = (f32[512]{0:T(512)S(1)}, f32[512]{0:T(512)S(1)}, u32[]{:S(2)}, u32[]{:S(2)}) collective-permute-start(f32[512]{0:T(512)S(1)} %reduce_sum.22), channel_id=1, source_target_pairs={{0,1},{1,0},{2,3},{3,2},{4,5},{5,4},{6,7},{7,6},{8,9},{9,8},{10,11... | collective-permute-start | bytes 6152 | tf_op jit(solution)/shard_map/ppermute | solution.py:323
  (15 other events, 121.3 us)

commit v2 on v1

--- a/solution.py
+++ b/solution.py
@@ -153,36 +153,144 @@
         sq_ref[rows, :] = total
 
 
-def gate_call(y, z, cols, h, c, gain):
+def gate_call(y, z, cols, h, c, gain, first):
     tokens, channels = y.shape
-    groups = cols.shape[0]
-    lanes = channels // groups
+    lanes = channels // cols.shape[0]
+    groups = h.shape[0] // lanes
     n = c.shape[1]
     return pl.pallas_call(
         gate_kernel,
         grid=(groups,),
         in_specs=[
-            pl.BlockSpec((tokens, lanes), lambda i: (0, i)),
-            pl.BlockSpec((tokens, lanes), lambda i: (0, i)),
-            pl.BlockSpec((None, tokens, GROUP), lambda i: (i, 0, 0)),
+            pl.BlockSpec((tokens, lanes), lambda i: (0, first + i)),
+            pl.BlockSpec((tokens, lanes), lambda i: (0, first + i)),
+            pl.BlockSpec((None, tokens, GROUP), lambda i: (first + i, 0, 0)),
             pl.BlockSpec((lanes, n), lambda i: (i, 0)),
             pl.BlockSpec((tokens, n), lambda i: (0, 0)),
-            pl.BlockSpec((1, lanes), lambda i: (0, i)),
+            pl.BlockSpec((1, lanes), lambda i: (0, first + i)),
         ],
         out_specs=[
             pl.BlockSpec((tokens, lanes), lambda i: (0, i)),
             pl.BlockSpec((tokens, 128), lambda i: (0, 0)),
         ],
         out_shape=[
-            jax.ShapeDtypeStruct((tokens, channels), jnp.bfloat16),
+            jax.ShapeDtypeStruct((tokens, groups * lanes), jnp.bfloat16),
             jax.ShapeDtypeStruct((tokens, 128), jnp.float32),
         ],
         compiler_params=pltpu.CompilerParams(vmem_limit_bytes=40 * 2**20),
         cost_estimate=pl.CostEstimate(
-            flops=2 * tokens * channels * 256, bytes_accessed=tokens * channels * 9, transcendentals=tokens * channels * 2
+            flops=2 * tokens * groups * lanes * 256,
+            bytes_accessed=tokens * groups * lanes * 9,
+            transcendentals=tokens * groups * lanes * 2,
         ),
         name="gate_blocks",
     )(y, z, cols, h, c, gain)
+
+
+def assemble_kernel(count, rows_ref, *refs):
+    pieces, out_ref, sems = refs[:count], refs[count], refs[count + 1]
+    copies = []
+    for i, piece in enumerate(pieces):
+        at = pl.multiple_of(rows_ref[i], 16)
+        copies.append(
+            pltpu.make_async_copy(piece, out_ref.at[pl.ds(at, piece.shape[0]), :], sems.at[i])
+        )
+    for copy in copies:
+        copy.start()
+    for copy in copies:
+        copy.wait()
+
+
+def assemble(pieces, rows):
+    total = sum(piece.shape[0] for piece in pieces)
+    return pl.pallas_call(
+        functools.partial(assemble_kernel, len(pieces)),
+        in_specs=[pl.BlockSpec(memory_space=pltpu.SMEM)]
+        + [pl.BlockSpec(memory_space=pl.ANY)] * len(pieces),
+        out_specs=pl.BlockSpec(memory_space=pl.ANY),
+        out_shape=jax.ShapeDtypeStruct((total, pieces[0].shape[1]), pieces[0].dtype),
+        scratch_shapes=[pltpu.SemaphoreType.DMA((len(pieces),))],
+        compiler_params=pltpu.CompilerParams(vmem_limit_bytes=16 * 2**20),
+        cost_estimate=pl.CostEstimate(
+            flops=0, bytes_accessed=2 * total * pieces[0].shape[1] * 2, transcendentals=0
+        ),
+        name="assemble_rows",
+    )(jnp.stack(rows).astype(jnp.int32), *pieces)
+
+
+def project_kernel(a_ref, b_ref, w_ref, send_ref, keep_ref):
+    depth = a_ref.shape[1]
+    part = lax.dot_general(
+        a_ref[...], w_ref[:, :depth], (((1,), (1,)), ((), ())), preferred_element_type=jnp.float32
+    ) + lax.dot_general(
+        b_ref[...], w_ref[:, depth:], (((1,), (1,)), ((), ())), preferred_element_type=jnp.float32
+    )
+
+    @pl.when(pl.program_id(0) == 0)
+    def _():
+        send_ref[...] = part.astype(jnp.bfloat16)
+
+    @pl.when(pl.program_id(0) == 1)
+    def _():
+        keep_ref[...] = part
+
+
+def project(a, b, weight):
+    tokens = a.shape[0]
+    rows, channels = weight.shape
+    half = rows // 2
+    return pl.pallas_call(
+        project_kernel,
+        grid=(2,),
+        in_specs=[
+            pl.BlockSpec(a.shape, lambda i: (0, 0)),
+            pl.BlockSpec(b.shape, lambda i: (0, 0)),
+            pl.BlockSpec((half, channels), lambda i: (1 - i, 0)),
+        ],
+        out_specs=[
+            pl.BlockSpec((tokens, half), lambda i: (0, 0)),
+            pl.BlockSpec((tokens, half), lambda i: (0, 0)),
+        ],
+        out_shape=[
+            jax.ShapeDtypeStruct((tokens, half), jnp.bfloat16),
+            jax.ShapeDtypeStruct((tokens, half), jnp.float32),
+        ],
+        compiler_params=pltpu.CompilerParams(vmem_limit_bytes=40 * 2**20),
+        cost_estimate=pl.CostEstimate(
+            flops=2 * tokens * rows * channels,
+            bytes_accessed=2 * (rows + tokens) * channels,
+            transcendentals=0,
+        ),
+        name="project_rows",
+    )(a, b, weight)
+
+
+def combine_kernel(width, odd_ref, keep_ref, other_ref, back_ref, scale_ref, out_ref):
+    mine = (keep_ref[...] + other_ref[...].astype(jnp.float32)) * scale_ref[...]
+    back = back_ref[...].astype(jnp.float32) * scale_ref[...]
+    even = odd_ref[0] == 0
+    for i in range(mine.shape[1] // width):
+        cols = slice(i * width, (i + 1) * width)
+        first = jnp.where(even, mine[:, cols], back[:, cols])
+        second = jnp.where(even, back[:, cols], mine[:, cols])
+        out_ref[:, 2 * i * width : (2 * i + 2) * width] = jnp.concatenate(
+            [first, second], axis=1
+        ).astype(jnp.bfloat16)
+
+
+def combine(odd, keep, other, back, scale, width):
+    tokens, half = keep.shape
+    return pl.pallas_call(
+        functools.partial(combine_kernel, width),
+        grid=(tokens // BLOCK,),
+        in_specs=[pl.BlockSpec(memory_space=pltpu.SMEM)]
+        + [pl.BlockSpec((BLOCK, half), lambda i: (i, 0))] * 3
+        + [pl.BlockSpec((BLOCK, 1), lambda i: (i, 0))],
+        out_specs=pl.BlockSpec((BLOCK, 2 * half), lambda i: (i, 0)),
+        out_shape=jax.ShapeDtypeStruct((tokens, 2 * half), jnp.bfloat16),
+        compiler_params=pltpu.CompilerParams(vmem_limit_bytes=16 * 2**20),
+        name="combine_blocks",
+    )(odd, keep, other, back, scale)
 
 
 def gather_all(value, axis):
@@ -202,39 +310,71 @@
     return held
 
 
-def ring_order(n):
-    if n == 8:
-        return [0, 2, 4, 6, 7, 5, 3, 1]
-    return list(range(n))
-
-
-def ring_gather(block, axis):
-    n = lax.axis_size(axis)
+def gather_parity(block, core):
+    n = lax.axis_size("cache")
+    me = lax.axis_index("cache")
     rows = block.shape[0]
-    order = ring_order(n)
-    place = [order.index(i) for i in range(n)]
-    ahead = [(order[i], order[(i + 1) % n]) for i in range(n)]
-    back = [(b, a) for a, b in ahead]
-    me = jnp.asarray(place)[lax.axis_index(axis)]
-    ids = jnp.asarray(order)
-    full = jnp.zeros((n * rows, block.shape[1]), block.dtype)
-
-    def put(full, piece, offset, first=0):
-        at = ids[lax.rem(me + offset + n, n)] * rows + first
-        return lax.dynamic_update_slice(full, piece, (at, 0))
-
-    full = put(full, block, 0)
+    m = n // 2
+    odd, spot = me % 2, me // 2
+
+    def row(index, first=0):
+        return lax.rem(index + m - core * (m // 2), m) * rows + first
+
+    def swap(value, pairs):
+        return lax.ppermute(
+            value, "cache", [(2 * i + p, 2 * j + p) for i, j in pairs for p in (0, 1)]
+        )
+
+    if m == 4 and lax.axis_size("groups") == 2 and rows % 32 == 0:
+        part = rows // 2
+        side = lax.axis_index("groups")
+        inner = (spot == 1) | (spot == 2)
+        own = lax.dynamic_slice_in_dim(block, side * part, part, 0)
+
+        def across(value):
+            return lax.ppermute(value, "groups", [(0, 1), (1, 0)])
+
+        pairs = [(0, 1), (1, 0), (2, 3), (3, 2)]
+        middle = [(1, 2), (2, 1)]
+        outward = [(1, 0), (2, 3)]
+        mate, far = swap(own, pairs), swap(own, middle)
+        mate, far = lax.optimization_barrier((mate, far))
+        mate_other = across(mate)
+        far_out, end = swap(far, outward), swap(mate, middle)
+        far_out, end = lax.optimization_barrier((far_out, end))
+        far = jnp.where(inner, far, far_out)
+        far_other = across(far)
+        end_out = swap(end, outward)
+        end_out, mate_other = lax.optimization_barrier((end_out, mate_other))
+        end = jnp.where(inner, end, end_out)
+        end_other = across(end)
+        at_far = jnp.where(spot < 2, 2, 1)
+        at_end = jnp.where(spot < 2, 3, 0)
+        here, there = side * part, (1 - side) * part
+        pieces = [block, mate, mate_other, far, far_other, end, end_other]
+        places = [
+            row(spot),
+            row(spot ^ 1, here),
+            row(spot ^ 1, there),
+            row(at_far, here),
+            row(at_far, there),
+            row(at_end, here),
+            row(at_end, there),
+        ]
+        return pieces, places
+    ahead = [(i, (i + 1) % m) for i in range(m)]
+    back = [(j, i) for i, j in ahead]
+    pieces, places = [block], [row(spot)]
     a = b = block
-    for k in range(1, (n - 1) // 2 + 1):
-        a = lax.ppermute(a, axis, ahead)
-        b = lax.ppermute(b, axis, back)
-        full = put(put(full, a, -k), b, k)
-    if n % 2 == 0:
-        k = n // 2
-        half = rows // 2
-        full = put(full, lax.ppermute(a[:half], axis, ahead), -k)
-        full = put(full, lax.ppermute(b[half:], axis, back), k, half)
-    return full
+    for k in range(1, m // 2 + 1):
+        a = swap(a, ahead)
+        pieces.append(a)
+        places.append(row(lax.rem(spot + m - k, m)))
+        if 2 * k < m:
+            b = swap(b, back)
+            pieces.append(b)
+            places.append(row(lax.rem(spot + k, m)))
+    return pieces, places
 
 
 def body(
@@ -269,11 +409,16 @@
     row_at = jnp.sum(position_hits * row_of[None, :], axis=1)
     row_here = row_at[lax.axis_index("cache")]
 
-    states = store_ssm.astype(jnp.bfloat16).reshape(local_slots, heads, width * n)
-    states = lax.all_to_all(states, "cache", split_axis=1, concat_axis=0, tiled=True)
-    states = jnp.take(states, row_at, axis=0)
-    start = lax.all_to_all(states, "cache", split_axis=0, concat_axis=1, tiled=True)
-    start = start.reshape(channels, n)
+    share = channels // (2 * ncache)
+    states = store_ssm.astype(jnp.bfloat16).reshape(local_slots, 2, ncache, share, n)
+    states = states.transpose(2, 0, 1, 3, 4)
+    states = lax.all_to_all(states, "cache", split_axis=0, concat_axis=0, tiled=True)
+    states = states.reshape(ncache * local_slots, 2, share, n)
+    starts = []
+    for part in range(2):
+        chosen = jnp.take(states[:, part], row_at, axis=0)
+        chosen = lax.all_to_all(chosen, "cache", split_axis=0, concat_axis=0, tiled=True)
+        starts.append(chosen.reshape(channels // 2, n))
 
     small = jnp.concatenate([stored_conv_inputs, store_convbc], axis=2)
     small = gather_all(small.reshape(-1, 128), "cache")
@@ -284,7 +429,9 @@
         [jnp.zeros((8 - taps_prev, channels), jnp.float32), small[:, :channels]], axis=0
     )
 
-    weight = ring_gather(out_weight, "cache")
+    core = lax.axis_index("tensor")
+    pieces, places = gather_parity(out_weight, core)
+    weight = assemble(pieces, places)
 
     bcs = conv_silu(small[:, channels:], bc_in, conv_bc)
     b = bcs[:, :n]
@@ -314,25 +461,27 @@
     cols = jnp.concatenate([grouped(cum), grouped(acol)], axis=2)
     skip = jnp.repeat(d_skip, width)[None, :]
     y = scan_call(x_in, prev_x, conv_x, cols, acol.T, skip, g, b.T, c)
-    gated, squares = gate_call(y, z_in, grouped(whole), start, c, norm_gain[None, :])
-
-    swap = [(0, 1), (1, 0)]
-    half = weight.shape[0] // 2
-    core = lax.axis_index("tensor")
-    squares = jnp.sum(squares, axis=1)
-    squares = squares + lax.ppermute(squares, "tensor", swap)
-
-    def project(index):
-        part = lax.dynamic_slice_in_dim(weight, index * half, half, 0)
-        return lax.dot_general(
-            gated, part, (((1,), (1,)), ((), ())), preferred_element_type=jnp.float32
-        )
-
-    other = lax.ppermute(project(1 - core).astype(jnp.bfloat16), "tensor", swap)
-    summed = project(core) + other.astype(jnp.float32)
-    mixed = summed * lax.rsqrt(squares / INNER + 1e-05)[:, None]
+    whole = grouped(whole)
+    gain = norm_gain[None, :]
+    cores = [(0, 1), (1, 0)]
+    partners = [(i, i ^ 1) for i in range(ncache)]
+    gated_a, squares_a = gate_call(y, z_in, whole, starts[0], c, gain, 0)
+    theirs_a = lax.ppermute(gated_a, "cache", partners)
+    gated_b, squares_b = gate_call(y, z_in, whole, starts[1], c, gain, groups // 2)
+    theirs_b = lax.ppermute(gated_b, "cache", partners)
+    squares = jnp.sum(squares_a + squares_b, axis=1)
+    squares = squares + lax.ppermute(squares, "tensor", cores)
     valid = jnp.arange(tokens) < lengths[0]
-    return jnp.where(valid[:, None], mixed, 0.0).astype(jnp.bfloat16)
+    scale = jnp.where(valid, lax.rsqrt(squares / INNER + 1e-05), 0.0)[:, None]
+
+    send, keep = project(gated_a, gated_b, weight)
+    other = lax.ppermute(send, "tensor", cores)
+    send, keep_back = project(theirs_a, theirs_b, weight)
+    other_back = lax.ppermute(send, "tensor", cores)
+    back = (keep_back + other_back.astype(jnp.float32)).astype(jnp.bfloat16)
+    back = lax.ppermute(back, "cache", partners)
+    odd = (lax.axis_index("cache") % 2).astype(jnp.int32)[None]
+    return combine(odd, keep, other, back, scale, out_weight.shape[0])
 
 
 def solution(mesh):

time: 195 us -> 206 us (1.056)
  waiting for transfers between devices: 42.2 us -> 99.2 us
  local copies, waits for them, and re-layouts: 58.8 us -> 23.2 us
  Pallas kernels: 15.4 us -> 32.6 us
  matrix products: 14.1 us -> 0.51 us
  between operations: 14.8 us -> 2.94 us
  other arithmetic: 16.2 us -> 6.46 us
  starting transfers between devices: 32.8 us -> 38.8 us
    ppermute x10 -> x14, waiting for transfers between devices: 33.3 us -> 64.5 us  [the longest x1 19.7 us: body(): theirs_a = lax.ppermute(gated_a, 'cache', partners)]
    dynamic_update_slice x9 -> x0, local copies, waits for them, and re-layouts: 19.3 us -> none  [put(): return lax.dynamic_update_slice(full, piece, (at, 0))]
    ppermute x3, waiting for transfers between devices: 8.92 us -> 24 us  [gather_all(): other = lax.ppermute(held, axis, [(i, i ^ step) for i in range(n)])]
    pallas_call x0 -> x4, Pallas kernels: none -> 15 us  [the longest x2 10.7 us: project(): pl.pallas_call(project_kernel, grid=(2,), in_specs=[pl.BlockSpec(a.shape,...]
    dot_general x2 -> x0, matrix products: 13.6 us -> none  [project(): lax.dot_general(gated, part, (((1,), (1,)), ((), ())), preferred_element_...]
    all_to_all x2 -> x3, waiting for transfers between devices: 0.01 us -> 10.6 us  [the longest x2 10.6 us: body(): lax.all_to_all(chosen, 'cache', split_axis=0, concat_axis=0, tiled=True)]
    all_to_all x2 -> x0, local copies, waits for them, and re-layouts: 9.01 us -> none  [body(): lax.all_to_all(states, 'cache', split_axis=1, concat_axis=0, tiled=True)]
    unnamed x1 -> x0, other arithmetic: 7.05 us -> none
  transfers between devices with their start and end apart: 15 -> 20, of which waited for: 7 -> 10; matrix products, arithmetic and copies ran while one was open for 35% -> 8% of each run, Pallas kernels for 8% -> 12%
where the time goes in v2:
time: 206 us; the launch traced here: 204 us
  waiting for transfers between devices  99.2 us (48%)
  starting transfers between devices  38.8 us (19%)
  Pallas kernels  32.6 us (16%)
  local copies, waits for them, and re-layouts  23.2 us (11%)
  other arithmetic  6.46 us (3%)
  between operations  2.94 us (1%)
    ppermute x3, waiting for transfers between devices, gather_all(): other = lax.ppermute(held, axis, [(i, i ^ step) for i in range(n)])  24 us
    ppermute x1, waiting for transfers between devices, body(): theirs_a = lax.ppermute(gated_a, 'cache', partners)  19.7 us
    ppermute x1, waiting for transfers between devices, body(): back = lax.ppermute(back, 'cache', partners)  14.8 us
    ppermute x3, waiting for transfers between devices, across(): return lax.ppermute(value, 'groups', [(0, 1), (1, 0)])  12.7 us
    unnamed x62, local copies, waits for them, and re-layouts  11.9 us
    pallas_call x1, Pallas kernels, scan_call(): pl.pallas_call(scan_kernel, grid=(groups,), in_specs=[pl.BlockSpec((token...  11.3 us
    pallas_call x2, Pallas kernels, project(): pl.pallas_call(project_kernel, grid=(2,), in_specs=[pl.BlockSpec(a.shape,...  10.7 us
    all_to_all x2, waiting for transfers between devices, body(): lax.all_to_all(chosen, 'cache', split_axis=0, concat_axis=0, tiled=True)  10.6 us
  transfers between devices with their start and end apart: 20, of which 10 were waited for; matrix products, arithmetic and copies ran while one was open for 8% of the time, Pallas kernels for 12%

profile of v2, /device:TPU:0, one launch (start us, length us, event | category | flops | bytes accessed | tf_op | source)
XLA Modules:
  0.0 203.8 jit_solution(3299632482459137375)
XLA Ops:
  0.0 2.0 constant_dynamic-slice_fusion
  2.0 3.0 %collective-permute-start.3 = (bf16[160,2048]{1,0:T(8,128)(2,1)}, bf16[160,2048]{1,0:T(8,128)(2,1)}, u32[]{:S(2)}, u32[]{:S(2)}) collective-permute-start(bf16[160,2048]{1,0:T(8,128)(2,1)} %constant_dynamic-slice_fusion), channel_id=1, source_target_pairs={{0,4},{2,6},{4,0},{6,2},{8,12},{10,14},{12,8},{14,10},{1,5},{3,7},... | collective-permute-start | bytes 1966088 | tf_op jit(solution)/shard_map/ppermute | solution.py:324
  11.1 5.0 %all-to-all-start = ((bf16[8,1,2,128,256]{4,3,2,1,0:T(8,128)(2,1)}), bf16[8,1,2,128,256]{4,3,2,1,0:T(8,128)(2,1)}, u32[]{:S(2)}, u32[]{:S(2)}) async-start(bf16[8,1,2,128,256]{4,3,2,1,0:T(8,128)(2,1)} %copy.55), calls=%async_computation | async-start | bytes 2097152 | tf_op jit(solution)/shard_map/all_to_all | solution.py:415
  17.3 3.0 %collective-permute-start.1 = (f32[2,60,128]{2,1,0:T(8,128)S(1)}, f32[2,60,128]{2,1,0:T(8,128)S(1)}, u32[]{:S(2)}, u32[]{:S(2)}) collective-permute-start(f32[2,60,128]{2,1,0:T(8,128)S(1)} %pad_maximum_fusion.4), channel_id=1, source_target_pairs={{0,4},{2,6},{4,0},{6,2},{8,12},{10,14},{12,8},{14,10},{1,5},{3,7},... | collective-permute-start | bytes 184328 | tf_op jit(solution)/shard_map/ppermute | solution.py:304
  20.3 17.3 %collective-permute-done.1 = f32[2,60,128]{2,1,0:T(8,128)S(1)} collective-permute-done((f32[2,60,128]{2,1,0:T(8,128)S(1)}, f32[2,60,128]{2,1,0:T(8,128)S(1)}, u32[]{:S(2)}, u32[]{:S(2)}) %collective-permute-start.1) | collective-permute-done | bytes 61472 | tf_op jit(solution)/shard_map/ppermute | solution.py:304
  37.6 3.6 %collective-permute-start.2 = (f32[4,60,128]{2,1,0:T(8,128)S(1)}, f32[4,60,128]{2,1,0:T(8,128)S(1)}, u32[]{:S(2)}, u32[]{:S(2)}) collective-permute-start(f32[4,60,128]{2,1,0:T(8,128)S(1)} %pad_maximum_fusion.2), channel_id=1, source_target_pairs={{0,8},{2,10},{4,12},{6,14},{8,0},{10,2},{12,4},{14,6},{1,9},{3,11}... | collective-permute-start | bytes 368648 | tf_op jit(solution)/shard_map/ppermute | solution.py:304
  45.5 6.7 %collective-permute-done.2 = f32[4,60,128]{2,1,0:T(8,128)S(1)} collective-permute-done((f32[4,60,128]{2,1,0:T(8,128)S(1)}, f32[4,60,128]{2,1,0:T(8,128)S(1)}, u32[]{:S(2)}, u32[]{:S(2)}) %collective-permute-start.2) | collective-permute-done | bytes 122912 | tf_op jit(solution)/shard_map/ppermute | solution.py:304
  52.3 2.1 %slice_bitcast_fusion = (bf16[8,128,256]{2,1,0:T(8,128)(2,1)}, bf16[8,128,256]{2,1,0:T(8,128)(2,1)S(1)}) fusion(bf16[8,2,128,256]{3,2,1,0:T(8,128)(2,1)} %bitcast.21), kind=kLoop, calls=%fused_computation.18 | loop fusion | bytes 2097152 | tf_op jit(solution)/shard_map/squeeze | solution.py:419
  57.8 4.9 %all-to-all-start.2 = ((bf16[8,128,256]{2,1,0:T(8,128)(2,1)}), bf16[8,128,256]{2,1,0:T(8,128)(2,1)S(1)}, u32[]{:S(2)}, u32[]{:S(2)}) async-start(bf16[8,128,256]{2,1,0:T(8,128)(2,1)} %get-tuple-element.51), calls=%async_computation.2 | async-start | bytes 1048576 | tf_op jit(solution)/shard_map/all_to_all | solution.py:420
  67.3 10.6 %all-to-all-done.2 = bf16[8,128,256]{2,1,0:T(8,128)(2,1)S(1)} async-done(((bf16[8,128,256]{2,1,0:T(8,128)(2,1)}), bf16[8,128,256]{2,1,0:T(8,128)(2,1)S(1)}, u32[]{:S(2)}, u32[]{:S(2)}) %all-to-all-start.2) | async-done | bytes 524320 | tf_op jit(solution)/shard_map/all_to_all | solution.py:420
  77.9 4.1 %all-to-all-start.1 = ((bf16[8,128,256]{2,1,0:T(8,128)(2,1)}), bf16[8,128,256]{2,1,0:T(8,128)(2,1)}, u32[]{:S(2)}, u32[]{:S(2)}) async-start(bf16[8,128,256]{2,1,0:T(8,128)(2,1)} %get-tuple-element.52), calls=%async_computation.1 | async-start | bytes 1048576 | tf_op jit(solution)/shard_map/all_to_all | solution.py:420
  83.9 7.4 %collective-permute-done.5 = bf16[160,2048]{1,0:T(8,128)(2,1)S(1)} collective-permute-done((bf16[160,2048]{1,0:T(8,128)(2,1)}, bf16[160,2048]{1,0:T(8,128)(2,1)S(1)}, u32[]{:S(2)}, u32[]{:S(2)}) %collective-permute-start.5) | collective-permute-done | bytes 655392 | tf_op jit(solution)/shard_map/ppermute | solution.py:324
  97.2 11.3 %scan_blocks.1.y_ref = f32[512,2048]{1,0:T(8,128)S(1)} custom-call(bf16[512,2048]{1,0:T(8,128)(2,1)S(1)} %copy-done.5, f32[8,2048]{1,0:T(8,128)S(1)} %concatenate.28.prev_ref, bf16[4,2048]{1,0:T(4,128)(2,1)S(1)} %copy-done.16, f32[4,512,16]{2,1,0:T(8,128)S(1)} %copy-done.3, f32[32,512]{1,0:T(8,128)S(1)} %get-tuple-element.41.arow_ref, ...), custom_call_target="tpu_custom_call" | custom-call | flops 2147483648 | bytes 6291456 | tf_op jit(solution)/shard_map/scan_blocks/pallas_call | solution.py:101
  114.5 2.8 %gate_blocks.3 = (bf16[512,1024]{1,0:T(8,128)(2,1)}, f32[512,128]{1,0:T(8,128)S(1)}) custom-call(f32[512,2048]{1,0:T(8,128)S(1)} %scan_blocks.1.y_ref, bf16[512,2048]{1,0:T(8,128)(2,1)S(1)} %copy-done.2, f32[4,512,8]{2,1,0:T(8,128)S(1)} %bitcast.72, bf16[1024,256]{1,0:T(8,128)(2,1)S(1)} %bitcast.75, bf16[512,256]{1,0:T(8,128)(2,1)S(1)} %get-tuple-element.38.c_ref, ...), custom_call_target="tpu_custom_call" | custom-call | flops 268435456 | bytes 4718592 | tf_op jit(solution)/shard_map/gate_blocks/pallas_call | solution.py:161
  120.0 2.2 %copy-done.1 = f32[512,2048]{1,0:T(8,128)S(1)} copy-done((f32[512,2048]{1,0:T(8,128)S(1)}, f32[512,2048]{1,0:T(8,128)}, u32[]{:S(2)}) %copy-start.1) | copy-done | bytes 4194328
  122.2 3.5 %gate_blocks.2 = (bf16[512,1024]{1,0:T(8,128)(2,1)}, f32[512,128]{1,0:T(8,128)S(1)}) custom-call(f32[512,2048]{1,0:T(8,128)S(1)} %copy-done.1, bf16[512,2048]{1,0:T(8,128)(2,1)S(1)} %copy-done.2, f32[4,512,8]{2,1,0:T(8,128)S(1)} %bitcast.73, bf16[1024,256]{1,0:T(8,128)(2,1)} %bitcast.23.h_ref, bf16[512,256]{1,0:T(8,128)(2,1)S(1)} %get-tuple-element.38.c_ref, ...), custom_call_target="tpu_custom_call" | custom-call | flops 268435456 | bytes 4718592 | tf_op jit(solution)/shard_map/gate_blocks/pallas_call | solution.py:161
  130.2 12.7 %collective-permute-done.10.refs_6_ = bf16[160,2048]{1,0:T(8,128)(2,1)S(1)} collective-permute-done((bf16[160,2048]{1,0:T(8,128)(2,1)S(1)}, bf16[160,2048]{1,0:T(8,128)(2,1)S(1)}, u32[]{:S(2)}, u32[]{:S(2)}) %collective-permute-start.10) | collective-permute-done | bytes 655392 | tf_op jit(solution)/shard_map/ppermute | solution.py:335
  142.9 2.2 %assemble_rows.1.w_ref = bf16[1280,2048]{1,0:T(8,128)(2,1)S(1)} custom-call(s32[7]{0:T(128)S(1)} %stack.31.rows_ref, bf16[320,2048]{1,0:T(8,128)(2,1)S(1)} %copy-done.4, bf16[160,2048]{1,0:T(8,128)(2,1)} %collective-permute-done.3.refs_1_, bf16[160,2048]{1,0:T(8,128)(2,1)S(1)} %copy-done.10, bf16[160,2048]{1,0:T(8,128)(2,1)} %broadcast_select_fusion.1.refs_3_, ...), custom_call_target="tpu_custom_call" | custom-call | bytes 10485760 | tf_op jit(solution)/shard_map/assemble_rows/pallas_call | solution.py:206
  145.2 7.7 %collective-permute-done.13.b_ref = bf16[512,1024]{1,0:T(8,128)(2,1)} collective-permute-done((bf16[512,1024]{1,0:T(8,128)(2,1)}, bf16[512,1024]{1,0:T(8,128)(2,1)}, u32[]{:S(2)}, u32[]{:S(2)}) %collective-permute-start.13) | collective-permute-done | bytes 1048608 | tf_op jit(solution)/shard_map/ppermute | solution.py:471
  152.8 19.7 %collective-permute-done.12.a_ref = bf16[512,1024]{1,0:T(8,128)(2,1)} collective-permute-done((bf16[512,1024]{1,0:T(8,128)(2,1)}, bf16[512,1024]{1,0:T(8,128)(2,1)}, u32[]{:S(2)}, u32[]{:S(2)}) %collective-permute-start.12) | collective-permute-done | bytes 1048608 | tf_op jit(solution)/shard_map/ppermute | solution.py:469
  172.5 5.4 %project_rows.3 = (bf16[512,640]{1,0:T(8,128)(2,1)S(1)}, f32[512,640]{1,0:T(8,128)S(1)}) custom-call(bf16[512,1024]{1,0:T(8,128)(2,1)} %collective-permute-done.12.a_ref, bf16[512,1024]{1,0:T(8,128)(2,1)} %collective-permute-done.13.b_ref, bf16[1280,2048]{1,0:T(8,128)(2,1)S(1)} %assemble_rows.1.w_ref), custom_call_target="tpu_custom_call" | custom-call | flops 2684354560 | bytes 7340032 | tf_op jit(solution)/shard_map/project_rows/pallas_call | solution.py:242
  177.9 5.4 %project_rows.2 = (bf16[512,640]{1,0:T(8,128)(2,1)S(1)}, f32[512,640]{1,0:T(8,128)S(1)}) custom-call(bf16[512,1024]{1,0:T(8,128)(2,1)} %get-tuple-element.20.a_ref, bf16[512,1024]{1,0:T(8,128)(2,1)} %get-tuple-element.21.b_ref, bf16[1280,2048]{1,0:T(8,128)(2,1)S(1)} %assemble_rows.1.w_ref), custom_call_target="tpu_custom_call" | custom-call | flops 2684354560 | bytes 7340032 | tf_op jit(solution)/shard_map/project_rows/pallas_call | solution.py:242
  186.9 14.8 %collective-permute-done.15.back_ref = bf16[512,640]{1,0:T(8,128)(2,1)S(1)} collective-permute-done((bf16[512,640]{1,0:T(8,128)(2,1)}, bf16[512,640]{1,0:T(8,128)(2,1)S(1)}, u32[]{:S(2)}, u32[]{:S(2)}) %collective-permute-start.15) | collective-permute-done | bytes 655392 | tf_op jit(solution)/shard_map/ppermute | solution.py:482
  201.7 2.1 %combine_blocks.1 = bf16[512,1280]{1,0:T(8,128)(2,1)} custom-call(s32[1]{0:T(128)} %bitcast.odd_ref, f32[512,640]{1,0:T(8,128)S(1)} %get-tuple-element.28.keep_ref, bf16[512,640]{1,0:T(8,128)(2,1)S(1)} %collective-permute-done.11.other_ref, bf16[512,640]{1,0:T(8,128)(2,1)S(1)} %collective-permute-done.15.back_ref, f32[512,1]{1,0:T(8,128)S(1)} %copy.56.scale_ref), custom_call_target="tpu_custom_call" | custom-call | tf_op jit(solution)/shard_map/combine_blocks/pallas_call | solution.py:283
  (141 shorter events, 41.5 us)
Async XLA Ops:
  2.0 60.8 %collective-permute-start.3 = (bf16[160,2048]{1,0:T(8,128)(2,1)}, bf16[160,2048]{1,0:T(8,128)(2,1)}, u32[]{:S(2)}, u32[]{:S(2)}) collective-permute-start(bf16[160,2048]{1,0:T(8,128)(2,1)} %constant_dynamic-slice_fusion), channel_id=1, source_target_pairs={{0,4},{2,6},{4,0},{6,2},{8,12},{10,14},{12,8},{14,10},{1,5},{3,7},... | collective-permute-start | bytes 1966088 | tf_op jit(solution)/shard_map/ppermute | solution.py:324
  5.0 57.8 %collective-permute-start.4 = (bf16[160,2048]{1,0:T(8,128)(2,1)}, bf16[160,2048]{1,0:T(8,128)(2,1)}, u32[]{:S(2)}, u32[]{:S(2)}) collective-permute-start(bf16[160,2048]{1,0:T(8,128)(2,1)} %constant_dynamic-slice_fusion), channel_id=1, source_target_pairs={{4,8},{6,10},{8,4},{10,6},{5,9},{7,11},{9,5},{11,7},{20,24},{22,26... | collective-permute-start | bytes 1966088 | tf_op jit(solution)/shard_map/ppermute | solution.py:324
  6.7 10.6 %collective-permute-start = (f32[1,60,128]{2,1,0:T(8,128)S(1)}, f32[1,60,128]{2,1,0:T(8,128)S(1)}, u32[]{:S(2)}, u32[]{:S(2)}) collective-permute-start(f32[1,60,128]{2,1,0:T(8,128)S(1)} %broadcast_in_dim_reshape.6), channel_id=1, source_target_pairs={{0,2},{2,0},{4,6},{6,4},{8,10},{10,8},{12,14},{14,12},{1,3},{3,1},... | collective-permute-start | bytes 92168 | tf_op jit(solution)/shard_map/ppermute | solution.py:304
  11.1 41.2 %all-to-all-start = ((bf16[8,1,2,128,256]{4,3,2,1,0:T(8,128)(2,1)}), bf16[8,1,2,128,256]{4,3,2,1,0:T(8,128)(2,1)}, u32[]{:S(2)}, u32[]{:S(2)}) async-start(bf16[8,1,2,128,256]{4,3,2,1,0:T(8,128)(2,1)} %copy.55), calls=%async_computation | async-start | bytes 2097152 | tf_op jit(solution)/shard_map/all_to_all | solution.py:415
  16.1 26.8 %copy-start.21 = (bf16[512,512]{1,0:T(8,128)(2,1)S(1)}, bf16[512,512]{1,0:T(8,128)(2,1)}, u32[]{:S(2)}) copy-start(bf16[512,512]{1,0:T(8,128)(2,1)} %param.21) | copy-start | bytes 1572868
  17.3 20.3 %collective-permute-start.1 = (f32[2,60,128]{2,1,0:T(8,128)S(1)}, f32[2,60,128]{2,1,0:T(8,128)S(1)}, u32[]{:S(2)}, u32[]{:S(2)}) collective-permute-start(f32[2,60,128]{2,1,0:T(8,128)S(1)} %pad_maximum_fusion.4), channel_id=1, source_target_pairs={{0,4},{2,6},{4,0},{6,2},{8,12},{10,14},{12,8},{14,10},{1,5},{3,7},... | collective-permute-start | bytes 184328 | tf_op jit(solution)/shard_map/ppermute | solution.py:304
  37.6 14.7 %collective-permute-start.2 = (f32[4,60,128]{2,1,0:T(8,128)S(1)}, f32[4,60,128]{2,1,0:T(8,128)S(1)}, u32[]{:S(2)}, u32[]{:S(2)}) collective-permute-start(f32[4,60,128]{2,1,0:T(8,128)S(1)} %pad_maximum_fusion.2), channel_id=1, source_target_pairs={{0,8},{2,10},{4,12},{6,14},{8,0},{10,2},{12,4},{14,6},{1,9},{3,11}... | collective-permute-start | bytes 368648 | tf_op jit(solution)/shard_map/ppermute | solution.py:304
  57.8 20.1 %all-to-all-start.2 = ((bf16[8,128,256]{2,1,0:T(8,128)(2,1)}), bf16[8,128,256]{2,1,0:T(8,128)(2,1)S(1)}, u32[]{:S(2)}, u32[]{:S(2)}) async-start(bf16[8,128,256]{2,1,0:T(8,128)(2,1)} %get-tuple-element.51), calls=%async_computation.2 | async-start | bytes 1048576 | tf_op jit(solution)/shard_map/all_to_all | solution.py:420
  62.9 21.0 %collective-permute-start.6 = (bf16[160,2048]{1,0:T(8,128)(2,1)}, bf16[160,2048]{1,0:T(8,128)(2,1)}, u32[]{:S(2)}, u32[]{:S(2)}) collective-permute-start(bf16[160,2048]{1,0:T(8,128)(2,1)} %collective-permute-done.3.refs_1_), channel_id=1, source_target_pairs={{4,8},{6,10},{8,4},{10,6},{5,9},{7,11},{9,5},{11,7},{20,24},{22,26... | collective-permute-start | bytes 1966088 | tf_op jit(solution)/shard_map/ppermute | solution.py:324
  64.4 26.8 %collective-permute-start.5 = (bf16[160,2048]{1,0:T(8,128)(2,1)}, bf16[160,2048]{1,0:T(8,128)(2,1)S(1)}, u32[]{:S(2)}, u32[]{:S(2)}) collective-permute-start(bf16[160,2048]{1,0:T(8,128)(2,1)} %collective-permute-done.4), channel_id=1, source_target_pairs={{4,0},{6,2},{8,12},{10,14},{5,1},{7,3},{9,13},{11,15},{20,16},{22,... | collective-permute-start | bytes 1966088 | tf_op jit(solution)/shard_map/ppermute | solution.py:324
  77.9 42.0 %all-to-all-start.1 = ((bf16[8,128,256]{2,1,0:T(8,128)(2,1)}), bf16[8,128,256]{2,1,0:T(8,128)(2,1)}, u32[]{:S(2)}, u32[]{:S(2)}) async-start(bf16[8,128,256]{2,1,0:T(8,128)(2,1)} %get-tuple-element.52), calls=%async_computation.1 | async-start | bytes 1048576 | tf_op jit(solution)/shard_map/all_to_all | solution.py:420
  82.3 28.7 %collective-permute-start.8 = (bf16[160,2048]{1,0:T(8,128)(2,1)}, bf16[160,2048]{1,0:T(8,128)(2,1)S(1)}, u32[]{:S(2)}, u32[]{:S(2)}) collective-permute-start(bf16[160,2048]{1,0:T(8,128)(2,1)} %collective-permute-done.3.refs_1_), channel_id=1, source_target_pairs={{0,16},{16,0},{1,17},{17,1},{2,18},{18,2},{3,19},{19,3},{4,20},{20... | collective-permute-start | bytes 1966088 | tf_op jit(solution)/shard_map/ppermute | solution.py:335
  91.2 22.4 %collective-permute-start.7 = (bf16[160,2048]{1,0:T(8,128)(2,1)}, bf16[160,2048]{1,0:T(8,128)(2,1)S(1)}, u32[]{:S(2)}, u32[]{:S(2)}) collective-permute-start(bf16[160,2048]{1,0:T(8,128)(2,1)} %collective-permute-done.6), channel_id=1, source_target_pairs={{4,0},{6,2},{8,12},{10,14},{5,1},{7,3},{9,13},{11,15},{20,16},{22,... | collective-permute-start | bytes 1966088 | tf_op jit(solution)/shard_map/ppermute | solution.py:324
  97.2 17.3 %copy-start.2 = (bf16[512,2048]{1,0:T(8,128)(2,1)S(1)}, bf16[512,2048]{1,0:T(8,128)(2,1)}, u32[]{:S(2)}) copy-start(bf16[512,2048]{1,0:T(8,128)(2,1)} %z_ref.3) | copy-start | bytes 6291460
  109.5 20.7 %collective-permute-start.9 = (bf16[160,2048]{1,0:T(8,128)(2,1)}, bf16[160,2048]{1,0:T(8,128)(2,1)}, u32[]{:S(2)}, u32[]{:S(2)}) collective-permute-start(bf16[160,2048]{1,0:T(8,128)(2,1)} %broadcast_select_fusion.1.refs_3_), channel_id=1, source_target_pairs={{0,16},{16,0},{1,17},{17,1},{2,18},{18,2},{3,19},{19,3},{4,20},{20... | collective-permute-start | bytes 1966088 | tf_op jit(solution)/shard_map/ppermute | solution.py:335
  126.4 16.5 %copy-start.4 = (bf16[320,2048]{1,0:T(8,128)(2,1)S(1)}, bf16[320,2048]{1,0:T(8,128)(2,1)}, u32[]{:S(2)}) copy-start(bf16[320,2048]{1,0:T(8,128)(2,1)} %refs_0_.1) | copy-start | bytes 3932164
  126.4 16.5 %copy-start.10 = (bf16[160,2048]{1,0:T(8,128)(2,1)S(1)}, bf16[160,2048]{1,0:T(8,128)(2,1)}, u32[]{:S(2)}) copy-start(bf16[160,2048]{1,0:T(8,128)(2,1)} %copy-done.9) | copy-start | bytes 1966084
  126.4 26.4 %collective-permute-start.13 = (bf16[512,1024]{1,0:T(8,128)(2,1)}, bf16[512,1024]{1,0:T(8,128)(2,1)}, u32[]{:S(2)}, u32[]{:S(2)}) collective-permute-start(bf16[512,1024]{1,0:T(8,128)(2,1)} %get-tuple-element.21.b_ref), channel_id=1, source_target_pairs={{0,2},{2,0},{4,6},{6,4},{8,10},{10,8},{12,14},{14,12},{1,3},{3,1},... | collective-permute-start | bytes 3145736 | tf_op jit(solution)/shard_map/ppermute | solution.py:471
  127.4 45.1 %collective-permute-start.12 = (bf16[512,1024]{1,0:T(8,128)(2,1)}, bf16[512,1024]{1,0:T(8,128)(2,1)}, u32[]{:S(2)}, u32[]{:S(2)}) collective-permute-start(bf16[512,1024]{1,0:T(8,128)(2,1)} %get-tuple-element.20.a_ref), channel_id=1, source_target_pairs={{0,2},{2,0},{4,6},{6,4},{8,10},{10,8},{12,14},{14,12},{1,3},{3,1},... | collective-permute-start | bytes 3145736 | tf_op jit(solution)/shard_map/ppermute | solution.py:469
  128.5 14.4 %collective-permute-start.10 = (bf16[160,2048]{1,0:T(8,128)(2,1)S(1)}, bf16[160,2048]{1,0:T(8,128)(2,1)S(1)}, u32[]{:S(2)}, u32[]{:S(2)}) collective-permute-start(bf16[160,2048]{1,0:T(8,128)(2,1)S(1)} %broadcast_select_fusion.refs_5_), channel_id=1, source_target_pairs={{0,16},{16,0},{1,17},{17,1},{2,18},{18,2},{3,19},{19,3},{4,20},{20... | collective-permute-start | bytes 1966088 | tf_op jit(solution)/shard_map/ppermute | solution.py:335
  177.9 6.0 %collective-permute-start.14 = (bf16[512,640]{1,0:T(8,128)(2,1)S(1)}, bf16[512,640]{1,0:T(8,128)(2,1)S(1)}, u32[]{:S(2)}, u32[]{:S(2)}) collective-permute-start(bf16[512,640]{1,0:T(8,128)(2,1)S(1)} %get-tuple-element.31), channel_id=1, source_target_pairs={{0,1},{1,0},{2,3},{3,2},{4,5},{5,4},{6,7},{7,6},{8,9},{9,8},{10,11... | collective-permute-start | bytes 1966088 | tf_op jit(solution)/shard_map/ppermute | solution.py:480
  183.3 3.6 %collective-permute-start.11 = (bf16[512,640]{1,0:T(8,128)(2,1)S(1)}, bf16[512,640]{1,0:T(8,128)(2,1)S(1)}, u32[]{:S(2)}, u32[]{:S(2)}) collective-permute-start(bf16[512,640]{1,0:T(8,128)(2,1)S(1)} %get-tuple-element.29), channel_id=1, source_target_pairs={{0,1},{1,0},{2,3},{3,2},{4,5},{5,4},{6,7},{7,6},{8,9},{9,8},{10,11... | collective-permute-start | bytes 1966088 | tf_op jit(solution)/shard_map/ppermute | solution.py:478
  184.8 16.9 %collective-permute-start.15 = (bf16[512,640]{1,0:T(8,128)(2,1)}, bf16[512,640]{1,0:T(8,128)(2,1)S(1)}, u32[]{:S(2)}, u32[]{:S(2)}) collective-permute-start(bf16[512,640]{1,0:T(8,128)(2,1)} %add_convert_fusion), channel_id=1, source_target_pairs={{0,2},{2,0},{4,6},{6,4},{8,10},{10,8},{12,14},{14,12},{1,3},{3,1},... | collective-permute-start | bytes 1966088 | tf_op jit(solution)/shard_map/ppermute | solution.py:482
  185.5 1.2 collective-permute-start.16
  (27 other events, 106.3 us)

commit v3 on v1

--- a/solution.py
+++ b/solution.py
@@ -11,6 +11,8 @@
 INNER = 4096
 LOG2E = 1.4426950408889634
 GROUP = 8
+VMEM = 40 * 2**20
+QUICK = pl.CostEstimate(flops=1, bytes_accessed=1, transcendentals=0)
 NEG = -1e30
 
 
@@ -118,10 +120,8 @@
             pltpu.VMEM((tokens + 8, lanes), jnp.float32),
             pltpu.VMEM((tokens, lanes), jnp.bfloat16),
         ],
-        compiler_params=pltpu.CompilerParams(vmem_limit_bytes=40 * 2**20),
-        cost_estimate=pl.CostEstimate(
-            flops=2 * tokens * channels * 1024, bytes_accessed=tokens * channels * 6, transcendentals=tokens * channels * 4
-        ),
+        compiler_params=pltpu.CompilerParams(vmem_limit_bytes=VMEM),
+        cost_estimate=QUICK,
         name="scan_blocks",
     )(x_in, prev, taps, cols, arow, skip, g, bt, c)
 
@@ -177,12 +177,81 @@
             jax.ShapeDtypeStruct((tokens, channels), jnp.bfloat16),
             jax.ShapeDtypeStruct((tokens, 128), jnp.float32),
         ],
-        compiler_params=pltpu.CompilerParams(vmem_limit_bytes=40 * 2**20),
-        cost_estimate=pl.CostEstimate(
-            flops=2 * tokens * channels * 256, bytes_accessed=tokens * channels * 9, transcendentals=tokens * channels * 2
-        ),
+        compiler_params=pltpu.CompilerParams(vmem_limit_bytes=VMEM),
+        cost_estimate=QUICK,
         name="gate_blocks",
     )(y, z, cols, h, c, gain)
+
+
+def project_kernel(cuts, rows_ref, mine_ref, value_ref, *refs):
+    pieces, out_ref, held, sems = refs[:-3], refs[-3], refs[-2], refs[-1]
+    copies = []
+    for i, (piece, first, size) in enumerate(cuts):
+        at = pl.multiple_of(rows_ref[i], 16)
+        copies.append(
+            pltpu.make_async_copy(
+                pieces[piece].at[pl.ds(first, size), :],
+                held.at[pl.ds(at, size), :],
+                sems.at[i],
+            )
+        )
+    for i, copy in enumerate(copies):
+        pl.when(mine_ref[i] == 1)(copy.start)
+    for i, copy in enumerate(copies):
+        pl.when(mine_ref[i] == 1)(copy.wait)
+    step = 256
+    for first in range(0, out_ref.shape[1], step):
+        cols = slice(first, min(first + step, out_ref.shape[1]))
+        out_ref[:, cols] = lax.dot_general(
+            value_ref[...], held[cols, :], (((1,), (1,)), ((), ())), preferred_element_type=jnp.float32
+        ).astype(out_ref.dtype)
+
+
+def project(value, pieces, cuts, rows, mine, total, dtype):
+    tokens, channels = value.shape
+    return pl.pallas_call(
+        functools.partial(project_kernel, cuts),
+        in_specs=[pl.BlockSpec(memory_space=pltpu.SMEM)] * 2
+        + [pl.BlockSpec(memory_space=pltpu.VMEM)]
+        + [pl.BlockSpec(memory_space=pl.ANY)] * len(pieces),
+        out_specs=pl.BlockSpec(memory_space=pltpu.VMEM),
+        out_shape=jax.ShapeDtypeStruct((tokens, total), dtype),
+        scratch_shapes=[
+            pltpu.VMEM((total, channels), pieces[0].dtype),
+            pltpu.SemaphoreType.DMA((len(cuts),)),
+        ],
+        compiler_params=pltpu.CompilerParams(vmem_limit_bytes=60 * 2**20),
+        cost_estimate=QUICK,
+        name="project_rows",
+    )(rows, mine, value, *pieces)
+
+
+def choose_kernel(rows_ref, states_ref, out_ref, sems):
+    copies = [
+        pltpu.make_async_copy(states_ref.at[rows_ref[j]], out_ref.at[j], sems.at[j])
+        for j in range(out_ref.shape[0])
+    ]
+    for copy in copies:
+        copy.start()
+    for copy in copies:
+        copy.wait()
+
+
+def choose(rows, states):
+    count = rows.shape[0]
+    return pl.pallas_call(
+        choose_kernel,
+        in_specs=[
+            pl.BlockSpec(memory_space=pltpu.SMEM),
+            pl.BlockSpec(memory_space=pl.ANY),
+        ],
+        out_specs=pl.BlockSpec(memory_space=pl.ANY),
+        out_shape=jax.ShapeDtypeStruct((count, *states.shape[1:]), states.dtype),
+        scratch_shapes=[pltpu.SemaphoreType.DMA((count,))],
+        compiler_params=pltpu.CompilerParams(vmem_limit_bytes=16 * 2**20),
+        cost_estimate=QUICK,
+        name="choose_rows",
+    )(rows, states)
 
 
 def gather_all(value, axis):
@@ -202,39 +271,73 @@
     return held
 
 
-def ring_order(n):
-    if n == 8:
-        return [0, 2, 4, 6, 7, 5, 3, 1]
-    return list(range(n))
-
-
-def ring_gather(block, axis):
-    n = lax.axis_size(axis)
+def gather_rows(block):
+    n = lax.axis_size("cache")
+    me = lax.axis_index("cache")
     rows = block.shape[0]
-    order = ring_order(n)
-    place = [order.index(i) for i in range(n)]
-    ahead = [(order[i], order[(i + 1) % n]) for i in range(n)]
-    back = [(b, a) for a, b in ahead]
-    me = jnp.asarray(place)[lax.axis_index(axis)]
-    ids = jnp.asarray(order)
-    full = jnp.zeros((n * rows, block.shape[1]), block.dtype)
-
-    def put(full, piece, offset, first=0):
-        at = ids[lax.rem(me + offset + n, n)] * rows + first
-        return lax.dynamic_update_slice(full, piece, (at, 0))
-
-    full = put(full, block, 0)
-    a = b = block
-    for k in range(1, (n - 1) // 2 + 1):
-        a = lax.ppermute(a, axis, ahead)
-        b = lax.ppermute(b, axis, back)
-        full = put(put(full, a, -k), b, k)
-    if n % 2 == 0:
-        k = n // 2
-        half = rows // 2
-        full = put(full, lax.ppermute(a[:half], axis, ahead), -k)
-        full = put(full, lax.ppermute(b[half:], axis, back), k, half)
-    return full
+    spot = me // 2
+    share = rows * 2 // 5
+    if not (n == 8 and lax.axis_size("groups") == 2 and share % 16 == 0 and rows % 16 == 0):
+        for _ in range(2):
+            yield ()
+        every = lax.all_gather(block, "cache", axis=0)
+        yield [every[i] for i in range(n)], [(i, 0, rows, i, 0) for i in range(n)]
+        return
+
+    def swap(value, pairs):
+        return lax.ppermute(
+            value, "cache", [(2 * i + p, 2 * j + p) for i, j in pairs for p in (0, 1)]
+        )
+
+    def across(value):
+        return lax.ppermute(value[:share], "groups", [(0, 1), (1, 0)])
+
+    def beside(value):
+        return lax.ppermute(value, "cache", [(i, i ^ 1) for i in range(n)])
+
+    tie = lambda *values: lax.optimization_barrier(values)
+    side = lax.axis_index("groups")
+    inner = (spot == 1) | (spot == 2)
+    own = jnp.concatenate(
+        [lax.dynamic_slice_in_dim(block, side * share, share, 0), block[2 * share :]], axis=0
+    )
+    pairs = [(0, 1), (1, 0), (2, 3), (3, 2)]
+    middle = [(1, 2), (2, 1)]
+    outward = [(1, 0), (2, 3)]
+    own_y, mate, far = beside(own), swap(own, pairs), swap(own, middle)
+    own_y, mate, far = yield own_y, mate, far
+    end, far_out, mate_y = swap(mate, middle), swap(far, outward), beside(mate)
+    own_yx, mate_x = across(own_y), across(mate)
+    end, far_out, mate_y, own_yx = tie(end, far_out, mate_y, own_yx)
+    far = jnp.where(inner, far, far_out)
+    end_out, far_y = swap(end, outward), beside(far)
+    mate_yx, far_x = across(mate_y), across(far)
+    end_out, far_y, mate_x, mate_yx, far_x = yield end_out, far_y, mate_x, mate_yx, far_x
+    end = jnp.where(inner, end, end_out)
+    end_y = beside(end)
+    end_x, far_yx = across(end), across(far_y)
+    end_yx = across(end_y)
+
+    z_far, z_end = jnp.where(spot < 2, 2, 1), jnp.where(spot < 2, 3, 0)
+    odd = me % 2
+    pieces, cuts = [block], [(0, 0, rows, me, 0)]
+    for index, plain, other in (
+        (me ^ 1, own_y, own_yx),
+        (me ^ 2, mate, mate_x),
+        (me ^ 3, mate_y, mate_yx),
+        (2 * z_far + odd, far, far_x),
+        (2 * z_far + 1 - odd, far_y, far_yx),
+        (2 * z_end + odd, end, end_x),
+        (2 * z_end + 1 - odd, end_y, end_yx),
+    ):
+        at = len(pieces)
+        pieces += [plain, other]
+        cuts += [
+            (at, 0, share, index, side * share),
+            (at, share, rows - 2 * share, index, 2 * share),
+            (at + 1, 0, share, index, (1 - side) * share),
+        ]
+    yield pieces, cuts
 
 
 def body(
@@ -269,22 +372,28 @@
     row_at = jnp.sum(position_hits * row_of[None, :], axis=1)
     row_here = row_at[lax.axis_index("cache")]
 
-    states = store_ssm.astype(jnp.bfloat16).reshape(local_slots, heads, width * n)
-    states = lax.all_to_all(states, "cache", split_axis=1, concat_axis=0, tiled=True)
-    states = jnp.take(states, row_at, axis=0)
-    start = lax.all_to_all(states, "cache", split_axis=0, concat_axis=1, tiled=True)
-    start = start.reshape(channels, n)
+    def tie(*values):
+        return lax.optimization_barrier(values)
 
     small = jnp.concatenate([stored_conv_inputs, store_convbc], axis=2)
     small = gather_all(small.reshape(-1, 128), "cache")
+    gathered = gather_rows(out_weight)
+    *step, store_ssm = tie(*next(gathered), store_ssm)
+    step = gathered.send(tuple(step))
+
+    share = channels // ncache
+    states = store_ssm.astype(jnp.bfloat16).reshape(local_slots, ncache, share, n)
+    states = states.transpose(1, 0, 2, 3)
+    states, small = tie(states, small)
+    states = lax.all_to_all(states, "cache", split_axis=0, concat_axis=0, tiled=True)
+    chosen = choose(row_at.astype(jnp.int32), states.reshape(ncache * local_slots, share, n))
+
     small = lax.dynamic_index_in_dim(
         small.reshape(ncache * local_slots, taps_prev, -1), row_here, 0, keepdims=False
     )
     prev_x = jnp.concatenate(
         [jnp.zeros((8 - taps_prev, channels), jnp.float32), small[:, :channels]], axis=0
     )
-
-    weight = ring_gather(out_weight, "cache")
 
     bcs = conv_silu(small[:, channels:], bc_in, conv_bc)
     b = bcs[:, :n]
@@ -314,25 +423,35 @@
     cols = jnp.concatenate([grouped(cum), grouped(acol)], axis=2)
     skip = jnp.repeat(d_skip, width)[None, :]
     y = scan_call(x_in, prev_x, conv_x, cols, acol.T, skip, g, b.T, c)
-    gated, squares = gate_call(y, z_in, grouped(whole), start, c, norm_gain[None, :])
-
-    swap = [(0, 1), (1, 0)]
-    half = weight.shape[0] // 2
+    whole = grouped(whole)
+    gain = norm_gain[None, :]
+    cores = [(0, 1), (1, 0)]
     core = lax.axis_index("tensor")
+    start = lax.all_to_all(chosen, "cache", split_axis=0, concat_axis=0, tiled=True)
+    start = start.reshape(channels, n)
+    *step, y = tie(*step, y)
+    pieces, cuts = gathered.send(tuple(step))
+    gated, squares = gate_call(y, z_in, whole, start, c, gain)
     squares = jnp.sum(squares, axis=1)
-    squares = squares + lax.ppermute(squares, "tensor", swap)
-
-    def project(index):
-        part = lax.dynamic_slice_in_dim(weight, index * half, half, 0)
-        return lax.dot_general(
-            gated, part, (((1,), (1,)), ((), ())), preferred_element_type=jnp.float32
-        )
-
-    other = lax.ppermute(project(1 - core).astype(jnp.bfloat16), "tensor", swap)
-    summed = project(core) + other.astype(jnp.float32)
-    mixed = summed * lax.rsqrt(squares / INNER + 1e-05)[:, None]
+    squares = squares + lax.ppermute(squares, "tensor", cores)
     valid = jnp.arange(tokens) < lengths[0]
-    return jnp.where(valid[:, None], mixed, 0.0).astype(jnp.bfloat16)
+    scale = jnp.where(valid, lax.rsqrt(squares / INNER + 1e-05), 0.0)[:, None]
+
+    half = ncache // 2
+    rows = out_weight.shape[0]
+    places = jnp.stack(
+        [lax.rem(jnp.int32(index), half) * rows + row for _, _, _, index, row in cuts]
+    )
+    owners = jnp.stack([jnp.int32(index) // half for _, _, _, index, _ in cuts])
+    cuts = tuple(cut[:3] for cut in cuts)
+
+    def products(owner, dtype):
+        mine = (owners == owner).astype(jnp.int32)
+        return project(gated, pieces, cuts, places.astype(jnp.int32), mine, half * rows, dtype)
+
+    other = lax.ppermute(products(1 - core, jnp.bfloat16), "tensor", cores)
+    summed = products(core, jnp.float32) + other.astype(jnp.float32)
+    return (summed * scale).astype(jnp.bfloat16)
 
 
 def solution(mesh):

time: 195 us -> 161 us (0.83)
  local copies, waits for them, and re-layouts: 58.8 us -> 24 us
  Pallas kernels: 15.4 us -> 33.6 us
  matrix products: 14.1 us -> 1.46 us
  between operations: 14.8 us -> 2.98 us
  starting transfers between devices: 32.8 us -> 42.6 us
  other arithmetic: 16.2 us -> 11.5 us
    dynamic_update_slice x9 -> x0, local copies, waits for them, and re-layouts: 19.3 us -> none  [put(): return lax.dynamic_update_slice(full, piece, (at, 0))]
    pallas_call x0 -> x3, Pallas kernels: none -> 18.5 us  [the longest x2 16.9 us: project(): pl.pallas_call(functools.partial(project_kernel, cuts), in_specs=[pl.Bloc...]
    dot_general x2 -> x0, matrix products: 13.6 us -> none  [project(): lax.dot_general(gated, part, (((1,), (1,)), ((), ())), preferred_element_...]
    ppermute x3, waiting for transfers between devices: 8.92 us -> 20.5 us  [gather_all(): other = lax.ppermute(held, axis, [(i, i ^ step) for i in range(n)])]
    ppermute x10 -> x18, starting transfers between devices: 14.7 us -> 25.1 us  [the longest x5 10.7 us: swap(): lax.ppermute(value, 'cache', [(2 * i + p, 2 * j + p) for i, j in pairs fo...]
    ppermute x10 -> x18, waiting for transfers between devices: 33.3 us -> 23.1 us  [the longest x4 14.3 us: beside(): return lax.ppermute(value, 'cache', [(i, i ^ 1) for i in range(n)])]
    all_to_all x2 -> x0, local copies, waits for them, and re-layouts: 9.01 us -> none  [body(): lax.all_to_all(states, 'cache', split_axis=1, concat_axis=0, tiled=True)]
    unnamed x1 -> x0, other arithmetic: 7.05 us -> none
  transfers between devices with their start and end apart: 15 -> 23, of which waited for: 7 -> 5; matrix products, arithmetic and copies ran while one was open for 35% -> 15% of each run, Pallas kernels for 8% -> 15%
where the time goes in v3:
time: 161 us; the launch traced here: 160 us
  waiting for transfers between devices  43.6 us (27%)
  starting transfers between devices  42.6 us (26%)
  Pallas kernels  33.6 us (21%)
  local copies, waits for them, and re-layouts  24 us (15%)
  other arithmetic  11.5 us (7%)
  between operations  2.98 us (2%)
    ppermute x3, waiting for transfers between devices, gather_all(): other = lax.ppermute(held, axis, [(i, i ^ step) for i in range(n)])  20.5 us
    pallas_call x2, Pallas kernels, project(): pl.pallas_call(functools.partial(project_kernel, cuts), in_specs=[pl.Bloc...  16.9 us
    ppermute x4, waiting for transfers between devices, beside(): return lax.ppermute(value, 'cache', [(i, i ^ 1) for i in range(n)])  14.3 us
    pallas_call x1, Pallas kernels, scan_call(): pl.pallas_call(scan_kernel, grid=(groups,), in_specs=[pl.BlockSpec((token...  11.3 us
    ppermute x5, starting transfers between devices, swap(): lax.ppermute(value, 'cache', [(2 * i + p, 2 * j + p) for i, j in pairs fo...  10.7 us
    all_to_all x1, starting transfers between devices, body(): lax.all_to_all(chosen, 'cache', split_axis=0, concat_axis=0, tiled=True)  10.3 us
    unnamed x52, local copies, waits for them, and re-layouts  8.77 us
    slice x7, local copies, waits for them, and re-layouts, across(): return lax.ppermute(value[:share], 'groups', [(0, 1), (1, 0)])  8.08 us
  transfers between devices with their start and end apart: 23, of which 5 were waited for; matrix products, arithmetic and copies ran while one was open for 15% of the time, Pallas kernels for 15%

profile of v3, /device:TPU:0, one launch (start us, length us, event | category | flops | bytes accessed | tf_op | source)
XLA Modules:
  0.0 159.8 jit_solution(6934924176975590288)
XLA Ops:
  1.3 1.6 %collective-permute-start.2 = (bf16[192,2048]{1,0:T(8,128)(2,1)S(1)}, bf16[192,2048]{1,0:T(8,128)(2,1)}, u32[]{:S(2)}, u32[]{:S(2)}) collective-permute-start(bf16[192,2048]{1,0:T(8,128)(2,1)S(1)} %pad_maximum_fusion.1), channel_id=1, source_target_pairs={{4,8},{6,10},{8,4},{10,6},{5,9},{7,11},{9,5},{11,7},{20,24},{22,26... | collective-permute-start | bytes 2359304 | tf_op jit(solution)/shard_map/ppermute | solution.py:288
  2.9 5.0 %collective-permute-start.1 = (bf16[192,2048]{1,0:T(8,128)(2,1)S(1)}, bf16[192,2048]{1,0:T(8,128)(2,1)S(1)}, u32[]{:S(2)}, u32[]{:S(2)}) collective-permute-start(bf16[192,2048]{1,0:T(8,128)(2,1)S(1)} %pad_maximum_fusion.1), channel_id=1, source_target_pairs={{0,4},{2,6},{4,0},{6,2},{8,12},{10,14},{12,8},{14,10},{1,5},{3,7},... | collective-permute-start | bytes 2359304 | tf_op jit(solution)/shard_map/ppermute | solution.py:288
  10.7 16.6 %collective-permute-done.12 = f32[1,60,128]{2,1,0:T(8,128)S(1)} collective-permute-done((f32[1,60,128]{2,1,0:T(8,128)S(1)}, f32[1,60,128]{2,1,0:T(8,128)S(1)}, u32[]{:S(2)}, u32[]{:S(2)}) %collective-permute-start.12) | collective-permute-done | bytes 30752 | tf_op jit(solution)/shard_map/ppermute | solution.py:265
  27.8 3.9 %collective-permute-done.13 = f32[2,60,128]{2,1,0:T(8,128)S(1)} collective-permute-done((f32[2,60,128]{2,1,0:T(8,128)S(1)}, f32[2,60,128]{2,1,0:T(8,128)S(1)}, u32[]{:S(2)}, u32[]{:S(2)}) %collective-permute-start.13) | collective-permute-done | bytes 61472 | tf_op jit(solution)/shard_map/ppermute | solution.py:265
  32.7 1.6 collective-permute-start.5
  39.5 2.2 %convert_element_type.33 = f32[512,512]{1,0:T(8,128)} convert(bf16[512,512]{1,0:T(8,128)(2,1)} %param.19) | non-fusion elementwise | flops 262144 | bytes 1572864 | tf_op jit(solution)/shard_map/convert_element_type | solution.py:25
  46.4 5.3 %all-to-all-start = ((bf16[8,1,256,256]{3,2,1,0:T(8,128)(2,1)}), bf16[8,1,256,256]{3,2,1,0:T(8,128)(2,1)S(1)}, u32[]{:S(2)}, u32[]{:S(2)}) async-start(bf16[8,1,256,256]{3,2,1,0:T(8,128)(2,1)} %bitcast.92), calls=%async_computation | async-start | bytes 2097152 | tf_op jit(solution)/shard_map/all_to_all | solution.py:388
  53.9 4.0 %collective-permute-done.6.refs_2_ = bf16[128,2048]{1,0:T(8,128)(2,1)} collective-permute-done((bf16[128,2048]{1,0:T(8,128)(2,1)}, bf16[128,2048]{1,0:T(8,128)(2,1)}, u32[]{:S(2)}, u32[]{:S(2)}) %collective-permute-start.6) | collective-permute-done | bytes 524320 | tf_op jit(solution)/shard_map/ppermute | solution.py:293
  57.9 4.7 %collective-permute-done.4 = bf16[192,2048]{1,0:T(8,128)(2,1)} collective-permute-done((bf16[192,2048]{1,0:T(8,128)(2,1)}, bf16[192,2048]{1,0:T(8,128)(2,1)}, u32[]{:S(2)}, u32[]{:S(2)}) %collective-permute-start.4) | collective-permute-done | bytes 786464 | tf_op jit(solution)/shard_map/ppermute | solution.py:288
  67.6 1.9 %slice.72 = bf16[128,2048]{1,0:T(8,128)(2,1)} slice(bf16[192,2048]{1,0:T(8,128)(2,1)} %collective-permute-done.5.refs_5_), slice={[0:128], [0:2048]} | slice | bytes 1048576 | tf_op jit(solution)/shard_map/slice | solution.py:293
  69.5 1.6 %collective-permute-start.10 = (bf16[128,2048]{1,0:T(8,128)(2,1)}, bf16[128,2048]{1,0:T(8,128)(2,1)}, u32[]{:S(2)}, u32[]{:S(2)}) collective-permute-start(bf16[128,2048]{1,0:T(8,128)(2,1)} %slice.72), channel_id=1, source_target_pairs={{0,16},{16,0},{1,17},{17,1},{2,18},{18,2},{3,19},{19,3},{4,20},{20... | collective-permute-start | bytes 1572872 | tf_op jit(solution)/shard_map/ppermute | solution.py:293
  77.0 11.3 %scan_blocks.1.y_ref = f32[512,2048]{1,0:T(8,128)S(1)} custom-call(bf16[512,2048]{1,0:T(8,128)(2,1)S(1)} %copy-done.3, f32[8,2048]{1,0:T(8,128)S(1)} %concatenate.32.prev_ref, bf16[4,2048]{1,0:T(4,128)(2,1)S(1)} %copy-done.5, f32[4,512,16]{2,1,0:T(8,128)S(1)} %copy.40.cols_ref, f32[32,512]{1,0:T(8,128)S(1)} %get-tuple-element.46.arow_ref, ...), custom_call_target="tpu_custom_call" | custom-call | flops 1 | bytes 1 | tf_op jit(solution)/shard_map/scan_blocks/pallas_call | solution.py:103
  88.3 2.0 %copy-done = f32[512,2048]{1,0:T(8,128)} copy-done((f32[512,2048]{1,0:T(8,128)}, f32[512,2048]{1,0:T(8,128)S(1)}, u32[]{:S(2)}) %copy-start) | copy-done | bytes 4194328
  91.9 10.3 %all-to-all-start.1 = ((bf16[8,256,256]{2,1,0:T(8,128)(2,1)}), bf16[8,256,256]{2,1,0:T(8,128)(2,1)S(1)}, u32[]{:S(2)}, u32[]{:S(2)}) async-start(bf16[8,256,256]{2,1,0:T(8,128)(2,1)} %choose_rows.1), calls=%async_computation.1 | async-start | bytes 2097152 | tf_op jit(solution)/shard_map/all_to_all | solution.py:430
  103.4 2.1 %collective-permute-start.17 = (bf16[192,2048]{1,0:T(8,128)(2,1)S(1)}, bf16[192,2048]{1,0:T(8,128)(2,1)S(1)}, u32[]{:S(2)}, u32[]{:S(2)}) collective-permute-start(bf16[192,2048]{1,0:T(8,128)(2,1)S(1)} %broadcast_select_fusion.refs_11_), channel_id=1, source_target_pairs={{0,2},{2,0},{4,6},{6,4},{8,10},{10,8},{12,14},{14,12},{1,3},{3,1},... | collective-permute-start | bytes 2359304 | tf_op jit(solution)/shard_map/ppermute | solution.py:296
  106.3 1.9 %slice.89 = bf16[128,2048]{1,0:T(8,128)(2,1)} slice(bf16[192,2048]{1,0:T(8,128)(2,1)} %collective-permute-done.8.refs_9_), slice={[0:128], [0:2048]} | slice | bytes 1048576 | tf_op jit(solution)/shard_map/slice | solution.py:293
  110.3 14.3 %collective-permute-done.17.refs_13_ = bf16[192,2048]{1,0:T(8,128)(2,1)S(1)} collective-permute-done((bf16[192,2048]{1,0:T(8,128)(2,1)S(1)}, bf16[192,2048]{1,0:T(8,128)(2,1)S(1)}, u32[]{:S(2)}, u32[]{:S(2)}) %collective-permute-start.17) | collective-permute-done | bytes 786464 | tf_op jit(solution)/shard_map/ppermute | solution.py:296
  125.5 1.7 %collective-permute-start.18 = (bf16[128,2048]{1,0:T(8,128)(2,1)}, bf16[128,2048]{1,0:T(8,128)(2,1)}, u32[]{:S(2)}, u32[]{:S(2)}) collective-permute-start(bf16[128,2048]{1,0:T(8,128)(2,1)} %slice.103), channel_id=1, source_target_pairs={{0,16},{16,0},{1,17},{17,1},{2,18},{18,2},{3,19},{19,3},{4,20},{20... | collective-permute-start | bytes 1572872 | tf_op jit(solution)/shard_map/ppermute | solution.py:293
  129.3 2.2 %copy-done.1 = f32[512,2048]{1,0:T(8,128)S(1)} copy-done((f32[512,2048]{1,0:T(8,128)S(1)}, f32[512,2048]{1,0:T(8,128)}, u32[]{:S(2)}) %copy-start.1) | copy-done | bytes 4194328
  131.4 1.6 copy-done.4
  133.0 3.8 %gate_blocks.1 = (bf16[512,2048]{1,0:T(8,128)(2,1)S(1)}, f32[512,128]{1,0:T(8,128)S(1)}) custom-call(f32[512,2048]{1,0:T(8,128)S(1)} %copy-done.1, bf16[512,2048]{1,0:T(8,128)(2,1)S(1)} %copy-done.4, f32[4,512,8]{2,1,0:T(8,128)S(1)} %bitcast.88, bf16[2048,256]{1,0:T(8,128)(2,1)S(1)} %bitcast.87, bf16[512,256]{1,0:T(8,128)(2,1)S(1)} %get-tuple-element.43.c_ref, ...), custom_call_target="tpu_custom_call" | custom-call | flops 1 | bytes 1 | tf_op jit(solution)/shard_map/gate_blocks/pallas_call | solution.py:161
  138.2 8.3 %project_rows.3 = bf16[512,1280]{1,0:T(8,128)(2,1)} custom-call(s32[22]{0:T(128)} %stack.132.rows_ref, s32[22]{0:T(128)} %get-tuple-element.56.mine_ref, bf16[512,2048]{1,0:T(8,128)(2,1)} %copy-done.2, bf16[320,2048]{1,0:T(8,128)(2,1)} %refs_0_.3, bf16[192,2048]{1,0:T(8,128)(2,1)} %copy-done.10, bf16[128,2048]{1,0:T(8,128)(2,1)} %collective-permute-done.6.refs_2_, ...), custom_call_target="tpu_custom_call" | custom-call | flops 1 | bytes 1 | tf_op jit(solution)/shard_map/project_rows/pallas_call | solution.py:212
  147.9 8.7 %project_rows.2 = f32[512,1280]{1,0:T(8,128)} custom-call(s32[22]{0:T(128)} %stack.132.rows_ref, s32[22]{0:T(128)} %get-tuple-element.57.mine_ref, bf16[512,2048]{1,0:T(8,128)(2,1)} %copy-done.2, bf16[320,2048]{1,0:T(8,128)(2,1)} %refs_0_.3, bf16[192,2048]{1,0:T(8,128)(2,1)} %copy-done.10, bf16[128,2048]{1,0:T(8,128)(2,1)} %collective-permute-done.6.refs_2_, ...), custom_call_target="tpu_custom_call" | custom-call | flops 1 | bytes 1 | tf_op jit(solution)/shard_map/project_rows/pallas_call | solution.py:212
  156.6 3.1 %multiply_convert_fusion = bf16[512,1280]{1,0:T(8,128)(2,1)} fusion(f32[512,1280]{1,0:T(8,128)} %project_rows.2, bf16[512,1280]{1,0:T(8,128)(2,1)S(1)} %collective-permute-done.19, f32[512]{0:T(512)S(1)} %rsqrt_select_fusion), kind=kLoop, calls=%fused_computation | loop fusion | flops 2621440 | bytes 5244928 | tf_op jit(solution)/shard_map/convert_element_type | solution.py:454
  (139 shorter events, 37.2 us)
Async XLA Ops:
  1.2 37.8 %copy-start.22 = (f32[32]{0:T(128)S(1)}, f32[32]{0:T(128)}, u32[]{:S(2)}) copy-start(f32[32]{0:T(128)} %param.25) | copy-start | bytes 388
  1.3 31.4 %collective-permute-start.2 = (bf16[192,2048]{1,0:T(8,128)(2,1)S(1)}, bf16[192,2048]{1,0:T(8,128)(2,1)}, u32[]{:S(2)}, u32[]{:S(2)}) collective-permute-start(bf16[192,2048]{1,0:T(8,128)(2,1)S(1)} %pad_maximum_fusion.1), channel_id=1, source_target_pairs={{4,8},{6,10},{8,4},{10,6},{5,9},{7,11},{9,5},{11,7},{20,24},{22,26... | collective-permute-start | bytes 2359304 | tf_op jit(solution)/shard_map/ppermute | solution.py:288
  2.9 29.8 %collective-permute-start.1 = (bf16[192,2048]{1,0:T(8,128)(2,1)S(1)}, bf16[192,2048]{1,0:T(8,128)(2,1)S(1)}, u32[]{:S(2)}, u32[]{:S(2)}) collective-permute-start(bf16[192,2048]{1,0:T(8,128)(2,1)S(1)} %pad_maximum_fusion.1), channel_id=1, source_target_pairs={{0,4},{2,6},{4,0},{6,2},{8,12},{10,14},{12,8},{14,10},{1,5},{3,7},... | collective-permute-start | bytes 2359304 | tf_op jit(solution)/shard_map/ppermute | solution.py:288
  7.9 24.8 %collective-permute-start = (bf16[192,2048]{1,0:T(8,128)(2,1)S(1)}, bf16[192,2048]{1,0:T(8,128)(2,1)S(1)}, u32[]{:S(2)}, u32[]{:S(2)}) collective-permute-start(bf16[192,2048]{1,0:T(8,128)(2,1)S(1)} %pad_maximum_fusion.1), channel_id=1, source_target_pairs={{0,2},{2,0},{4,6},{6,4},{8,10},{10,8},{12,14},{14,12},{1,3},{3,1},... | collective-permute-start | bytes 2359304 | tf_op jit(solution)/shard_map/ppermute | solution.py:296
  9.5 17.8 %collective-permute-start.12 = (f32[1,60,128]{2,1,0:T(8,128)S(1)}, f32[1,60,128]{2,1,0:T(8,128)S(1)}, u32[]{:S(2)}, u32[]{:S(2)}) collective-permute-start(f32[1,60,128]{2,1,0:T(8,128)S(1)} %broadcast_in_dim_reshape.6), channel_id=1, source_target_pairs={{0,2},{2,0},{4,6},{6,4},{8,10},{10,8},{12,14},{14,12},{1,3},{3,1},... | collective-permute-start | bytes 92168 | tf_op jit(solution)/shard_map/ppermute | solution.py:265
  27.3 4.3 %collective-permute-start.13 = (f32[2,60,128]{2,1,0:T(8,128)S(1)}, f32[2,60,128]{2,1,0:T(8,128)S(1)}, u32[]{:S(2)}, u32[]{:S(2)}) collective-permute-start(f32[2,60,128]{2,1,0:T(8,128)S(1)} %pad_maximum_fusion.5), channel_id=1, source_target_pairs={{0,4},{2,6},{4,0},{6,2},{8,12},{10,14},{12,8},{14,10},{1,5},{3,7},... | collective-permute-start | bytes 184328 | tf_op jit(solution)/shard_map/ppermute | solution.py:265
  31.7 13.5 %collective-permute-start.14 = (f32[4,60,128]{2,1,0:T(8,128)S(1)}, f32[4,60,128]{2,1,0:T(8,128)S(1)}, u32[]{:S(2)}, u32[]{:S(2)}) collective-permute-start(f32[4,60,128]{2,1,0:T(8,128)S(1)} %pad_maximum_fusion.3), channel_id=1, source_target_pairs={{0,8},{2,10},{4,12},{6,14},{8,0},{10,2},{12,4},{14,6},{1,9},{3,11}... | collective-permute-start | bytes 368648 | tf_op jit(solution)/shard_map/ppermute | solution.py:265
  32.7 29.9 %collective-permute-start.5 = (bf16[192,2048]{1,0:T(8,128)(2,1)S(1)}, bf16[192,2048]{1,0:T(8,128)(2,1)}, u32[]{:S(2)}, u32[]{:S(2)}) collective-permute-start(bf16[192,2048]{1,0:T(8,128)(2,1)S(1)} %collective-permute-done.1.refs_3_), channel_id=1, source_target_pairs={{0,2},{2,0},{4,6},{6,4},{8,10},{10,8},{12,14},{14,12},{1,3},{3,1},... | collective-permute-start | bytes 2359304 | tf_op jit(solution)/shard_map/ppermute | solution.py:296
  34.3 28.4 %collective-permute-start.3 = (bf16[192,2048]{1,0:T(8,128)(2,1)S(1)}, bf16[192,2048]{1,0:T(8,128)(2,1)}, u32[]{:S(2)}, u32[]{:S(2)}) collective-permute-start(bf16[192,2048]{1,0:T(8,128)(2,1)S(1)} %collective-permute-done.1.refs_3_), channel_id=1, source_target_pairs={{4,8},{6,10},{8,4},{10,6},{5,9},{7,11},{9,5},{11,7},{20,24},{22,26... | collective-permute-start | bytes 2359304 | tf_op jit(solution)/shard_map/ppermute | solution.py:288
  35.8 26.8 %collective-permute-start.4 = (bf16[192,2048]{1,0:T(8,128)(2,1)}, bf16[192,2048]{1,0:T(8,128)(2,1)}, u32[]{:S(2)}, u32[]{:S(2)}) collective-permute-start(bf16[192,2048]{1,0:T(8,128)(2,1)} %collective-permute-done.2), channel_id=1, source_target_pairs={{4,0},{6,2},{8,12},{10,14},{5,1},{7,3},{9,13},{11,15},{20,16},{22,... | collective-permute-start | bytes 2359304 | tf_op jit(solution)/shard_map/ppermute | solution.py:288
  43.7 14.3 %collective-permute-start.6 = (bf16[128,2048]{1,0:T(8,128)(2,1)}, bf16[128,2048]{1,0:T(8,128)(2,1)}, u32[]{:S(2)}, u32[]{:S(2)}) collective-permute-start(bf16[128,2048]{1,0:T(8,128)(2,1)} %slice.70), channel_id=1, source_target_pairs={{0,16},{16,0},{1,17},{17,1},{2,18},{18,2},{3,19},{19,3},{4,20},{20... | collective-permute-start | bytes 1572872 | tf_op jit(solution)/shard_map/ppermute | solution.py:293
  46.4 43.9 %all-to-all-start = ((bf16[8,1,256,256]{3,2,1,0:T(8,128)(2,1)}), bf16[8,1,256,256]{3,2,1,0:T(8,128)(2,1)S(1)}, u32[]{:S(2)}, u32[]{:S(2)}) async-start(bf16[8,1,256,256]{3,2,1,0:T(8,128)(2,1)} %bitcast.92), calls=%async_computation | async-start | bytes 2097152 | tf_op jit(solution)/shard_map/all_to_all | solution.py:388
  52.5 37.8 %collective-permute-start.9 = (bf16[128,2048]{1,0:T(8,128)(2,1)}, bf16[128,2048]{1,0:T(8,128)(2,1)}, u32[]{:S(2)}, u32[]{:S(2)}) collective-permute-start(bf16[128,2048]{1,0:T(8,128)(2,1)} %slice.71), channel_id=1, source_target_pairs={{0,16},{16,0},{1,17},{17,1},{2,18},{18,2},{3,19},{19,3},{4,20},{20... | collective-permute-start | bytes 1572872 | tf_op jit(solution)/shard_map/ppermute | solution.py:293
  63.9 26.4 %collective-permute-start.8 = (bf16[192,2048]{1,0:T(8,128)(2,1)S(1)}, bf16[192,2048]{1,0:T(8,128)(2,1)}, u32[]{:S(2)}, u32[]{:S(2)}) collective-permute-start(bf16[192,2048]{1,0:T(8,128)(2,1)S(1)} %broadcast_select_fusion.1.refs_7_), channel_id=1, source_target_pairs={{0,2},{2,0},{4,6},{6,4},{8,10},{10,8},{12,14},{14,12},{1,3},{3,1},... | collective-permute-start | bytes 2359304 | tf_op jit(solution)/shard_map/ppermute | solution.py:296
  64.7 25.6 %collective-permute-start.7 = (bf16[192,2048]{1,0:T(8,128)(2,1)}, bf16[192,2048]{1,0:T(8,128)(2,1)}, u32[]{:S(2)}, u32[]{:S(2)}) collective-permute-start(bf16[192,2048]{1,0:T(8,128)(2,1)} %collective-permute-done.3), channel_id=1, source_target_pairs={{4,0},{6,2},{8,12},{10,14},{5,1},{7,3},{9,13},{11,15},{20,16},{22,... | collective-permute-start | bytes 2359304 | tf_op jit(solution)/shard_map/ppermute | solution.py:288
  69.5 20.7 %collective-permute-start.10 = (bf16[128,2048]{1,0:T(8,128)(2,1)}, bf16[128,2048]{1,0:T(8,128)(2,1)}, u32[]{:S(2)}, u32[]{:S(2)}) collective-permute-start(bf16[128,2048]{1,0:T(8,128)(2,1)} %slice.72), channel_id=1, source_target_pairs={{0,16},{16,0},{1,17},{17,1},{2,18},{18,2},{3,19},{19,3},{4,20},{20... | collective-permute-start | bytes 1572872 | tf_op jit(solution)/shard_map/ppermute | solution.py:293
  71.1 19.1 %collective-permute-start.11 = (bf16[128,2048]{1,0:T(8,128)(2,1)}, bf16[128,2048]{1,0:T(8,128)(2,1)}, u32[]{:S(2)}, u32[]{:S(2)}) collective-permute-start(bf16[128,2048]{1,0:T(8,128)(2,1)} %slice.92), channel_id=1, source_target_pairs={{0,16},{16,0},{1,17},{17,1},{2,18},{18,2},{3,19},{19,3},{4,20},{20... | collective-permute-start | bytes 1572872 | tf_op jit(solution)/shard_map/ppermute | solution.py:293
  91.9 37.4 %all-to-all-start.1 = ((bf16[8,256,256]{2,1,0:T(8,128)(2,1)}), bf16[8,256,256]{2,1,0:T(8,128)(2,1)S(1)}, u32[]{:S(2)}, u32[]{:S(2)}) async-start(bf16[8,256,256]{2,1,0:T(8,128)(2,1)} %choose_rows.1), calls=%async_computation.1 | async-start | bytes 2097152 | tf_op jit(solution)/shard_map/all_to_all | solution.py:430
  103.4 21.2 %collective-permute-start.17 = (bf16[192,2048]{1,0:T(8,128)(2,1)S(1)}, bf16[192,2048]{1,0:T(8,128)(2,1)S(1)}, u32[]{:S(2)}, u32[]{:S(2)}) collective-permute-start(bf16[192,2048]{1,0:T(8,128)(2,1)S(1)} %broadcast_select_fusion.refs_11_), channel_id=1, source_target_pairs={{0,2},{2,0},{4,6},{6,4},{8,10},{10,8},{12,14},{14,12},{1,3},{3,1},... | collective-permute-start | bytes 2359304 | tf_op jit(solution)/shard_map/ppermute | solution.py:296
  108.2 30.0 %collective-permute-start.15 = (bf16[128,2048]{1,0:T(8,128)(2,1)}, bf16[128,2048]{1,0:T(8,128)(2,1)}, u32[]{:S(2)}, u32[]{:S(2)}) collective-permute-start(bf16[128,2048]{1,0:T(8,128)(2,1)} %slice.89), channel_id=1, source_target_pairs={{0,16},{16,0},{1,17},{17,1},{2,18},{18,2},{3,19},{19,3},{4,20},{20... | collective-permute-start | bytes 1572872 | tf_op jit(solution)/shard_map/ppermute | solution.py:293
  109.7 28.5 %collective-permute-start.16 = (bf16[128,2048]{1,0:T(8,128)(2,1)}, bf16[128,2048]{1,0:T(8,128)(2,1)}, u32[]{:S(2)}, u32[]{:S(2)}) collective-permute-start(bf16[128,2048]{1,0:T(8,128)(2,1)} %slice.102), channel_id=1, source_target_pairs={{0,16},{16,0},{1,17},{17,1},{2,18},{18,2},{3,19},{19,3},{4,20},{20... | collective-permute-start | bytes 1572872 | tf_op jit(solution)/shard_map/ppermute | solution.py:293
  125.5 12.8 %collective-permute-start.18 = (bf16[128,2048]{1,0:T(8,128)(2,1)}, bf16[128,2048]{1,0:T(8,128)(2,1)}, u32[]{:S(2)}, u32[]{:S(2)}) collective-permute-start(bf16[128,2048]{1,0:T(8,128)(2,1)} %slice.103), channel_id=1, source_target_pairs={{0,16},{16,0},{1,17},{17,1},{2,18},{18,2},{3,19},{19,3},{4,20},{20... | collective-permute-start | bytes 1572872 | tf_op jit(solution)/shard_map/ppermute | solution.py:293
  146.5 10.2 %collective-permute-start.19 = (bf16[512,1280]{1,0:T(8,128)(2,1)}, bf16[512,1280]{1,0:T(8,128)(2,1)S(1)}, u32[]{:S(2)}, u32[]{:S(2)}) collective-permute-start(bf16[512,1280]{1,0:T(8,128)(2,1)} %project_rows.3), channel_id=1, source_target_pairs={{0,1},{1,0},{2,3},{3,2},{4,5},{5,4},{6,7},{7,6},{8,9},{9,8},{10,11... | collective-permute-start | bytes 3932168 | tf_op jit(solution)/shard_map/ppermute | solution.py:452
  146.7 9.9 %collective-permute-start.20 = (f32[512]{0:T(512)S(1)}, f32[512]{0:T(512)S(1)}, u32[]{:S(2)}, u32[]{:S(2)}) collective-permute-start(f32[512]{0:T(512)S(1)} %reduce_sum.19), channel_id=1, source_target_pairs={{0,1},{1,0},{2,3},{3,2},{4,5},{5,4},{6,7},{7,6},{8,9},{9,8},{10,11... | collective-permute-start | bytes 6152 | tf_op jit(solution)/shard_map/ppermute | solution.py:436
  (27 other events, 269.3 us)

commit v4 on v3

--- a/solution.py
+++ b/solution.py
@@ -254,21 +254,11 @@
     )(rows, states)
 
 
-def gather_all(value, axis):
+def gather_step(held, axis, step):
     n = lax.axis_size(axis)
-    if n & (n - 1):
-        return lax.all_gather(value, axis, axis=0)
-    me = lax.axis_index(axis)
-    held = value[None]
-    step = 1
-    while step < n:
-        other = lax.ppermute(held, axis, [(i, i ^ step) for i in range(n)])
-        low = (me & step) == 0
-        held = jnp.concatenate(
-            [jnp.where(low, held, other), jnp.where(low, other, held)], axis=0
-        )
-        step *= 2
-    return held
+    low = (lax.axis_index(axis) & step) == 0
+    other = lax.ppermute(held, axis, [(i, i ^ step) for i in range(n)])
+    return jnp.concatenate([jnp.where(low, held, other), jnp.where(low, other, held)], axis=0)
 
 
 def gather_rows(block):
@@ -315,8 +305,10 @@
     end_out, far_y, mate_x, mate_yx, far_x = yield end_out, far_y, mate_x, mate_yx, far_x
     end = jnp.where(inner, end, end_out)
     end_y = beside(end)
-    end_x, far_yx = across(end), across(far_y)
-    end_yx = across(end_y)
+    end_x = across(end)
+    end_yx = beside(end_x)
+    far_y, end_x = tie(far_y, end_x)
+    far_yx = across(far_y)
 
     z_far, z_end = jnp.where(spot < 2, 2, 1), jnp.where(spot < 2, 3, 0)
     odd = me % 2
@@ -376,9 +368,15 @@
         return lax.optimization_barrier(values)
 
     small = jnp.concatenate([stored_conv_inputs, store_convbc], axis=2)
-    small = gather_all(small.reshape(-1, 128), "cache")
+    small = gather_step(small.reshape(1, -1, 128), "cache", 1)
+    small, out_weight = tie(small, out_weight)
+    size = 2
+    while 2 * size < ncache:
+        small = gather_step(small, "cache", size)
+        size *= 2
     gathered = gather_rows(out_weight)
-    *step, store_ssm = tie(*next(gathered), store_ssm)
+    *step, store_ssm, small = tie(*next(gathered), store_ssm, small)
+    small = gather_step(small, "cache", size)
     step = gathered.send(tuple(step))
 
     share = channels // ncache

time: 161 us -> 156 us (0.969)
  waiting for transfers between devices: 43.6 us -> 33.7 us
  other arithmetic: 11.5 us -> 16.3 us
    ppermute x4 -> x5, waiting for transfers between devices: 14.3 us -> 1.6 us  [beside(): return lax.ppermute(value, 'cache', [(i, i ^ 1) for i in range(n)])]
    ppermute x5, waiting for transfers between devices: 4.72 us -> 11.1 us  [swap(): lax.ppermute(value, 'cache', [(2 * i + p, 2 * j + p) for i, j in pairs fo...]
    ppermute x3, waiting for transfers between devices: 20.5 us -> 14.5 us  [gather_step(): other = lax.ppermute(held, axis, [(i, i ^ step) for i in range(n)])]
    all_to_all x1, starting transfers between devices: 10.3 us -> 6.51 us  [body(): lax.all_to_all(chosen, 'cache', split_axis=0, concat_axis=0, tiled=True)]
    ppermute x4 -> x5, starting transfers between devices: 5.97 us -> 8.92 us  [beside(): return lax.ppermute(value, 'cache', [(i, i ^ 1) for i in range(n)])]
    ppermute x3, starting transfers between devices: 1.98 us -> 4.87 us  [gather_step(): other = lax.ppermute(held, axis, [(i, i ^ step) for i in range(n)])]
    ppermute x7 -> x6, waiting for transfers between devices: 4.06 us -> 6.48 us  [across(): return lax.ppermute(value[:share], 'groups', [(0, 1), (1, 0)])]
    convert_element_type x1, other arithmetic: 1.14 us -> 2.75 us  [body(): store_ssm.astype(jnp.bfloat16).reshape(local_slots, ncache, share, n)]
  transfers between devices with their start and end apart: 23 -> 23, of which waited for: 5 -> 5; matrix products, arithmetic and copies ran while one was open for 15% -> 17% of each run, Pallas kernels for 15% -> 16%
where the time goes in v4:
time: 156 us; the launch traced here: 154 us
  starting transfers between devices  43.6 us (28%)
  waiting for transfers between devices  33.7 us (22%)
  Pallas kernels  33.6 us (22%)
  local copies, waits for them, and re-layouts  22.7 us (15%)
  other arithmetic  16.3 us (10%)
  between operations  3.04 us (2%)
    pallas_call x2, Pallas kernels, project(): pl.pallas_call(functools.partial(project_kernel, cuts), in_specs=[pl.Bloc...  16.9 us
    ppermute x3, waiting for transfers between devices, gather_step(): other = lax.ppermute(held, axis, [(i, i ^ step) for i in range(n)])  14.5 us
    pallas_call x1, Pallas kernels, scan_call(): pl.pallas_call(scan_kernel, grid=(groups,), in_specs=[pl.BlockSpec((token...  11.3 us
    ppermute x5, waiting for transfers between devices, swap(): lax.ppermute(value, 'cache', [(2 * i + p, 2 * j + p) for i, j in pairs fo...  11.1 us
    ppermute x5, starting transfers between devices, swap(): lax.ppermute(value, 'cache', [(2 * i + p, 2 * j + p) for i, j in pairs fo...  9.74 us
    unnamed x50, local copies, waits for them, and re-layouts  9.57 us
    ppermute x5, starting transfers between devices, beside(): return lax.ppermute(value, 'cache', [(i, i ^ 1) for i in range(n)])  8.92 us
    slice x6, local copies, waits for them, and re-layouts, across(): return lax.ppermute(value[:share], 'groups', [(0, 1), (1, 0)])  7.49 us
  transfers between devices with their start and end apart: 23, of which 5 were waited for; matrix products, arithmetic and copies ran while one was open for 17% of the time, Pallas kernels for 16%

profile of v4, /device:TPU:0, one launch (start us, length us, event | category | flops | bytes accessed | tf_op | source)
XLA Modules:
  0.0 154.4 jit_solution(14572320011278989000)
XLA Ops:
  0.9 3.0 %collective-permute-start = (f32[1,60,128]{2,1,0:T(8,128)S(1)}, f32[1,60,128]{2,1,0:T(8,128)S(1)}, u32[]{:S(2)}, u32[]{:S(2)}) collective-permute-start(f32[1,60,128]{2,1,0:T(8,128)S(1)} %reshape.57), channel_id=1, source_target_pairs={{0,2},{2,0},{4,6},{6,4},{8,10},{10,8},{12,14},{14,12},{1,3},{3,1},... | collective-permute-start | bytes 92168 | tf_op jit(solution)/shard_map/ppermute | solution.py:260
  8.8 4.0 %collective-permute-start.2 = (bf16[192,2048]{1,0:T(8,128)(2,1)S(1)}, bf16[192,2048]{1,0:T(8,128)(2,1)S(1)}, u32[]{:S(2)}, u32[]{:S(2)}) collective-permute-start(bf16[192,2048]{1,0:T(8,128)(2,1)S(1)} %pad_maximum_fusion.1), channel_id=1, source_target_pairs={{0,4},{2,6},{4,0},{6,2},{8,12},{10,14},{12,8},{14,10},{1,5},{3,7},... | collective-permute-start | bytes 2359304 | tf_op jit(solution)/shard_map/ppermute | solution.py:278
  16.9 13.4 %collective-permute-done.4 = f32[2,60,128]{2,1,0:T(8,128)S(1)} collective-permute-done((f32[2,60,128]{2,1,0:T(8,128)S(1)}, f32[2,60,128]{2,1,0:T(8,128)S(1)}, u32[]{:S(2)}, u32[]{:S(2)}) %collective-permute-start.4) | collective-permute-done | bytes 61472 | tf_op jit(solution)/shard_map/ppermute | solution.py:260
  30.4 1.7 %collective-permute-start.14 = (f32[4,60,128]{2,1,0:T(8,128)S(1)}, f32[4,60,128]{2,1,0:T(8,128)S(1)}, u32[]{:S(2)}, u32[]{:S(2)}) collective-permute-start(f32[4,60,128]{2,1,0:T(8,128)S(1)} %pad_maximum_fusion.3), channel_id=1, source_target_pairs={{0,8},{2,10},{4,12},{6,14},{8,0},{10,2},{12,4},{14,6},{1,9},{3,11}... | collective-permute-start | bytes 368648 | tf_op jit(solution)/shard_map/ppermute | solution.py:260
  38.9 2.8 %convert_element_type.32 = bf16[1,32,64,256]{3,2,1,0:T(8,128)(2,1)} convert(f32[1,32,64,256]{3,2,1,0:T(8,128)} %param.28) | non-fusion elementwise | flops 524288 | bytes 3145728 | tf_op jit(solution)/shard_map/convert_element_type | solution.py:383
  41.8 5.8 %all-to-all-start = ((bf16[8,1,256,256]{3,2,1,0:T(8,128)(2,1)}), bf16[8,1,256,256]{3,2,1,0:T(8,128)(2,1)S(1)}, u32[]{:S(2)}, u32[]{:S(2)}) async-start(bf16[8,1,256,256]{3,2,1,0:T(8,128)(2,1)} %bitcast.30), calls=%async_computation | async-start | bytes 2097152 | tf_op jit(solution)/shard_map/all_to_all | solution.py:386
  48.0 2.2 %convert_element_type.33 = f32[512,512]{1,0:T(8,128)} convert(bf16[512,512]{1,0:T(8,128)(2,1)} %param.19) | non-fusion elementwise | flops 262144 | bytes 1572864 | tf_op jit(solution)/shard_map/convert_element_type | solution.py:25
  53.4 11.1 %collective-permute-done.6 = bf16[192,2048]{1,0:T(8,128)(2,1)} collective-permute-done((bf16[192,2048]{1,0:T(8,128)(2,1)}, bf16[192,2048]{1,0:T(8,128)(2,1)}, u32[]{:S(2)}, u32[]{:S(2)}) %collective-permute-start.6) | collective-permute-done | bytes 786464 | tf_op jit(solution)/shard_map/ppermute | solution.py:278
  64.5 2.2 %broadcast_select_fusion.1.refs_7_ = bf16[192,2048]{1,0:T(8,128)(2,1)} fusion(bf16[192,2048]{1,0:T(8,128)(2,1)} %collective-permute-done.3, bf16[192,2048]{1,0:T(8,128)(2,1)} %collective-permute-done.6, pred[]{:T(512)S(6)} %or.3), kind=kLoop, calls=%fused_computation.16 | loop fusion | flops 393216 | bytes 2359297 | tf_op jit(solution)/shard_map/jit(_where)/select_n | solution.py:302
  69.5 1.9 %slice.88 = bf16[128,2048]{1,0:T(8,128)(2,1)} slice(bf16[192,2048]{1,0:T(8,128)(2,1)} %broadcast_select_fusion.1.refs_7_), slice={[0:128], [0:2048]} | slice | bytes 1048576 | tf_op jit(solution)/shard_map/slice | solution.py:283
  71.4 1.9 %slice.69 = bf16[128,2048]{1,0:T(8,128)(2,1)} slice(bf16[192,2048]{1,0:T(8,128)(2,1)} %collective-permute-done.7.refs_5_), slice={[0:128], [0:2048]} | slice | bytes 1048576 | tf_op jit(solution)/shard_map/slice | solution.py:283
  73.7 1.7 %collective-permute-start.13 = (bf16[128,2048]{1,0:T(8,128)(2,1)}, bf16[128,2048]{1,0:T(8,128)(2,1)}, u32[]{:S(2)}, u32[]{:S(2)}) collective-permute-start(bf16[128,2048]{1,0:T(8,128)(2,1)} %slice.88), channel_id=1, source_target_pairs={{0,16},{16,0},{1,17},{17,1},{2,18},{18,2},{3,19},{19,3},{4,20},{20... | collective-permute-start | bytes 1572872 | tf_op jit(solution)/shard_map/ppermute | solution.py:283
  79.6 6.5 %all-to-all-start.1 = ((bf16[8,256,256]{2,1,0:T(8,128)(2,1)}), bf16[8,256,256]{2,1,0:T(8,128)(2,1)S(1)}, u32[]{:S(2)}, u32[]{:S(2)}) async-start(bf16[8,256,256]{2,1,0:T(8,128)(2,1)} %choose_rows.1), calls=%async_computation.1 | async-start | bytes 2097152 | tf_op jit(solution)/shard_map/all_to_all | solution.py:428
  88.9 11.3 %scan_blocks.1.y_ref = f32[512,2048]{1,0:T(8,128)S(1)} custom-call(bf16[512,2048]{1,0:T(8,128)(2,1)S(1)} %copy-done.3, f32[8,2048]{1,0:T(8,128)S(1)} %concatenate.32.prev_ref, bf16[4,2048]{1,0:T(4,128)(2,1)S(1)} %copy-done.5, f32[4,512,16]{2,1,0:T(8,128)S(1)} %copy.40.cols_ref, f32[32,512]{1,0:T(8,128)S(1)} %get-tuple-element.56.arow_ref, ...), custom_call_target="tpu_custom_call" | custom-call | flops 1 | bytes 1 | tf_op jit(solution)/shard_map/scan_blocks/pallas_call | solution.py:103
  100.2 2.0 %copy-done = f32[512,2048]{1,0:T(8,128)} copy-done((f32[512,2048]{1,0:T(8,128)}, f32[512,2048]{1,0:T(8,128)S(1)}, u32[]{:S(2)}) %copy-start) | copy-done | bytes 4194328
  105.9 2.0 %collective-permute-start.17 = (bf16[192,2048]{1,0:T(8,128)(2,1)S(1)}, bf16[192,2048]{1,0:T(8,128)(2,1)}, u32[]{:S(2)}, u32[]{:S(2)}) collective-permute-start(bf16[192,2048]{1,0:T(8,128)(2,1)S(1)} %broadcast_select_fusion.refs_11_), channel_id=1, source_target_pairs={{0,2},{2,0},{4,6},{6,4},{8,10},{10,8},{12,14},{14,12},{1,3},{3,1},... | collective-permute-start | bytes 2359304 | tf_op jit(solution)/shard_map/ppermute | solution.py:286
  107.9 6.5 %collective-permute-done.15.refs_12_ = bf16[128,2048]{1,0:T(8,128)(2,1)} collective-permute-done((bf16[128,2048]{1,0:T(8,128)(2,1)S(1)}, bf16[128,2048]{1,0:T(8,128)(2,1)}, u32[]{:S(2)}, u32[]{:S(2)}) %collective-permute-start.15) | collective-permute-done | bytes 524320 | tf_op jit(solution)/shard_map/ppermute | solution.py:283
  114.4 1.9 %slice.87 = bf16[128,2048]{1,0:T(8,128)(2,1)} slice(bf16[192,2048]{1,0:T(8,128)(2,1)} %collective-permute-done.10.refs_9_), slice={[0:128], [0:2048]} | slice | bytes 1048576 | tf_op jit(solution)/shard_map/slice | solution.py:283
  117.8 2.3 %collective-permute-start.18 = (bf16[128,2048]{1,0:T(8,128)(2,1)}, bf16[128,2048]{1,0:T(8,128)(2,1)}, u32[]{:S(2)}, u32[]{:S(2)}) collective-permute-start(bf16[128,2048]{1,0:T(8,128)(2,1)} %collective-permute-done.15.refs_12_), channel_id=1, source_target_pairs={{0,2},{2,0},{4,6},{6,4},{8,10},{10,8},{12,14},{14,12},{1,3},{3,1},... | collective-permute-start | bytes 1572872 | tf_op jit(solution)/shard_map/ppermute | solution.py:286
  122.3 2.2 %copy-done.1 = f32[512,2048]{1,0:T(8,128)S(1)} copy-done((f32[512,2048]{1,0:T(8,128)S(1)}, f32[512,2048]{1,0:T(8,128)}, u32[]{:S(2)}) %copy-start.1) | copy-done | bytes 4194328
  126.1 3.8 %gate_blocks.1 = (bf16[512,2048]{1,0:T(8,128)(2,1)S(1)}, f32[512,128]{1,0:T(8,128)S(1)}) custom-call(f32[512,2048]{1,0:T(8,128)S(1)} %copy-done.1, bf16[512,2048]{1,0:T(8,128)(2,1)S(1)} %copy-done.4, f32[4,512,8]{2,1,0:T(8,128)S(1)} %bitcast.88, bf16[2048,256]{1,0:T(8,128)(2,1)S(1)} %bitcast.87, bf16[512,256]{1,0:T(8,128)(2,1)S(1)} %get-tuple-element.53.c_ref, ...), custom_call_target="tpu_custom_call" | custom-call | flops 1 | bytes 1 | tf_op jit(solution)/shard_map/gate_blocks/pallas_call | solution.py:161
  132.8 8.2 %project_rows.3 = bf16[512,1280]{1,0:T(8,128)(2,1)} custom-call(s32[22]{0:T(128)} %stack.132.rows_ref, s32[22]{0:T(128)} %get-tuple-element.66.mine_ref, bf16[512,2048]{1,0:T(8,128)(2,1)} %copy-done.2, bf16[320,2048]{1,0:T(8,128)(2,1)} %refs_0_.1, bf16[192,2048]{1,0:T(8,128)(2,1)} %copy-done.9, bf16[128,2048]{1,0:T(8,128)(2,1)} %collective-permute-done.8.refs_2_, ...), custom_call_target="tpu_custom_call" | custom-call | flops 1 | bytes 1 | tf_op jit(solution)/shard_map/project_rows/pallas_call | solution.py:212
  142.5 8.7 %project_rows.2 = f32[512,1280]{1,0:T(8,128)} custom-call(s32[22]{0:T(128)} %stack.132.rows_ref, s32[22]{0:T(128)} %get-tuple-element.67.mine_ref, bf16[512,2048]{1,0:T(8,128)(2,1)} %copy-done.2, bf16[320,2048]{1,0:T(8,128)(2,1)} %refs_0_.1, bf16[192,2048]{1,0:T(8,128)(2,1)} %copy-done.9, bf16[128,2048]{1,0:T(8,128)(2,1)} %collective-permute-done.8.refs_2_, ...), custom_call_target="tpu_custom_call" | custom-call | flops 1 | bytes 1 | tf_op jit(solution)/shard_map/project_rows/pallas_call | solution.py:212
  151.3 3.1 %multiply_convert_fusion = bf16[512,1280]{1,0:T(8,128)(2,1)} fusion(f32[512,1280]{1,0:T(8,128)} %project_rows.2, bf16[512,1280]{1,0:T(8,128)(2,1)S(1)} %collective-permute-done.19, f32[512]{0:T(512)S(1)} %rsqrt_select_fusion), kind=kLoop, calls=%fused_computation | loop fusion | flops 2621440 | bytes 5244928 | tf_op jit(solution)/shard_map/convert_element_type | solution.py:452
  (136 shorter events, 41.3 us)
Async XLA Ops:
  0.9 4.9 %collective-permute-start = (f32[1,60,128]{2,1,0:T(8,128)S(1)}, f32[1,60,128]{2,1,0:T(8,128)S(1)}, u32[]{:S(2)}, u32[]{:S(2)}) collective-permute-start(f32[1,60,128]{2,1,0:T(8,128)S(1)} %reshape.57), channel_id=1, source_target_pairs={{0,2},{2,0},{4,6},{6,4},{8,10},{10,8},{12,14},{14,12},{1,3},{3,1},... | collective-permute-start | bytes 92168 | tf_op jit(solution)/shard_map/ppermute | solution.py:260
  7.1 23.2 %collective-permute-start.3 = (bf16[192,2048]{1,0:T(8,128)(2,1)S(1)}, bf16[192,2048]{1,0:T(8,128)(2,1)}, u32[]{:S(2)}, u32[]{:S(2)}) collective-permute-start(bf16[192,2048]{1,0:T(8,128)(2,1)S(1)} %pad_maximum_fusion.1), channel_id=1, source_target_pairs={{4,8},{6,10},{8,4},{10,6},{5,9},{7,11},{9,5},{11,7},{20,24},{22,26... | collective-permute-start | bytes 2359304 | tf_op jit(solution)/shard_map/ppermute | solution.py:278
  8.8 21.6 %collective-permute-start.2 = (bf16[192,2048]{1,0:T(8,128)(2,1)S(1)}, bf16[192,2048]{1,0:T(8,128)(2,1)S(1)}, u32[]{:S(2)}, u32[]{:S(2)}) collective-permute-start(bf16[192,2048]{1,0:T(8,128)(2,1)S(1)} %pad_maximum_fusion.1), channel_id=1, source_target_pairs={{0,4},{2,6},{4,0},{6,2},{8,12},{10,14},{12,8},{14,10},{1,5},{3,7},... | collective-permute-start | bytes 2359304 | tf_op jit(solution)/shard_map/ppermute | solution.py:278
  12.8 17.6 %collective-permute-start.1 = (bf16[192,2048]{1,0:T(8,128)(2,1)S(1)}, bf16[192,2048]{1,0:T(8,128)(2,1)S(1)}, u32[]{:S(2)}, u32[]{:S(2)}) collective-permute-start(bf16[192,2048]{1,0:T(8,128)(2,1)S(1)} %pad_maximum_fusion.1), channel_id=1, source_target_pairs={{0,2},{2,0},{4,6},{6,4},{8,10},{10,8},{12,14},{14,12},{1,3},{3,1},... | collective-permute-start | bytes 2359304 | tf_op jit(solution)/shard_map/ppermute | solution.py:286
  14.6 27.1 %copy-start.12 = (f32[4,32,128]{2,1,0:T(8,128)}, f32[4,32,128]{2,1,0:T(8,128)S(1)}, u32[]{:S(2)}) copy-start(f32[4,32,128]{2,1,0:T(8,128)S(1)} %fusion.8) | copy-start | bytes 196612
  14.6 15.7 %collective-permute-start.4 = (f32[2,60,128]{2,1,0:T(8,128)S(1)}, f32[2,60,128]{2,1,0:T(8,128)S(1)}, u32[]{:S(2)}, u32[]{:S(2)}) collective-permute-start(f32[2,60,128]{2,1,0:T(8,128)S(1)} %pad_maximum_fusion.5), channel_id=1, source_target_pairs={{0,4},{2,6},{4,0},{6,2},{8,12},{10,14},{12,8},{14,10},{1,5},{3,7},... | collective-permute-start | bytes 184328 | tf_op jit(solution)/shard_map/ppermute | solution.py:260
  30.4 11.3 %collective-permute-start.14 = (f32[4,60,128]{2,1,0:T(8,128)S(1)}, f32[4,60,128]{2,1,0:T(8,128)S(1)}, u32[]{:S(2)}, u32[]{:S(2)}) collective-permute-start(f32[4,60,128]{2,1,0:T(8,128)S(1)} %pad_maximum_fusion.3), channel_id=1, source_target_pairs={{0,8},{2,10},{4,12},{6,14},{8,0},{10,2},{12,4},{14,6},{1,9},{3,11}... | collective-permute-start | bytes 368648 | tf_op jit(solution)/shard_map/ppermute | solution.py:260
  32.2 32.3 %collective-permute-start.7 = (bf16[192,2048]{1,0:T(8,128)(2,1)S(1)}, bf16[192,2048]{1,0:T(8,128)(2,1)}, u32[]{:S(2)}, u32[]{:S(2)}) collective-permute-start(bf16[192,2048]{1,0:T(8,128)(2,1)S(1)} %collective-permute-done.2.refs_3_), channel_id=1, source_target_pairs={{0,2},{2,0},{4,6},{6,4},{8,10},{10,8},{12,14},{14,12},{1,3},{3,1},... | collective-permute-start | bytes 2359304 | tf_op jit(solution)/shard_map/ppermute | solution.py:286
  33.8 30.7 %collective-permute-start.5 = (bf16[192,2048]{1,0:T(8,128)(2,1)S(1)}, bf16[192,2048]{1,0:T(8,128)(2,1)}, u32[]{:S(2)}, u32[]{:S(2)}) collective-permute-start(bf16[192,2048]{1,0:T(8,128)(2,1)S(1)} %collective-permute-done.2.refs_3_), channel_id=1, source_target_pairs={{4,8},{6,10},{8,4},{10,6},{5,9},{7,11},{9,5},{11,7},{20,24},{22,26... | collective-permute-start | bytes 2359304 | tf_op jit(solution)/shard_map/ppermute | solution.py:278
  36.2 17.2 %collective-permute-start.8 = (bf16[128,2048]{1,0:T(8,128)(2,1)}, bf16[128,2048]{1,0:T(8,128)(2,1)}, u32[]{:S(2)}, u32[]{:S(2)}) collective-permute-start(bf16[128,2048]{1,0:T(8,128)(2,1)} %slice.67), channel_id=1, source_target_pairs={{0,16},{16,0},{1,17},{17,1},{2,18},{18,2},{3,19},{19,3},{4,20},{20... | collective-permute-start | bytes 1572872 | tf_op jit(solution)/shard_map/ppermute | solution.py:283
  37.7 26.8 %collective-permute-start.6 = (bf16[192,2048]{1,0:T(8,128)(2,1)}, bf16[192,2048]{1,0:T(8,128)(2,1)}, u32[]{:S(2)}, u32[]{:S(2)}) collective-permute-start(bf16[192,2048]{1,0:T(8,128)(2,1)} %collective-permute-done.3), channel_id=1, source_target_pairs={{4,0},{6,2},{8,12},{10,14},{5,1},{7,3},{9,13},{11,15},{20,16},{22,... | collective-permute-start | bytes 2359304 | tf_op jit(solution)/shard_map/ppermute | solution.py:278
  41.8 36.3 %all-to-all-start = ((bf16[8,1,256,256]{3,2,1,0:T(8,128)(2,1)}), bf16[8,1,256,256]{3,2,1,0:T(8,128)(2,1)S(1)}, u32[]{:S(2)}, u32[]{:S(2)}) async-start(bf16[8,1,256,256]{3,2,1,0:T(8,128)(2,1)} %bitcast.30), calls=%async_computation | async-start | bytes 2097152 | tf_op jit(solution)/shard_map/all_to_all | solution.py:386
  52.7 49.5 %collective-permute-start.11 = (bf16[128,2048]{1,0:T(8,128)(2,1)}, bf16[128,2048]{1,0:T(8,128)(2,1)}, u32[]{:S(2)}, u32[]{:S(2)}) collective-permute-start(bf16[128,2048]{1,0:T(8,128)(2,1)} %slice.68), channel_id=1, source_target_pairs={{0,16},{16,0},{1,17},{17,1},{2,18},{18,2},{3,19},{19,3},{4,20},{20... | collective-permute-start | bytes 1572872 | tf_op jit(solution)/shard_map/ppermute | solution.py:283
  66.7 35.6 %collective-permute-start.10 = (bf16[192,2048]{1,0:T(8,128)(2,1)}, bf16[192,2048]{1,0:T(8,128)(2,1)}, u32[]{:S(2)}, u32[]{:S(2)}) collective-permute-start(bf16[192,2048]{1,0:T(8,128)(2,1)} %broadcast_select_fusion.1.refs_7_), channel_id=1, source_target_pairs={{0,2},{2,0},{4,6},{6,4},{8,10},{10,8},{12,14},{14,12},{1,3},{3,1},... | collective-permute-start | bytes 2359304 | tf_op jit(solution)/shard_map/ppermute | solution.py:286
  68.2 34.9 %collective-permute-start.9 = (bf16[192,2048]{1,0:T(8,128)(2,1)}, bf16[192,2048]{1,0:T(8,128)(2,1)}, u32[]{:S(2)}, u32[]{:S(2)}) collective-permute-start(bf16[192,2048]{1,0:T(8,128)(2,1)} %collective-permute-done.5), channel_id=1, source_target_pairs={{4,0},{6,2},{8,12},{10,14},{5,1},{7,3},{9,13},{11,15},{20,16},{22,... | collective-permute-start | bytes 2359304 | tf_op jit(solution)/shard_map/ppermute | solution.py:278
  73.3 28.9 %collective-permute-start.12 = (bf16[128,2048]{1,0:T(8,128)(2,1)}, bf16[128,2048]{1,0:T(8,128)(2,1)S(1)}, u32[]{:S(2)}, u32[]{:S(2)}) collective-permute-start(bf16[128,2048]{1,0:T(8,128)(2,1)} %slice.69), channel_id=1, source_target_pairs={{0,16},{16,0},{1,17},{17,1},{2,18},{18,2},{3,19},{19,3},{4,20},{20... | collective-permute-start | bytes 1572872 | tf_op jit(solution)/shard_map/ppermute | solution.py:283
  73.7 28.5 %collective-permute-start.13 = (bf16[128,2048]{1,0:T(8,128)(2,1)}, bf16[128,2048]{1,0:T(8,128)(2,1)}, u32[]{:S(2)}, u32[]{:S(2)}) collective-permute-start(bf16[128,2048]{1,0:T(8,128)(2,1)} %slice.88), channel_id=1, source_target_pairs={{0,16},{16,0},{1,17},{17,1},{2,18},{18,2},{3,19},{19,3},{4,20},{20... | collective-permute-start | bytes 1572872 | tf_op jit(solution)/shard_map/ppermute | solution.py:283
  79.6 42.6 %all-to-all-start.1 = ((bf16[8,256,256]{2,1,0:T(8,128)(2,1)}), bf16[8,256,256]{2,1,0:T(8,128)(2,1)S(1)}, u32[]{:S(2)}, u32[]{:S(2)}) async-start(bf16[8,256,256]{2,1,0:T(8,128)(2,1)} %choose_rows.1), calls=%async_computation.1 | async-start | bytes 2097152 | tf_op jit(solution)/shard_map/all_to_all | solution.py:428
  104.3 10.0 %collective-permute-start.15 = (bf16[128,2048]{1,0:T(8,128)(2,1)S(1)}, bf16[128,2048]{1,0:T(8,128)(2,1)}, u32[]{:S(2)}, u32[]{:S(2)}) collective-permute-start(bf16[128,2048]{1,0:T(8,128)(2,1)S(1)} %slice.98), channel_id=1, source_target_pairs={{0,16},{16,0},{1,17},{17,1},{2,18},{18,2},{3,19},{19,3},{4,20},{20... | collective-permute-start | bytes 1572872 | tf_op jit(solution)/shard_map/ppermute | solution.py:283
  105.9 25.3 %collective-permute-start.17 = (bf16[192,2048]{1,0:T(8,128)(2,1)S(1)}, bf16[192,2048]{1,0:T(8,128)(2,1)}, u32[]{:S(2)}, u32[]{:S(2)}) collective-permute-start(bf16[192,2048]{1,0:T(8,128)(2,1)S(1)} %broadcast_select_fusion.refs_11_), channel_id=1, source_target_pairs={{0,2},{2,0},{4,6},{6,4},{8,10},{10,8},{12,14},{14,12},{1,3},{3,1},... | collective-permute-start | bytes 2359304 | tf_op jit(solution)/shard_map/ppermute | solution.py:286
  116.3 15.0 %collective-permute-start.16 = (bf16[128,2048]{1,0:T(8,128)(2,1)}, bf16[128,2048]{1,0:T(8,128)(2,1)}, u32[]{:S(2)}, u32[]{:S(2)}) collective-permute-start(bf16[128,2048]{1,0:T(8,128)(2,1)} %slice.87), channel_id=1, source_target_pairs={{0,16},{16,0},{1,17},{17,1},{2,18},{18,2},{3,19},{19,3},{4,20},{20... | collective-permute-start | bytes 1572872 | tf_op jit(solution)/shard_map/ppermute | solution.py:283
  117.8 15.1 %collective-permute-start.18 = (bf16[128,2048]{1,0:T(8,128)(2,1)}, bf16[128,2048]{1,0:T(8,128)(2,1)}, u32[]{:S(2)}, u32[]{:S(2)}) collective-permute-start(bf16[128,2048]{1,0:T(8,128)(2,1)} %collective-permute-done.15.refs_12_), channel_id=1, source_target_pairs={{0,2},{2,0},{4,6},{6,4},{8,10},{10,8},{12,14},{14,12},{1,3},{3,1},... | collective-permute-start | bytes 1572872 | tf_op jit(solution)/shard_map/ppermute | solution.py:286
  141.1 10.2 %collective-permute-start.19 = (bf16[512,1280]{1,0:T(8,128)(2,1)}, bf16[512,1280]{1,0:T(8,128)(2,1)S(1)}, u32[]{:S(2)}, u32[]{:S(2)}) collective-permute-start(bf16[512,1280]{1,0:T(8,128)(2,1)} %project_rows.3), channel_id=1, source_target_pairs={{0,1},{1,0},{2,3},{3,2},{4,5},{5,4},{6,7},{7,6},{8,9},{9,8},{10,11... | collective-permute-start | bytes 3932168 | tf_op jit(solution)/shard_map/ppermute | solution.py:450
  141.3 9.9 %collective-permute-start.20 = (f32[512]{0:T(512)S(1)}, f32[512]{0:T(512)S(1)}, u32[]{:S(2)}, u32[]{:S(2)}) collective-permute-start(f32[512]{0:T(512)S(1)} %reduce_sum.19), channel_id=1, source_target_pairs={{0,1},{1,0},{2,3},{3,2},{4,5},{5,4},{6,7},{7,6},{8,9},{9,8},{10,11... | collective-permute-start | bytes 6152 | tf_op jit(solution)/shard_map/ppermute | solution.py:434
  (26 other events, 206.0 us)

commit v5 on v4

--- a/solution.py
+++ b/solution.py
@@ -184,27 +184,43 @@
 
 
 def project_kernel(cuts, rows_ref, mine_ref, value_ref, *refs):
-    pieces, out_ref, held, sems = refs[:-3], refs[-3], refs[-2], refs[-1]
-    copies = []
-    for i, (piece, first, size) in enumerate(cuts):
-        at = pl.multiple_of(rows_ref[i], 16)
-        copies.append(
-            pltpu.make_async_copy(
-                pieces[piece].at[pl.ds(first, size), :],
-                held.at[pl.ds(at, size), :],
-                sems.at[i],
+    pieces, out_ref, value, held, total, sems = refs[:-5], *refs[-5:]
+    depth = value.shape[1] // 2
+    loads = []
+    for half in range(2):
+        span = slice(half * depth, (half + 1) * depth)
+        whole = pltpu.make_async_copy(
+            value_ref.at[:, span], value.at[:, span], sems.at[half, len(cuts)]
+        )
+        whole.start()
+        copies = []
+        for i, (piece, first, size) in enumerate(cuts):
+            at = pl.multiple_of(rows_ref[i], 16)
+            copy = pltpu.make_async_copy(
+                pieces[piece].at[pl.ds(first, size), span],
+                held.at[pl.ds(at, size), span],
+                sems.at[half, i],
             )
-        )
-    for i, copy in enumerate(copies):
-        pl.when(mine_ref[i] == 1)(copy.start)
-    for i, copy in enumerate(copies):
-        pl.when(mine_ref[i] == 1)(copy.wait)
+            pl.when(mine_ref[i] == 1)(copy.start)
+            copies.append(copy)
+        loads.append((span, whole, copies))
     step = 256
-    for first in range(0, out_ref.shape[1], step):
-        cols = slice(first, min(first + step, out_ref.shape[1]))
-        out_ref[:, cols] = lax.dot_general(
-            value_ref[...], held[cols, :], (((1,), (1,)), ((), ())), preferred_element_type=jnp.float32
-        ).astype(out_ref.dtype)
+    for half, (span, whole, copies) in enumerate(loads):
+        whole.wait()
+        for i, copy in enumerate(copies):
+            pl.when(mine_ref[i] == 1)(copy.wait)
+        for at in range(0, out_ref.shape[1], step):
+            cols = slice(at, min(at + step, out_ref.shape[1]))
+            part = lax.dot_general(
+                value[:, span],
+                held[cols, span],
+                (((1,), (1,)), ((), ())),
+                preferred_element_type=jnp.float32,
+            )
+            if half == 0:
+                total[:, cols] = part
+            else:
+                out_ref[:, cols] = (total[:, cols] + part).astype(out_ref.dtype)
 
 
 def project(value, pieces, cuts, rows, mine, total, dtype):
@@ -212,13 +228,14 @@
     return pl.pallas_call(
         functools.partial(project_kernel, cuts),
         in_specs=[pl.BlockSpec(memory_space=pltpu.SMEM)] * 2
-        + [pl.BlockSpec(memory_space=pltpu.VMEM)]
-        + [pl.BlockSpec(memory_space=pl.ANY)] * len(pieces),
+        + [pl.BlockSpec(memory_space=pl.ANY)] * (1 + len(pieces)),
         out_specs=pl.BlockSpec(memory_space=pltpu.VMEM),
         out_shape=jax.ShapeDtypeStruct((tokens, total), dtype),
         scratch_shapes=[
+            pltpu.VMEM((tokens, channels), value.dtype),
             pltpu.VMEM((total, channels), pieces[0].dtype),
-            pltpu.SemaphoreType.DMA((len(cuts),)),
+            pltpu.VMEM((tokens, total), jnp.float32),
+            pltpu.SemaphoreType.DMA((2, len(cuts) + 1)),
         ],
         compiler_params=pltpu.CompilerParams(vmem_limit_bytes=60 * 2**20),
         cost_estimate=QUICK,

time: 156 us -> 154 us (0.987)
  no operation moved by 1% of the time
where the time goes in v5:
time: 154 us; the launch traced here: 153 us
  starting transfers between devices  43.6 us (28%)
  waiting for transfers between devices  33.7 us (22%)
  Pallas kernels  32.5 us (21%)
  local copies, waits for them, and re-layouts  22.7 us (15%)
  other arithmetic  16.3 us (11%)
  between operations  3.04 us (2%)
    pallas_call x2, Pallas kernels, project(): pl.pallas_call(functools.partial(project_kernel, cuts), in_specs=[pl.Bloc...  15.9 us
    ppermute x3, waiting for transfers between devices, gather_step(): other = lax.ppermute(held, axis, [(i, i ^ step) for i in range(n)])  14.5 us
    pallas_call x1, Pallas kernels, scan_call(): pl.pallas_call(scan_kernel, grid=(groups,), in_specs=[pl.BlockSpec((token...  11.3 us
    ppermute x5, waiting for transfers between devices, swap(): lax.ppermute(value, 'cache', [(2 * i + p, 2 * j + p) for i, j in pairs fo...  11.1 us
    ppermute x5, starting transfers between devices, swap(): lax.ppermute(value, 'cache', [(2 * i + p, 2 * j + p) for i, j in pairs fo...  9.74 us
    unnamed x50, local copies, waits for them, and re-layouts  9.57 us
    ppermute x5, starting transfers between devices, beside(): return lax.ppermute(value, 'cache', [(i, i ^ 1) for i in range(n)])  8.92 us
    slice x6, local copies, waits for them, and re-layouts, across(): return lax.ppermute(value[:share], 'groups', [(0, 1), (1, 0)])  7.49 us
  transfers between devices with their start and end apart: 23, of which 5 were waited for; matrix products, arithmetic and copies ran while one was open for 17% of the time, Pallas kernels for 16%

profile of v5, /device:TPU:0, one launch (start us, length us, event | category | flops | bytes accessed | tf_op | source)
XLA Modules:
  0.0 153.3 jit_solution(8511712870839585082)
XLA Ops:
  0.9 3.0 %collective-permute-start = (f32[1,60,128]{2,1,0:T(8,128)S(1)}, f32[1,60,128]{2,1,0:T(8,128)S(1)}, u32[]{:S(2)}, u32[]{:S(2)}) collective-permute-start(f32[1,60,128]{2,1,0:T(8,128)S(1)} %reshape.57), channel_id=1, source_target_pairs={{0,2},{2,0},{4,6},{6,4},{8,10},{10,8},{12,14},{14,12},{1,3},{3,1},... | collective-permute-start | bytes 92168 | tf_op jit(solution)/shard_map/ppermute | solution.py:277
  8.8 4.0 %collective-permute-start.2 = (bf16[192,2048]{1,0:T(8,128)(2,1)S(1)}, bf16[192,2048]{1,0:T(8,128)(2,1)S(1)}, u32[]{:S(2)}, u32[]{:S(2)}) collective-permute-start(bf16[192,2048]{1,0:T(8,128)(2,1)S(1)} %pad_maximum_fusion.1), channel_id=1, source_target_pairs={{0,4},{2,6},{4,0},{6,2},{8,12},{10,14},{12,8},{14,10},{1,5},{3,7},... | collective-permute-start | bytes 2359304 | tf_op jit(solution)/shard_map/ppermute | solution.py:295
  16.9 13.4 %collective-permute-done.4 = f32[2,60,128]{2,1,0:T(8,128)S(1)} collective-permute-done((f32[2,60,128]{2,1,0:T(8,128)S(1)}, f32[2,60,128]{2,1,0:T(8,128)S(1)}, u32[]{:S(2)}, u32[]{:S(2)}) %collective-permute-start.4) | collective-permute-done | bytes 61472 | tf_op jit(solution)/shard_map/ppermute | solution.py:277
  30.4 1.7 %collective-permute-start.14 = (f32[4,60,128]{2,1,0:T(8,128)S(1)}, f32[4,60,128]{2,1,0:T(8,128)S(1)}, u32[]{:S(2)}, u32[]{:S(2)}) collective-permute-start(f32[4,60,128]{2,1,0:T(8,128)S(1)} %pad_maximum_fusion.3), channel_id=1, source_target_pairs={{0,8},{2,10},{4,12},{6,14},{8,0},{10,2},{12,4},{14,6},{1,9},{3,11}... | collective-permute-start | bytes 368648 | tf_op jit(solution)/shard_map/ppermute | solution.py:277
  38.9 2.8 %convert_element_type.32 = bf16[1,32,64,256]{3,2,1,0:T(8,128)(2,1)} convert(f32[1,32,64,256]{3,2,1,0:T(8,128)} %param.28) | non-fusion elementwise | flops 524288 | bytes 3145728 | tf_op jit(solution)/shard_map/convert_element_type | solution.py:400
  41.8 5.8 %all-to-all-start = ((bf16[8,1,256,256]{3,2,1,0:T(8,128)(2,1)}), bf16[8,1,256,256]{3,2,1,0:T(8,128)(2,1)S(1)}, u32[]{:S(2)}, u32[]{:S(2)}) async-start(bf16[8,1,256,256]{3,2,1,0:T(8,128)(2,1)} %bitcast.30), calls=%async_computation | async-start | bytes 2097152 | tf_op jit(solution)/shard_map/all_to_all | solution.py:403
  48.0 2.2 %convert_element_type.33 = f32[512,512]{1,0:T(8,128)} convert(bf16[512,512]{1,0:T(8,128)(2,1)} %param.19) | non-fusion elementwise | flops 262144 | bytes 1572864 | tf_op jit(solution)/shard_map/convert_element_type | solution.py:25
  53.4 11.1 %collective-permute-done.6 = bf16[192,2048]{1,0:T(8,128)(2,1)} collective-permute-done((bf16[192,2048]{1,0:T(8,128)(2,1)}, bf16[192,2048]{1,0:T(8,128)(2,1)}, u32[]{:S(2)}, u32[]{:S(2)}) %collective-permute-start.6) | collective-permute-done | bytes 786464 | tf_op jit(solution)/shard_map/ppermute | solution.py:295
  64.5 2.2 %broadcast_select_fusion.1.refs_7_ = bf16[192,2048]{1,0:T(8,128)(2,1)} fusion(bf16[192,2048]{1,0:T(8,128)(2,1)} %collective-permute-done.3, bf16[192,2048]{1,0:T(8,128)(2,1)} %collective-permute-done.6, pred[]{:T(512)S(6)} %or.3), kind=kLoop, calls=%fused_computation.16 | loop fusion | flops 393216 | bytes 2359297 | tf_op jit(solution)/shard_map/jit(_where)/select_n | solution.py:319
  69.5 1.9 %slice.88 = bf16[128,2048]{1,0:T(8,128)(2,1)} slice(bf16[192,2048]{1,0:T(8,128)(2,1)} %broadcast_select_fusion.1.refs_7_), slice={[0:128], [0:2048]} | slice | bytes 1048576 | tf_op jit(solution)/shard_map/slice | solution.py:300
  71.4 1.9 %slice.69 = bf16[128,2048]{1,0:T(8,128)(2,1)} slice(bf16[192,2048]{1,0:T(8,128)(2,1)} %collective-permute-done.7.refs_5_), slice={[0:128], [0:2048]} | slice | bytes 1048576 | tf_op jit(solution)/shard_map/slice | solution.py:300
  73.7 1.7 %collective-permute-start.13 = (bf16[128,2048]{1,0:T(8,128)(2,1)}, bf16[128,2048]{1,0:T(8,128)(2,1)}, u32[]{:S(2)}, u32[]{:S(2)}) collective-permute-start(bf16[128,2048]{1,0:T(8,128)(2,1)} %slice.88), channel_id=1, source_target_pairs={{0,16},{16,0},{1,17},{17,1},{2,18},{18,2},{3,19},{19,3},{4,20},{20... | collective-permute-start | bytes 1572872 | tf_op jit(solution)/shard_map/ppermute | solution.py:300
  79.6 6.5 %all-to-all-start.1 = ((bf16[8,256,256]{2,1,0:T(8,128)(2,1)}), bf16[8,256,256]{2,1,0:T(8,128)(2,1)S(1)}, u32[]{:S(2)}, u32[]{:S(2)}) async-start(bf16[8,256,256]{2,1,0:T(8,128)(2,1)} %choose_rows.1), calls=%async_computation.1 | async-start | bytes 2097152 | tf_op jit(solution)/shard_map/all_to_all | solution.py:445
  88.9 11.3 %scan_blocks.1.y_ref = f32[512,2048]{1,0:T(8,128)S(1)} custom-call(bf16[512,2048]{1,0:T(8,128)(2,1)S(1)} %copy-done.3, f32[8,2048]{1,0:T(8,128)S(1)} %concatenate.32.prev_ref, bf16[4,2048]{1,0:T(4,128)(2,1)S(1)} %copy-done.5, f32[4,512,16]{2,1,0:T(8,128)S(1)} %copy.40.cols_ref, f32[32,512]{1,0:T(8,128)S(1)} %get-tuple-element.56.arow_ref, ...), custom_call_target="tpu_custom_call" | custom-call | flops 1 | bytes 1 | tf_op jit(solution)/shard_map/scan_blocks/pallas_call | solution.py:103
  100.2 2.0 %copy-done = f32[512,2048]{1,0:T(8,128)} copy-done((f32[512,2048]{1,0:T(8,128)}, f32[512,2048]{1,0:T(8,128)S(1)}, u32[]{:S(2)}) %copy-start) | copy-done | bytes 4194328
  105.9 2.0 %collective-permute-start.17 = (bf16[192,2048]{1,0:T(8,128)(2,1)S(1)}, bf16[192,2048]{1,0:T(8,128)(2,1)}, u32[]{:S(2)}, u32[]{:S(2)}) collective-permute-start(bf16[192,2048]{1,0:T(8,128)(2,1)S(1)} %broadcast_select_fusion.refs_11_), channel_id=1, source_target_pairs={{0,2},{2,0},{4,6},{6,4},{8,10},{10,8},{12,14},{14,12},{1,3},{3,1},... | collective-permute-start | bytes 2359304 | tf_op jit(solution)/shard_map/ppermute | solution.py:303
  107.9 6.5 %collective-permute-done.15.refs_12_ = bf16[128,2048]{1,0:T(8,128)(2,1)} collective-permute-done((bf16[128,2048]{1,0:T(8,128)(2,1)S(1)}, bf16[128,2048]{1,0:T(8,128)(2,1)}, u32[]{:S(2)}, u32[]{:S(2)}) %collective-permute-start.15) | collective-permute-done | bytes 524320 | tf_op jit(solution)/shard_map/ppermute | solution.py:300
  114.4 1.9 %slice.87 = bf16[128,2048]{1,0:T(8,128)(2,1)} slice(bf16[192,2048]{1,0:T(8,128)(2,1)} %collective-permute-done.10.refs_9_), slice={[0:128], [0:2048]} | slice | bytes 1048576 | tf_op jit(solution)/shard_map/slice | solution.py:300
  117.8 2.3 %collective-permute-start.18 = (bf16[128,2048]{1,0:T(8,128)(2,1)}, bf16[128,2048]{1,0:T(8,128)(2,1)}, u32[]{:S(2)}, u32[]{:S(2)}) collective-permute-start(bf16[128,2048]{1,0:T(8,128)(2,1)} %collective-permute-done.15.refs_12_), channel_id=1, source_target_pairs={{0,2},{2,0},{4,6},{6,4},{8,10},{10,8},{12,14},{14,12},{1,3},{3,1},... | collective-permute-start | bytes 1572872 | tf_op jit(solution)/shard_map/ppermute | solution.py:303
  122.3 2.2 %copy-done.1 = f32[512,2048]{1,0:T(8,128)S(1)} copy-done((f32[512,2048]{1,0:T(8,128)S(1)}, f32[512,2048]{1,0:T(8,128)}, u32[]{:S(2)}) %copy-start.1) | copy-done | bytes 4194328
  126.1 3.8 %gate_blocks.1 = (bf16[512,2048]{1,0:T(8,128)(2,1)S(1)}, f32[512,128]{1,0:T(8,128)S(1)}) custom-call(f32[512,2048]{1,0:T(8,128)S(1)} %copy-done.1, bf16[512,2048]{1,0:T(8,128)(2,1)S(1)} %copy-done.4, f32[4,512,8]{2,1,0:T(8,128)S(1)} %bitcast.88, bf16[2048,256]{1,0:T(8,128)(2,1)S(1)} %bitcast.87, bf16[512,256]{1,0:T(8,128)(2,1)S(1)} %get-tuple-element.53.c_ref, ...), custom_call_target="tpu_custom_call" | custom-call | flops 1 | bytes 1 | tf_op jit(solution)/shard_map/gate_blocks/pallas_call | solution.py:161
  132.8 7.7 %project_rows.3 = bf16[512,1280]{1,0:T(8,128)(2,1)} custom-call(s32[22]{0:T(128)} %stack.132.rows_ref, s32[22]{0:T(128)} %get-tuple-element.66.mine_ref, bf16[512,2048]{1,0:T(8,128)(2,1)} %copy-done.2, bf16[320,2048]{1,0:T(8,128)(2,1)} %refs_0_.1, bf16[192,2048]{1,0:T(8,128)(2,1)} %copy-done.9, bf16[128,2048]{1,0:T(8,128)(2,1)} %collective-permute-done.8.refs_2_, ...), custom_call_target="tpu_custom_call" | custom-call | flops 1 | bytes 1 | tf_op jit(solution)/shard_map/project_rows/pallas_call | solution.py:228
  142.0 8.2 %project_rows.2 = f32[512,1280]{1,0:T(8,128)} custom-call(s32[22]{0:T(128)} %stack.132.rows_ref, s32[22]{0:T(128)} %get-tuple-element.67.mine_ref, bf16[512,2048]{1,0:T(8,128)(2,1)} %copy-done.2, bf16[320,2048]{1,0:T(8,128)(2,1)} %refs_0_.1, bf16[192,2048]{1,0:T(8,128)(2,1)} %copy-done.9, bf16[128,2048]{1,0:T(8,128)(2,1)} %collective-permute-done.8.refs_2_, ...), custom_call_target="tpu_custom_call" | custom-call | flops 1 | bytes 1 | tf_op jit(solution)/shard_map/project_rows/pallas_call | solution.py:228
  150.2 3.1 %multiply_convert_fusion = bf16[512,1280]{1,0:T(8,128)(2,1)} fusion(f32[512,1280]{1,0:T(8,128)} %project_rows.2, bf16[512,1280]{1,0:T(8,128)(2,1)S(1)} %collective-permute-done.19, f32[512]{0:T(512)S(1)} %rsqrt_select_fusion), kind=kLoop, calls=%fused_computation | loop fusion | flops 2621440 | bytes 5244928 | tf_op jit(solution)/shard_map/convert_element_type | solution.py:469
  (136 shorter events, 41.3 us)
Async XLA Ops:
  0.9 4.9 %collective-permute-start = (f32[1,60,128]{2,1,0:T(8,128)S(1)}, f32[1,60,128]{2,1,0:T(8,128)S(1)}, u32[]{:S(2)}, u32[]{:S(2)}) collective-permute-start(f32[1,60,128]{2,1,0:T(8,128)S(1)} %reshape.57), channel_id=1, source_target_pairs={{0,2},{2,0},{4,6},{6,4},{8,10},{10,8},{12,14},{14,12},{1,3},{3,1},... | collective-permute-start | bytes 92168 | tf_op jit(solution)/shard_map/ppermute | solution.py:277
  7.1 23.2 %collective-permute-start.3 = (bf16[192,2048]{1,0:T(8,128)(2,1)S(1)}, bf16[192,2048]{1,0:T(8,128)(2,1)}, u32[]{:S(2)}, u32[]{:S(2)}) collective-permute-start(bf16[192,2048]{1,0:T(8,128)(2,1)S(1)} %pad_maximum_fusion.1), channel_id=1, source_target_pairs={{4,8},{6,10},{8,4},{10,6},{5,9},{7,11},{9,5},{11,7},{20,24},{22,26... | collective-permute-start | bytes 2359304 | tf_op jit(solution)/shard_map/ppermute | solution.py:295
  8.8 21.6 %collective-permute-start.2 = (bf16[192,2048]{1,0:T(8,128)(2,1)S(1)}, bf16[192,2048]{1,0:T(8,128)(2,1)S(1)}, u32[]{:S(2)}, u32[]{:S(2)}) collective-permute-start(bf16[192,2048]{1,0:T(8,128)(2,1)S(1)} %pad_maximum_fusion.1), channel_id=1, source_target_pairs={{0,4},{2,6},{4,0},{6,2},{8,12},{10,14},{12,8},{14,10},{1,5},{3,7},... | collective-permute-start | bytes 2359304 | tf_op jit(solution)/shard_map/ppermute | solution.py:295
  12.8 17.6 %collective-permute-start.1 = (bf16[192,2048]{1,0:T(8,128)(2,1)S(1)}, bf16[192,2048]{1,0:T(8,128)(2,1)S(1)}, u32[]{:S(2)}, u32[]{:S(2)}) collective-permute-start(bf16[192,2048]{1,0:T(8,128)(2,1)S(1)} %pad_maximum_fusion.1), channel_id=1, source_target_pairs={{0,2},{2,0},{4,6},{6,4},{8,10},{10,8},{12,14},{14,12},{1,3},{3,1},... | collective-permute-start | bytes 2359304 | tf_op jit(solution)/shard_map/ppermute | solution.py:303
  14.6 27.1 %copy-start.12 = (f32[4,32,128]{2,1,0:T(8,128)}, f32[4,32,128]{2,1,0:T(8,128)S(1)}, u32[]{:S(2)}) copy-start(f32[4,32,128]{2,1,0:T(8,128)S(1)} %fusion.8) | copy-start | bytes 196612
  14.6 15.7 %collective-permute-start.4 = (f32[2,60,128]{2,1,0:T(8,128)S(1)}, f32[2,60,128]{2,1,0:T(8,128)S(1)}, u32[]{:S(2)}, u32[]{:S(2)}) collective-permute-start(f32[2,60,128]{2,1,0:T(8,128)S(1)} %pad_maximum_fusion.5), channel_id=1, source_target_pairs={{0,4},{2,6},{4,0},{6,2},{8,12},{10,14},{12,8},{14,10},{1,5},{3,7},... | collective-permute-start | bytes 184328 | tf_op jit(solution)/shard_map/ppermute | solution.py:277
  30.4 11.3 %collective-permute-start.14 = (f32[4,60,128]{2,1,0:T(8,128)S(1)}, f32[4,60,128]{2,1,0:T(8,128)S(1)}, u32[]{:S(2)}, u32[]{:S(2)}) collective-permute-start(f32[4,60,128]{2,1,0:T(8,128)S(1)} %pad_maximum_fusion.3), channel_id=1, source_target_pairs={{0,8},{2,10},{4,12},{6,14},{8,0},{10,2},{12,4},{14,6},{1,9},{3,11}... | collective-permute-start | bytes 368648 | tf_op jit(solution)/shard_map/ppermute | solution.py:277
  32.2 32.3 %collective-permute-start.7 = (bf16[192,2048]{1,0:T(8,128)(2,1)S(1)}, bf16[192,2048]{1,0:T(8,128)(2,1)}, u32[]{:S(2)}, u32[]{:S(2)}) collective-permute-start(bf16[192,2048]{1,0:T(8,128)(2,1)S(1)} %collective-permute-done.2.refs_3_), channel_id=1, source_target_pairs={{0,2},{2,0},{4,6},{6,4},{8,10},{10,8},{12,14},{14,12},{1,3},{3,1},... | collective-permute-start | bytes 2359304 | tf_op jit(solution)/shard_map/ppermute | solution.py:303
  33.8 30.7 %collective-permute-start.5 = (bf16[192,2048]{1,0:T(8,128)(2,1)S(1)}, bf16[192,2048]{1,0:T(8,128)(2,1)}, u32[]{:S(2)}, u32[]{:S(2)}) collective-permute-start(bf16[192,2048]{1,0:T(8,128)(2,1)S(1)} %collective-permute-done.2.refs_3_), channel_id=1, source_target_pairs={{4,8},{6,10},{8,4},{10,6},{5,9},{7,11},{9,5},{11,7},{20,24},{22,26... | collective-permute-start | bytes 2359304 | tf_op jit(solution)/shard_map/ppermute | solution.py:295
  36.2 17.2 %collective-permute-start.8 = (bf16[128,2048]{1,0:T(8,128)(2,1)}, bf16[128,2048]{1,0:T(8,128)(2,1)}, u32[]{:S(2)}, u32[]{:S(2)}) collective-permute-start(bf16[128,2048]{1,0:T(8,128)(2,1)} %slice.67), channel_id=1, source_target_pairs={{0,16},{16,0},{1,17},{17,1},{2,18},{18,2},{3,19},{19,3},{4,20},{20... | collective-permute-start | bytes 1572872 | tf_op jit(solution)/shard_map/ppermute | solution.py:300
  37.7 26.8 %collective-permute-start.6 = (bf16[192,2048]{1,0:T(8,128)(2,1)}, bf16[192,2048]{1,0:T(8,128)(2,1)}, u32[]{:S(2)}, u32[]{:S(2)}) collective-permute-start(bf16[192,2048]{1,0:T(8,128)(2,1)} %collective-permute-done.3), channel_id=1, source_target_pairs={{4,0},{6,2},{8,12},{10,14},{5,1},{7,3},{9,13},{11,15},{20,16},{22,... | collective-permute-start | bytes 2359304 | tf_op jit(solution)/shard_map/ppermute | solution.py:295
  41.8 36.3 %all-to-all-start = ((bf16[8,1,256,256]{3,2,1,0:T(8,128)(2,1)}), bf16[8,1,256,256]{3,2,1,0:T(8,128)(2,1)S(1)}, u32[]{:S(2)}, u32[]{:S(2)}) async-start(bf16[8,1,256,256]{3,2,1,0:T(8,128)(2,1)} %bitcast.30), calls=%async_computation | async-start | bytes 2097152 | tf_op jit(solution)/shard_map/all_to_all | solution.py:403
  52.7 49.5 %collective-permute-start.11 = (bf16[128,2048]{1,0:T(8,128)(2,1)}, bf16[128,2048]{1,0:T(8,128)(2,1)}, u32[]{:S(2)}, u32[]{:S(2)}) collective-permute-start(bf16[128,2048]{1,0:T(8,128)(2,1)} %slice.68), channel_id=1, source_target_pairs={{0,16},{16,0},{1,17},{17,1},{2,18},{18,2},{3,19},{19,3},{4,20},{20... | collective-permute-start | bytes 1572872 | tf_op jit(solution)/shard_map/ppermute | solution.py:300
  66.7 35.6 %collective-permute-start.10 = (bf16[192,2048]{1,0:T(8,128)(2,1)}, bf16[192,2048]{1,0:T(8,128)(2,1)}, u32[]{:S(2)}, u32[]{:S(2)}) collective-permute-start(bf16[192,2048]{1,0:T(8,128)(2,1)} %broadcast_select_fusion.1.refs_7_), channel_id=1, source_target_pairs={{0,2},{2,0},{4,6},{6,4},{8,10},{10,8},{12,14},{14,12},{1,3},{3,1},... | collective-permute-start | bytes 2359304 | tf_op jit(solution)/shard_map/ppermute | solution.py:303
  68.2 34.9 %collective-permute-start.9 = (bf16[192,2048]{1,0:T(8,128)(2,1)}, bf16[192,2048]{1,0:T(8,128)(2,1)}, u32[]{:S(2)}, u32[]{:S(2)}) collective-permute-start(bf16[192,2048]{1,0:T(8,128)(2,1)} %collective-permute-done.5), channel_id=1, source_target_pairs={{4,0},{6,2},{8,12},{10,14},{5,1},{7,3},{9,13},{11,15},{20,16},{22,... | collective-permute-start | bytes 2359304 | tf_op jit(solution)/shard_map/ppermute | solution.py:295
  73.3 28.9 %collective-permute-start.12 = (bf16[128,2048]{1,0:T(8,128)(2,1)}, bf16[128,2048]{1,0:T(8,128)(2,1)S(1)}, u32[]{:S(2)}, u32[]{:S(2)}) collective-permute-start(bf16[128,2048]{1,0:T(8,128)(2,1)} %slice.69), channel_id=1, source_target_pairs={{0,16},{16,0},{1,17},{17,1},{2,18},{18,2},{3,19},{19,3},{4,20},{20... | collective-permute-start | bytes 1572872 | tf_op jit(solution)/shard_map/ppermute | solution.py:300
  73.7 28.5 %collective-permute-start.13 = (bf16[128,2048]{1,0:T(8,128)(2,1)}, bf16[128,2048]{1,0:T(8,128)(2,1)}, u32[]{:S(2)}, u32[]{:S(2)}) collective-permute-start(bf16[128,2048]{1,0:T(8,128)(2,1)} %slice.88), channel_id=1, source_target_pairs={{0,16},{16,0},{1,17},{17,1},{2,18},{18,2},{3,19},{19,3},{4,20},{20... | collective-permute-start | bytes 1572872 | tf_op jit(solution)/shard_map/ppermute | solution.py:300
  79.6 42.6 %all-to-all-start.1 = ((bf16[8,256,256]{2,1,0:T(8,128)(2,1)}), bf16[8,256,256]{2,1,0:T(8,128)(2,1)S(1)}, u32[]{:S(2)}, u32[]{:S(2)}) async-start(bf16[8,256,256]{2,1,0:T(8,128)(2,1)} %choose_rows.1), calls=%async_computation.1 | async-start | bytes 2097152 | tf_op jit(solution)/shard_map/all_to_all | solution.py:445
  104.3 10.0 %collective-permute-start.15 = (bf16[128,2048]{1,0:T(8,128)(2,1)S(1)}, bf16[128,2048]{1,0:T(8,128)(2,1)}, u32[]{:S(2)}, u32[]{:S(2)}) collective-permute-start(bf16[128,2048]{1,0:T(8,128)(2,1)S(1)} %slice.98), channel_id=1, source_target_pairs={{0,16},{16,0},{1,17},{17,1},{2,18},{18,2},{3,19},{19,3},{4,20},{20... | collective-permute-start | bytes 1572872 | tf_op jit(solution)/shard_map/ppermute | solution.py:300
  105.9 25.3 %collective-permute-start.17 = (bf16[192,2048]{1,0:T(8,128)(2,1)S(1)}, bf16[192,2048]{1,0:T(8,128)(2,1)}, u32[]{:S(2)}, u32[]{:S(2)}) collective-permute-start(bf16[192,2048]{1,0:T(8,128)(2,1)S(1)} %broadcast_select_fusion.refs_11_), channel_id=1, source_target_pairs={{0,2},{2,0},{4,6},{6,4},{8,10},{10,8},{12,14},{14,12},{1,3},{3,1},... | collective-permute-start | bytes 2359304 | tf_op jit(solution)/shard_map/ppermute | solution.py:303
  116.3 15.0 %collective-permute-start.16 = (bf16[128,2048]{1,0:T(8,128)(2,1)}, bf16[128,2048]{1,0:T(8,128)(2,1)}, u32[]{:S(2)}, u32[]{:S(2)}) collective-permute-start(bf16[128,2048]{1,0:T(8,128)(2,1)} %slice.87), channel_id=1, source_target_pairs={{0,16},{16,0},{1,17},{17,1},{2,18},{18,2},{3,19},{19,3},{4,20},{20... | collective-permute-start | bytes 1572872 | tf_op jit(solution)/shard_map/ppermute | solution.py:300
  117.8 15.1 %collective-permute-start.18 = (bf16[128,2048]{1,0:T(8,128)(2,1)}, bf16[128,2048]{1,0:T(8,128)(2,1)}, u32[]{:S(2)}, u32[]{:S(2)}) collective-permute-start(bf16[128,2048]{1,0:T(8,128)(2,1)} %collective-permute-done.15.refs_12_), channel_id=1, source_target_pairs={{0,2},{2,0},{4,6},{6,4},{8,10},{10,8},{12,14},{14,12},{1,3},{3,1},... | collective-permute-start | bytes 1572872 | tf_op jit(solution)/shard_map/ppermute | solution.py:303
  140.6 9.6 %collective-permute-start.19 = (bf16[512,1280]{1,0:T(8,128)(2,1)}, bf16[512,1280]{1,0:T(8,128)(2,1)S(1)}, u32[]{:S(2)}, u32[]{:S(2)}) collective-permute-start(bf16[512,1280]{1,0:T(8,128)(2,1)} %project_rows.3), channel_id=1, source_target_pairs={{0,1},{1,0},{2,3},{3,2},{4,5},{5,4},{6,7},{7,6},{8,9},{9,8},{10,11... | collective-permute-start | bytes 3932168 | tf_op jit(solution)/shard_map/ppermute | solution.py:467
  140.8 9.4 %collective-permute-start.20 = (f32[512]{0:T(512)S(1)}, f32[512]{0:T(512)S(1)}, u32[]{:S(2)}, u32[]{:S(2)}) collective-permute-start(f32[512]{0:T(512)S(1)} %reduce_sum.19), channel_id=1, source_target_pairs={{0,1},{1,0},{2,3},{3,2},{4,5},{5,4},{6,7},{7,6},{8,9},{9,8},{10,11... | collective-permute-start | bytes 6152 | tf_op jit(solution)/shard_map/ppermute | solution.py:451
  (26 other events, 206.0 us)

commit v6 on v5

--- a/solution.py
+++ b/solution.py
@@ -465,7 +465,7 @@
         return project(gated, pieces, cuts, places.astype(jnp.int32), mine, half * rows, dtype)
 
     other = lax.ppermute(products(1 - core, jnp.bfloat16), "tensor", cores)
-    summed = products(core, jnp.float32) + other.astype(jnp.float32)
+    summed = products(core, jnp.bfloat16).astype(jnp.float32) + other.astype(jnp.float32)
     return (summed * scale).astype(jnp.bfloat16)
 
 

time: 154 us -> 154 us (level)
  no operation moved by 1% of the time
where the time goes in v6:
time: 154 us; the launch traced here: 153 us
  starting transfers between devices  43.5 us (28%)
  waiting for transfers between devices  34 us (22%)
  Pallas kernels  32.1 us (21%)
  local copies, waits for them, and re-layouts  22.7 us (15%)
  other arithmetic  15.8 us (10%)
  between operations  2.97 us (2%)
    pallas_call x2, Pallas kernels, project(): pl.pallas_call(functools.partial(project_kernel, cuts), in_specs=[pl.Bloc...  15.4 us
    ppermute x3, waiting for transfers between devices, gather_step(): other = lax.ppermute(held, axis, [(i, i ^ step) for i in range(n)])  14.6 us
    pallas_call x1, Pallas kernels, scan_call(): pl.pallas_call(scan_kernel, grid=(groups,), in_specs=[pl.BlockSpec((token...  11.3 us
    ppermute x5, waiting for transfers between devices, swap(): lax.ppermute(value, 'cache', [(2 * i + p, 2 * j + p) for i, j in pairs fo...  11.1 us
    ppermute x5, starting transfers between devices, swap(): lax.ppermute(value, 'cache', [(2 * i + p, 2 * j + p) for i, j in pairs fo...  9.81 us
    unnamed x50, local copies, waits for them, and re-layouts  9.54 us
    ppermute x5, starting transfers between devices, beside(): return lax.ppermute(value, 'cache', [(i, i ^ 1) for i in range(n)])  8.9 us
    slice x6, local copies, waits for them, and re-layouts, across(): return lax.ppermute(value[:share], 'groups', [(0, 1), (1, 0)])  7.45 us
  transfers between devices with their start and end apart: 23, of which 5 were waited for; matrix products, arithmetic and copies ran while one was open for 17% of the time, Pallas kernels for 16%

profile of v6, /device:TPU:0, one launch (start us, length us, event | category | flops | bytes accessed | tf_op | source)
XLA Modules:
  0.0 152.6 jit_solution(5234469645213228929)
XLA Ops:
  0.9 3.0 %collective-permute-start = (f32[1,60,128]{2,1,0:T(8,128)S(1)}, f32[1,60,128]{2,1,0:T(8,128)S(1)}, u32[]{:S(2)}, u32[]{:S(2)}) collective-permute-start(f32[1,60,128]{2,1,0:T(8,128)S(1)} %reshape.57), channel_id=1, source_target_pairs={{0,2},{2,0},{4,6},{6,4},{8,10},{10,8},{12,14},{14,12},{1,3},{3,1},... | collective-permute-start | bytes 92168 | tf_op jit(solution)/shard_map/ppermute | solution.py:277
  8.8 4.0 %collective-permute-start.2 = (bf16[192,2048]{1,0:T(8,128)(2,1)S(1)}, bf16[192,2048]{1,0:T(8,128)(2,1)S(1)}, u32[]{:S(2)}, u32[]{:S(2)}) collective-permute-start(bf16[192,2048]{1,0:T(8,128)(2,1)S(1)} %pad_maximum_fusion.1), channel_id=1, source_target_pairs={{0,4},{2,6},{4,0},{6,2},{8,12},{10,14},{12,8},{14,10},{1,5},{3,7},... | collective-permute-start | bytes 2359304 | tf_op jit(solution)/shard_map/ppermute | solution.py:295
  16.9 13.4 %collective-permute-done.4 = f32[2,60,128]{2,1,0:T(8,128)S(1)} collective-permute-done((f32[2,60,128]{2,1,0:T(8,128)S(1)}, f32[2,60,128]{2,1,0:T(8,128)S(1)}, u32[]{:S(2)}, u32[]{:S(2)}) %collective-permute-start.4) | collective-permute-done | bytes 61472 | tf_op jit(solution)/shard_map/ppermute | solution.py:277
  30.4 1.7 %collective-permute-start.14 = (f32[4,60,128]{2,1,0:T(8,128)S(1)}, f32[4,60,128]{2,1,0:T(8,128)S(1)}, u32[]{:S(2)}, u32[]{:S(2)}) collective-permute-start(f32[4,60,128]{2,1,0:T(8,128)S(1)} %pad_maximum_fusion.3), channel_id=1, source_target_pairs={{0,8},{2,10},{4,12},{6,14},{8,0},{10,2},{12,4},{14,6},{1,9},{3,11}... | collective-permute-start | bytes 368648 | tf_op jit(solution)/shard_map/ppermute | solution.py:277
  39.0 2.8 %convert_element_type.35 = bf16[1,32,64,256]{3,2,1,0:T(8,128)(2,1)} convert(f32[1,32,64,256]{3,2,1,0:T(8,128)} %param.28) | non-fusion elementwise | flops 524288 | bytes 3145728 | tf_op jit(solution)/shard_map/convert_element_type | solution.py:400
  41.8 5.8 %all-to-all-start = ((bf16[8,1,256,256]{3,2,1,0:T(8,128)(2,1)}), bf16[8,1,256,256]{3,2,1,0:T(8,128)(2,1)S(1)}, u32[]{:S(2)}, u32[]{:S(2)}) async-start(bf16[8,1,256,256]{3,2,1,0:T(8,128)(2,1)} %bitcast.30), calls=%async_computation | async-start | bytes 2097152 | tf_op jit(solution)/shard_map/all_to_all | solution.py:403
  48.0 2.2 %convert_element_type.36 = f32[512,512]{1,0:T(8,128)} convert(bf16[512,512]{1,0:T(8,128)(2,1)} %param.19) | non-fusion elementwise | flops 262144 | bytes 1572864 | tf_op jit(solution)/shard_map/convert_element_type | solution.py:25
  53.4 11.1 %collective-permute-done.6 = bf16[192,2048]{1,0:T(8,128)(2,1)} collective-permute-done((bf16[192,2048]{1,0:T(8,128)(2,1)}, bf16[192,2048]{1,0:T(8,128)(2,1)}, u32[]{:S(2)}, u32[]{:S(2)}) %collective-permute-start.6) | collective-permute-done | bytes 786464 | tf_op jit(solution)/shard_map/ppermute | solution.py:295
  64.5 2.1 %broadcast_select_fusion.1.refs_7_ = bf16[192,2048]{1,0:T(8,128)(2,1)} fusion(bf16[192,2048]{1,0:T(8,128)(2,1)} %collective-permute-done.3, bf16[192,2048]{1,0:T(8,128)(2,1)} %collective-permute-done.6, pred[]{:T(512)S(6)} %or.3), kind=kLoop, calls=%fused_computation.16 | loop fusion | flops 393216 | bytes 2359297 | tf_op jit(solution)/shard_map/jit(_where)/select_n | solution.py:319
  69.5 1.9 %slice.88 = bf16[128,2048]{1,0:T(8,128)(2,1)} slice(bf16[192,2048]{1,0:T(8,128)(2,1)} %broadcast_select_fusion.1.refs_7_), slice={[0:128], [0:2048]} | slice | bytes 1048576 | tf_op jit(solution)/shard_map/slice | solution.py:300
  71.4 1.9 %slice.69 = bf16[128,2048]{1,0:T(8,128)(2,1)} slice(bf16[192,2048]{1,0:T(8,128)(2,1)} %collective-permute-done.7.refs_5_), slice={[0:128], [0:2048]} | slice | bytes 1048576 | tf_op jit(solution)/shard_map/slice | solution.py:300
  79.6 6.4 %all-to-all-start.1 = ((bf16[8,256,256]{2,1,0:T(8,128)(2,1)}), bf16[8,256,256]{2,1,0:T(8,128)(2,1)S(1)}, u32[]{:S(2)}, u32[]{:S(2)}) async-start(bf16[8,256,256]{2,1,0:T(8,128)(2,1)} %choose_rows.1), calls=%async_computation.1 | async-start | bytes 2097152 | tf_op jit(solution)/shard_map/all_to_all | solution.py:445
  88.9 11.3 %scan_blocks.1.y_ref = f32[512,2048]{1,0:T(8,128)S(1)} custom-call(bf16[512,2048]{1,0:T(8,128)(2,1)S(1)} %copy-done.3, f32[8,2048]{1,0:T(8,128)S(1)} %concatenate.32.prev_ref, bf16[4,2048]{1,0:T(4,128)(2,1)S(1)} %copy-done.5, f32[4,512,16]{2,1,0:T(8,128)S(1)} %copy.40.cols_ref, f32[32,512]{1,0:T(8,128)S(1)} %get-tuple-element.56.arow_ref, ...), custom_call_target="tpu_custom_call" | custom-call | flops 1 | bytes 1 | tf_op jit(solution)/shard_map/scan_blocks/pallas_call | solution.py:103
  100.2 2.0 %copy-done = f32[512,2048]{1,0:T(8,128)} copy-done((f32[512,2048]{1,0:T(8,128)}, f32[512,2048]{1,0:T(8,128)S(1)}, u32[]{:S(2)}) %copy-start) | copy-done | bytes 4194328
  105.8 2.0 %collective-permute-start.17 = (bf16[192,2048]{1,0:T(8,128)(2,1)S(1)}, bf16[192,2048]{1,0:T(8,128)(2,1)}, u32[]{:S(2)}, u32[]{:S(2)}) collective-permute-start(bf16[192,2048]{1,0:T(8,128)(2,1)S(1)} %broadcast_select_fusion.refs_11_), channel_id=1, source_target_pairs={{0,2},{2,0},{4,6},{6,4},{8,10},{10,8},{12,14},{14,12},{1,3},{3,1},... | collective-permute-start | bytes 2359304 | tf_op jit(solution)/shard_map/ppermute | solution.py:303
  107.8 6.5 %collective-permute-done.15.refs_12_ = bf16[128,2048]{1,0:T(8,128)(2,1)} collective-permute-done((bf16[128,2048]{1,0:T(8,128)(2,1)S(1)}, bf16[128,2048]{1,0:T(8,128)(2,1)}, u32[]{:S(2)}, u32[]{:S(2)}) %collective-permute-start.15) | collective-permute-done | bytes 524320 | tf_op jit(solution)/shard_map/ppermute | solution.py:300
  114.3 1.9 %slice.87 = bf16[128,2048]{1,0:T(8,128)(2,1)} slice(bf16[192,2048]{1,0:T(8,128)(2,1)} %collective-permute-done.10.refs_9_), slice={[0:128], [0:2048]} | slice | bytes 1048576 | tf_op jit(solution)/shard_map/slice | solution.py:300
  117.7 2.3 %collective-permute-start.18 = (bf16[128,2048]{1,0:T(8,128)(2,1)}, bf16[128,2048]{1,0:T(8,128)(2,1)}, u32[]{:S(2)}, u32[]{:S(2)}) collective-permute-start(bf16[128,2048]{1,0:T(8,128)(2,1)} %collective-permute-done.15.refs_12_), channel_id=1, source_target_pairs={{0,2},{2,0},{4,6},{6,4},{8,10},{10,8},{12,14},{14,12},{1,3},{3,1},... | collective-permute-start | bytes 1572872 | tf_op jit(solution)/shard_map/ppermute | solution.py:303
  122.2 2.2 %copy-done.1 = f32[512,2048]{1,0:T(8,128)S(1)} copy-done((f32[512,2048]{1,0:T(8,128)S(1)}, f32[512,2048]{1,0:T(8,128)}, u32[]{:S(2)}) %copy-start.1) | copy-done | bytes 4194328
  125.9 3.8 %gate_blocks.1 = (bf16[512,2048]{1,0:T(8,128)(2,1)S(1)}, f32[512,128]{1,0:T(8,128)S(1)}) custom-call(f32[512,2048]{1,0:T(8,128)S(1)} %copy-done.1, bf16[512,2048]{1,0:T(8,128)(2,1)S(1)} %copy-done.4, f32[4,512,8]{2,1,0:T(8,128)S(1)} %bitcast.88, bf16[2048,256]{1,0:T(8,128)(2,1)S(1)} %bitcast.87, bf16[512,256]{1,0:T(8,128)(2,1)S(1)} %get-tuple-element.53.c_ref, ...), custom_call_target="tpu_custom_call" | custom-call | flops 1 | bytes 1 | tf_op jit(solution)/shard_map/gate_blocks/pallas_call | solution.py:161
  131.1 1.8 %collective-permute-done.18.refs_14_ = bf16[128,2048]{1,0:T(8,128)(2,1)} collective-permute-done((bf16[128,2048]{1,0:T(8,128)(2,1)}, bf16[128,2048]{1,0:T(8,128)(2,1)}, u32[]{:S(2)}, u32[]{:S(2)}) %collective-permute-start.18) | collective-permute-done | bytes 524320 | tf_op jit(solution)/shard_map/ppermute | solution.py:303
  132.9 7.7 %project_rows.3 = bf16[512,1280]{1,0:T(8,128)(2,1)} custom-call(s32[22]{0:T(128)} %stack.132.rows_ref, s32[22]{0:T(128)} %get-tuple-element.67.mine_ref, bf16[512,2048]{1,0:T(8,128)(2,1)} %copy-done.2, bf16[320,2048]{1,0:T(8,128)(2,1)} %refs_0_.1, bf16[192,2048]{1,0:T(8,128)(2,1)} %copy-done.9, bf16[128,2048]{1,0:T(8,128)(2,1)} %collective-permute-done.8.refs_2_, ...), custom_call_target="tpu_custom_call" | custom-call | flops 1 | bytes 1 | tf_op jit(solution)/shard_map/project_rows/pallas_call | solution.py:228
  142.0 7.7 %project_rows.2 = bf16[512,1280]{1,0:T(8,128)(2,1)} custom-call(s32[22]{0:T(128)} %stack.132.rows_ref, s32[22]{0:T(128)} %get-tuple-element.66.mine_ref, bf16[512,2048]{1,0:T(8,128)(2,1)} %copy-done.2, bf16[320,2048]{1,0:T(8,128)(2,1)} %refs_0_.1, bf16[192,2048]{1,0:T(8,128)(2,1)} %copy-done.9, bf16[128,2048]{1,0:T(8,128)(2,1)} %collective-permute-done.8.refs_2_, ...), custom_call_target="tpu_custom_call" | custom-call | flops 1 | bytes 1 | tf_op jit(solution)/shard_map/project_rows/pallas_call | solution.py:228
  149.8 2.8 %multiply_convert_fusion = bf16[512,1280]{1,0:T(8,128)(2,1)} fusion(bf16[512,1280]{1,0:T(8,128)(2,1)S(1)} %collective-permute-done.19, bf16[512,1280]{1,0:T(8,128)(2,1)} %project_rows.2, f32[512]{0:T(512)S(1)} %rsqrt_select_fusion), kind=kLoop, calls=%fused_computation | loop fusion | flops 3276800 | bytes 3934208 | tf_op jit(solution)/shard_map/convert_element_type | solution.py:469
  (136 shorter events, 41.4 us)
Async XLA Ops:
  0.9 4.9 %collective-permute-start = (f32[1,60,128]{2,1,0:T(8,128)S(1)}, f32[1,60,128]{2,1,0:T(8,128)S(1)}, u32[]{:S(2)}, u32[]{:S(2)}) collective-permute-start(f32[1,60,128]{2,1,0:T(8,128)S(1)} %reshape.57), channel_id=1, source_target_pairs={{0,2},{2,0},{4,6},{6,4},{8,10},{10,8},{12,14},{14,12},{1,3},{3,1},... | collective-permute-start | bytes 92168 | tf_op jit(solution)/shard_map/ppermute | solution.py:277
  7.1 23.2 %collective-permute-start.3 = (bf16[192,2048]{1,0:T(8,128)(2,1)S(1)}, bf16[192,2048]{1,0:T(8,128)(2,1)}, u32[]{:S(2)}, u32[]{:S(2)}) collective-permute-start(bf16[192,2048]{1,0:T(8,128)(2,1)S(1)} %pad_maximum_fusion.1), channel_id=1, source_target_pairs={{4,8},{6,10},{8,4},{10,6},{5,9},{7,11},{9,5},{11,7},{20,24},{22,26... | collective-permute-start | bytes 2359304 | tf_op jit(solution)/shard_map/ppermute | solution.py:295
  8.8 21.6 %collective-permute-start.2 = (bf16[192,2048]{1,0:T(8,128)(2,1)S(1)}, bf16[192,2048]{1,0:T(8,128)(2,1)S(1)}, u32[]{:S(2)}, u32[]{:S(2)}) collective-permute-start(bf16[192,2048]{1,0:T(8,128)(2,1)S(1)} %pad_maximum_fusion.1), channel_id=1, source_target_pairs={{0,4},{2,6},{4,0},{6,2},{8,12},{10,14},{12,8},{14,10},{1,5},{3,7},... | collective-permute-start | bytes 2359304 | tf_op jit(solution)/shard_map/ppermute | solution.py:295
  12.8 17.6 %collective-permute-start.1 = (bf16[192,2048]{1,0:T(8,128)(2,1)S(1)}, bf16[192,2048]{1,0:T(8,128)(2,1)S(1)}, u32[]{:S(2)}, u32[]{:S(2)}) collective-permute-start(bf16[192,2048]{1,0:T(8,128)(2,1)S(1)} %pad_maximum_fusion.1), channel_id=1, source_target_pairs={{0,2},{2,0},{4,6},{6,4},{8,10},{10,8},{12,14},{14,12},{1,3},{3,1},... | collective-permute-start | bytes 2359304 | tf_op jit(solution)/shard_map/ppermute | solution.py:303
  14.6 27.2 %copy-start.12 = (f32[4,32,128]{2,1,0:T(8,128)}, f32[4,32,128]{2,1,0:T(8,128)S(1)}, u32[]{:S(2)}) copy-start(f32[4,32,128]{2,1,0:T(8,128)S(1)} %fusion.8) | copy-start | bytes 196612
  14.6 15.7 %collective-permute-start.4 = (f32[2,60,128]{2,1,0:T(8,128)S(1)}, f32[2,60,128]{2,1,0:T(8,128)S(1)}, u32[]{:S(2)}, u32[]{:S(2)}) collective-permute-start(f32[2,60,128]{2,1,0:T(8,128)S(1)} %pad_maximum_fusion.5), channel_id=1, source_target_pairs={{0,4},{2,6},{4,0},{6,2},{8,12},{10,14},{12,8},{14,10},{1,5},{3,7},... | collective-permute-start | bytes 184328 | tf_op jit(solution)/shard_map/ppermute | solution.py:277
  30.4 11.4 %collective-permute-start.14 = (f32[4,60,128]{2,1,0:T(8,128)S(1)}, f32[4,60,128]{2,1,0:T(8,128)S(1)}, u32[]{:S(2)}, u32[]{:S(2)}) collective-permute-start(f32[4,60,128]{2,1,0:T(8,128)S(1)} %pad_maximum_fusion.3), channel_id=1, source_target_pairs={{0,8},{2,10},{4,12},{6,14},{8,0},{10,2},{12,4},{14,6},{1,9},{3,11}... | collective-permute-start | bytes 368648 | tf_op jit(solution)/shard_map/ppermute | solution.py:277
  32.2 32.3 %collective-permute-start.7 = (bf16[192,2048]{1,0:T(8,128)(2,1)S(1)}, bf16[192,2048]{1,0:T(8,128)(2,1)}, u32[]{:S(2)}, u32[]{:S(2)}) collective-permute-start(bf16[192,2048]{1,0:T(8,128)(2,1)S(1)} %collective-permute-done.2.refs_3_), channel_id=1, source_target_pairs={{0,2},{2,0},{4,6},{6,4},{8,10},{10,8},{12,14},{14,12},{1,3},{3,1},... | collective-permute-start | bytes 2359304 | tf_op jit(solution)/shard_map/ppermute | solution.py:303
  33.8 30.8 %collective-permute-start.5 = (bf16[192,2048]{1,0:T(8,128)(2,1)S(1)}, bf16[192,2048]{1,0:T(8,128)(2,1)}, u32[]{:S(2)}, u32[]{:S(2)}) collective-permute-start(bf16[192,2048]{1,0:T(8,128)(2,1)S(1)} %collective-permute-done.2.refs_3_), channel_id=1, source_target_pairs={{4,8},{6,10},{8,4},{10,6},{5,9},{7,11},{9,5},{11,7},{20,24},{22,26... | collective-permute-start | bytes 2359304 | tf_op jit(solution)/shard_map/ppermute | solution.py:295
  36.2 17.2 %collective-permute-start.8 = (bf16[128,2048]{1,0:T(8,128)(2,1)}, bf16[128,2048]{1,0:T(8,128)(2,1)}, u32[]{:S(2)}, u32[]{:S(2)}) collective-permute-start(bf16[128,2048]{1,0:T(8,128)(2,1)} %slice.67), channel_id=1, source_target_pairs={{0,16},{16,0},{1,17},{17,1},{2,18},{18,2},{3,19},{19,3},{4,20},{20... | collective-permute-start | bytes 1572872 | tf_op jit(solution)/shard_map/ppermute | solution.py:300
  37.7 26.8 %collective-permute-start.6 = (bf16[192,2048]{1,0:T(8,128)(2,1)}, bf16[192,2048]{1,0:T(8,128)(2,1)}, u32[]{:S(2)}, u32[]{:S(2)}) collective-permute-start(bf16[192,2048]{1,0:T(8,128)(2,1)} %collective-permute-done.3), channel_id=1, source_target_pairs={{4,0},{6,2},{8,12},{10,14},{5,1},{7,3},{9,13},{11,15},{20,16},{22,... | collective-permute-start | bytes 2359304 | tf_op jit(solution)/shard_map/ppermute | solution.py:295
  41.8 36.2 %all-to-all-start = ((bf16[8,1,256,256]{3,2,1,0:T(8,128)(2,1)}), bf16[8,1,256,256]{3,2,1,0:T(8,128)(2,1)S(1)}, u32[]{:S(2)}, u32[]{:S(2)}) async-start(bf16[8,1,256,256]{3,2,1,0:T(8,128)(2,1)} %bitcast.30), calls=%async_computation | async-start | bytes 2097152 | tf_op jit(solution)/shard_map/all_to_all | solution.py:403
  52.8 49.3 %collective-permute-start.11 = (bf16[128,2048]{1,0:T(8,128)(2,1)}, bf16[128,2048]{1,0:T(8,128)(2,1)}, u32[]{:S(2)}, u32[]{:S(2)}) collective-permute-start(bf16[128,2048]{1,0:T(8,128)(2,1)} %slice.68), channel_id=1, source_target_pairs={{0,16},{16,0},{1,17},{17,1},{2,18},{18,2},{3,19},{19,3},{4,20},{20... | collective-permute-start | bytes 1572872 | tf_op jit(solution)/shard_map/ppermute | solution.py:300
  66.7 35.5 %collective-permute-start.10 = (bf16[192,2048]{1,0:T(8,128)(2,1)}, bf16[192,2048]{1,0:T(8,128)(2,1)}, u32[]{:S(2)}, u32[]{:S(2)}) collective-permute-start(bf16[192,2048]{1,0:T(8,128)(2,1)} %broadcast_select_fusion.1.refs_7_), channel_id=1, source_target_pairs={{0,2},{2,0},{4,6},{6,4},{8,10},{10,8},{12,14},{14,12},{1,3},{3,1},... | collective-permute-start | bytes 2359304 | tf_op jit(solution)/shard_map/ppermute | solution.py:303
  68.2 34.8 %collective-permute-start.9 = (bf16[192,2048]{1,0:T(8,128)(2,1)}, bf16[192,2048]{1,0:T(8,128)(2,1)}, u32[]{:S(2)}, u32[]{:S(2)}) collective-permute-start(bf16[192,2048]{1,0:T(8,128)(2,1)} %collective-permute-done.5), channel_id=1, source_target_pairs={{4,0},{6,2},{8,12},{10,14},{5,1},{7,3},{9,13},{11,15},{20,16},{22,... | collective-permute-start | bytes 2359304 | tf_op jit(solution)/shard_map/ppermute | solution.py:295
  73.4 28.8 %collective-permute-start.12 = (bf16[128,2048]{1,0:T(8,128)(2,1)}, bf16[128,2048]{1,0:T(8,128)(2,1)S(1)}, u32[]{:S(2)}, u32[]{:S(2)}) collective-permute-start(bf16[128,2048]{1,0:T(8,128)(2,1)} %slice.69), channel_id=1, source_target_pairs={{0,16},{16,0},{1,17},{17,1},{2,18},{18,2},{3,19},{19,3},{4,20},{20... | collective-permute-start | bytes 1572872 | tf_op jit(solution)/shard_map/ppermute | solution.py:300
  73.7 28.4 %collective-permute-start.13 = (bf16[128,2048]{1,0:T(8,128)(2,1)}, bf16[128,2048]{1,0:T(8,128)(2,1)}, u32[]{:S(2)}, u32[]{:S(2)}) collective-permute-start(bf16[128,2048]{1,0:T(8,128)(2,1)} %slice.88), channel_id=1, source_target_pairs={{0,16},{16,0},{1,17},{17,1},{2,18},{18,2},{3,19},{19,3},{4,20},{20... | collective-permute-start | bytes 1572872 | tf_op jit(solution)/shard_map/ppermute | solution.py:300
  79.6 42.5 %all-to-all-start.1 = ((bf16[8,256,256]{2,1,0:T(8,128)(2,1)}), bf16[8,256,256]{2,1,0:T(8,128)(2,1)S(1)}, u32[]{:S(2)}, u32[]{:S(2)}) async-start(bf16[8,256,256]{2,1,0:T(8,128)(2,1)} %choose_rows.1), calls=%async_computation.1 | async-start | bytes 2097152 | tf_op jit(solution)/shard_map/all_to_all | solution.py:445
  104.2 10.1 %collective-permute-start.15 = (bf16[128,2048]{1,0:T(8,128)(2,1)S(1)}, bf16[128,2048]{1,0:T(8,128)(2,1)}, u32[]{:S(2)}, u32[]{:S(2)}) collective-permute-start(bf16[128,2048]{1,0:T(8,128)(2,1)S(1)} %slice.98), channel_id=1, source_target_pairs={{0,16},{16,0},{1,17},{17,1},{2,18},{18,2},{3,19},{19,3},{4,20},{20... | collective-permute-start | bytes 1572872 | tf_op jit(solution)/shard_map/ppermute | solution.py:300
  105.8 25.3 %collective-permute-start.17 = (bf16[192,2048]{1,0:T(8,128)(2,1)S(1)}, bf16[192,2048]{1,0:T(8,128)(2,1)}, u32[]{:S(2)}, u32[]{:S(2)}) collective-permute-start(bf16[192,2048]{1,0:T(8,128)(2,1)S(1)} %broadcast_select_fusion.refs_11_), channel_id=1, source_target_pairs={{0,2},{2,0},{4,6},{6,4},{8,10},{10,8},{12,14},{14,12},{1,3},{3,1},... | collective-permute-start | bytes 2359304 | tf_op jit(solution)/shard_map/ppermute | solution.py:303
  116.2 14.9 %collective-permute-start.16 = (bf16[128,2048]{1,0:T(8,128)(2,1)}, bf16[128,2048]{1,0:T(8,128)(2,1)}, u32[]{:S(2)}, u32[]{:S(2)}) collective-permute-start(bf16[128,2048]{1,0:T(8,128)(2,1)} %slice.87), channel_id=1, source_target_pairs={{0,16},{16,0},{1,17},{17,1},{2,18},{18,2},{3,19},{19,3},{4,20},{20... | collective-permute-start | bytes 1572872 | tf_op jit(solution)/shard_map/ppermute | solution.py:300
  117.7 15.2 %collective-permute-start.18 = (bf16[128,2048]{1,0:T(8,128)(2,1)}, bf16[128,2048]{1,0:T(8,128)(2,1)}, u32[]{:S(2)}, u32[]{:S(2)}) collective-permute-start(bf16[128,2048]{1,0:T(8,128)(2,1)} %collective-permute-done.15.refs_12_), channel_id=1, source_target_pairs={{0,2},{2,0},{4,6},{6,4},{8,10},{10,8},{12,14},{14,12},{1,3},{3,1},... | collective-permute-start | bytes 1572872 | tf_op jit(solution)/shard_map/ppermute | solution.py:303
  140.6 9.2 %collective-permute-start.19 = (bf16[512,1280]{1,0:T(8,128)(2,1)}, bf16[512,1280]{1,0:T(8,128)(2,1)S(1)}, u32[]{:S(2)}, u32[]{:S(2)}) collective-permute-start(bf16[512,1280]{1,0:T(8,128)(2,1)} %project_rows.3), channel_id=1, source_target_pairs={{0,1},{1,0},{2,3},{3,2},{4,5},{5,4},{6,7},{7,6},{8,9},{9,8},{10,11... | collective-permute-start | bytes 3932168 | tf_op jit(solution)/shard_map/ppermute | solution.py:467
  140.8 8.9 %collective-permute-start.20 = (f32[512]{0:T(512)S(1)}, f32[512]{0:T(512)S(1)}, u32[]{:S(2)}, u32[]{:S(2)}) collective-permute-start(f32[512]{0:T(512)S(1)} %reduce_sum.19), channel_id=1, source_target_pairs={{0,1},{1,0},{2,3},{3,2},{4,5},{5,4},{6,7},{7,6},{8,9},{9,8},{10,11... | collective-permute-start | bytes 6152 | tf_op jit(solution)/shard_map/ppermute | solution.py:451
  (26 other events, 205.8 us)
